TPU v7x, 32 devices: a whole 2x2x4 slice. The times are simulated.
32 devices in a mesh: dp: 2 (over x), row: 8 (over z, core), col: 2 (over y).
Axes of the slice: x: 2, y: 2, z: 4, core: 2. Of those that a mesh axis runs over, the one named last changes fastest.
Arguments:
- streams: float32 [2, 4, 3072, 2048], P(None, None, ('dp', 'row'), 'col'), may hold values from -6 to 6
- cotangent: float32 [2, 4, 3072, 2048], P(None, None, ('dp', 'row'), 'col'), may hold values from -6 to 6
- destination: int32 [2, 3072], P(None, ('dp', 'row')), may hold values from 0 to 3071, as said below
- segments: int32 [2, 2, 1536], P(None, 'dp'), may hold values from 0 to 3, never falling along the last dimension, each value on 1 to 1152 neighbouring positions
- attention_in: float32 [3, 2048, 2048], P(None, ('col', 'dp'), 'row'), may hold values from -0.125 to 0.125
- feedforward_in: float32 [2, 2048, 8192], P(None, ('col', 'dp'), 'row'), may hold values from -0.125 to 0.125
- attention_out: float32 [2048, 2048], P(('row', 'dp'), 'col'), may hold values from -1.5 to 1.5
- feedforward_out: float32 [8192, 2048], P(('row', 'dp'), 'col'), may hold values from -0.0625 to 0.0625
- attention_in_moment: float32 [3, 2048, 2048], P(None, ('col', 'dp'), 'row')
- feedforward_in_moment: float32 [2, 2048, 8192], P(None, ('col', 'dp'), 'row')
- attention_out_moment: float32 [2048, 2048], P(('row', 'dp'), 'col')
- feedforward_out_moment: float32 [8192, 2048], P(('row', 'dp'), 'col')
- attention_in_second: float32 [3, 2048, 2048], P(None, ('col', 'dp'), 'row'), as said below
- feedforward_in_second: float32 [2, 2048, 8192], P(None, ('col', 'dp'), 'row'), as said below
- attention_out_second: float32 [2048, 2048], P(('row', 'dp'), 'col'), as said below
- feedforward_out_second: float32 [8192, 2048], P(('row', 'dp'), 'col'), as said below
- hyper_weights: float32 [2, 4, 6], replicated, may hold values from 0.2 to 0.8
- hyper_moment: float32 [2, 4, 6], replicated, may hold values from -0.15625 to 0.15625
- hyper_second: float32 [2, 4, 6], replicated, may hold values from 6e-06 to 0.0001
- step_count: int32 [1], replicated, may hold values from 1 to 20
Outputs:
- streams_out: float32 [2, 4, 3072, 2048], P(None, None, ('dp', 'row'), 'col')
- stream_grad: float32 [2, 4, 3072, 2048], P(None, None, ('dp', 'row'), 'col')
- grad_norm: float32 [1], replicated
- attention_in_grad: float32 [3, 2048, 2048], P(None, ('col', 'dp'), 'row')
- feedforward_in_grad: float32 [2, 2048, 8192], P(None, ('col', 'dp'), 'row')
- attention_out_grad: float32 [2048, 2048], P(('row', 'dp'), 'col')
- feedforward_out_grad: float32 [8192, 2048], P(('row', 'dp'), 'col')
- hyper_grad: float32 [2, 4, 6], replicated
- attention_in_master: float32 [3, 2048, 2048], P(None, ('col', 'dp'), 'row')
- feedforward_in_master: float32 [2, 2048, 8192], P(None, ('col', 'dp'), 'row')
- attention_out_master: float32 [2048, 2048], P(('row', 'dp'), 'col')
- feedforward_out_master: float32 [8192, 2048], P(('row', 'dp'), 'col')
- hyper_master: float32 [2, 4, 6], replicated
- attention_in_moment_new: float32 [3, 2048, 2048], P(None, ('col', 'dp'), 'row')
- feedforward_in_moment_new: float32 [2, 2048, 8192], P(None, ('col', 'dp'), 'row')
- attention_out_moment_new: float32 [2048, 2048], P(('row', 'dp'), 'col')
- feedforward_out_moment_new: float32 [8192, 2048], P(('row', 'dp'), 'col')
- hyper_moment_new: float32 [2, 4, 6], replicated
- attention_in_second_new: float32 [3, 2048, 2048], P(None, ('col', 'dp'), 'row')
- feedforward_in_second_new: float32 [2, 2048, 8192], P(None, ('col', 'dp'), 'row')
- attention_out_second_new: float32 [2048, 2048], P(('row', 'dp'), 'col')
- feedforward_out_second_new: float32 [8192, 2048], P(('row', 'dp'), 'col')
- hyper_second_new: float32 [2, 4, 6], replicated
Inputs may be any that keep to these rules, and one draw needn't show every extreme that they name: `destination`: each row is a permutation of 0 to 3071. The token at given position t = a * 1536 + r * 192 + i goes to a working position b * 1536 + r * 192 + a * 96 + j with j < 96; each (a, r) sends exactly 96 tokens to each b. `attention_in_second`: entries are positive. `feedforward_in_second`: entries are positive. `attention_out_second`: entries are positive. `feedforward_out_second`: entries are positive.
All inputs are finite; a program needn't handle non-finite values.
Results may differ from a plain program's by a relative error of at most 0.012.
The roundings to bfloat16 on the way count: a program that leaves them out, or rounds other values in their place, can miss the bound.
Values may be sent and summed in bfloat16 or wider, within the bound.
A program may use at most 320 MiB of HBM per device.

v0:
```python
import math

import jax
import jax.numpy as jnp
from jax import lax
from jax.sharding import PartitionSpec as P

D = 2048
HEAD = 128
STREAMS = 4
MICRO = 2


HIGHEST = lax.Precision.HIGHEST
norm_eps = 1e-05
beta_first = 0.9
beta_second = 0.95
adam_eps = 1e-08
learning_rate = 0.05
weight_decay = 0.1


def rotary_tables(segment):
    length = segment.shape[0]
    places = jnp.arange(length, dtype=jnp.int32)
    starts = jnp.searchsorted(segment, segment, side="left")
    offsets = (places - starts).astype(jnp.float32)
    halves = jnp.arange(HEAD // 2, dtype=jnp.float32)
    inverse = jnp.exp(halves * (-2.0 * math.log(10000.0) / HEAD))
    angles = offsets[:, None] * inverse[None, :]
    return (jnp.cos(angles), jnp.sin(angles))


def rotate(values_in, cosine, sine):
    half_width = values_in.shape[-1] // 2
    leading = values_in[..., :half_width]
    trailing = values_in[..., half_width:]
    return jnp.concatenate(
        [leading * cosine - trailing * sine, leading * sine + trailing * cosine], axis=-1
    )


def token_stats(first_sum, second_sum):
    return lax.psum((first_sum, second_sum), "col")


def norm_forward(hidden):
    total_one, total_two = token_stats(jnp.sum(hidden, axis=-1), jnp.sum(hidden * hidden, axis=-1))
    means = total_one / D
    inverse = lax.rsqrt(total_two / D - means * means + norm_eps)
    return ((hidden - means[:, None]) * inverse[:, None], inverse)


def norm_backward(upstream, normed, inverse):
    total_one, total_two = token_stats(
        jnp.sum(upstream, axis=-1), jnp.sum(upstream * normed, axis=-1)
    )
    return inverse[:, None] * (
        upstream - total_one[:, None] / D - normed * (total_two[:, None] / D)
    )


def gather_tokens(rows_low):
    return lax.all_gather(rows_low, "row", axis=0, tiled=True)


def sum_units(partial_sums):
    return lax.psum_scatter(partial_sums, "col", scatter_dimension=2, tiled=True)


def gather_units(units_low):
    return lax.all_gather(units_low, "col", axis=2, tiled=True)


def project_units(rows_low, weight_low):
    return sum_units(
        jnp.einsum("td,kdu->tku", rows_low, weight_low, preferred_element_type=jnp.float32)
    )


def sum_tokens(left_side, right_side, formula):
    return lax.psum_scatter(
        jnp.einsum(formula, left_side, right_side, preferred_element_type=jnp.float32),
        "row",
        scatter_dimension=0,
        tiled=True,
    )


def mix_in(layer_weights, stream_set):
    return jnp.einsum("i,itd->td", layer_weights[:, 0], stream_set, precision=HIGHEST)


def mix_out(layer_weights, stream_set, branch):
    mixed = jnp.einsum(
        "ij,itd->jtd", layer_weights[:, 1 : STREAMS + 1], stream_set, precision=HIGHEST
    )
    return mixed + layer_weights[:, STREAMS + 1][:, None, None] * branch[None]


def mix_back(layer_weights, stream_set, branch, upstream):
    grad_branch = jnp.einsum(
        "j,jtd->td", layer_weights[:, STREAMS + 1], upstream, precision=HIGHEST
    )
    grad_streams = jnp.einsum(
        "ij,jtd->itd", layer_weights[:, 1 : STREAMS + 1], upstream, precision=HIGHEST
    )
    grad_mix = jnp.einsum("itd,jtd->ij", stream_set, upstream, precision=HIGHEST)
    grad_scale = jnp.einsum("td,jtd->j", branch, upstream, precision=HIGHEST)
    return (grad_branch, grad_streams, grad_mix, grad_scale)


def mix_finish(layer_weights, stream_set, grad_streams, grad_input, grad_mix, grad_scale):
    streams_total = grad_streams + layer_weights[:, 0][:, None, None] * grad_input[None]
    grad_width = jnp.einsum("itd,td->i", stream_set, grad_input, precision=HIGHEST)
    layer_grad = jnp.concatenate([grad_width[:, None], grad_mix, grad_scale[:, None]], axis=1)
    return (streams_total, layer_grad)


def block_masks(segment):
    length = segment.shape[0]
    block_rows = min(512, length)
    blocks = length // block_rows
    places = jnp.arange(length, dtype=jnp.int32)
    return (length, block_rows, blocks, places)


def masked_scores(query_part, key_low, segment_part, place_part, segment, places):
    scores = jnp.einsum(
        "qe,ke->qk", query_part, key_low, preferred_element_type=jnp.float32
    ) * HEAD ** (-0.5)
    allowed = (segment_part[:, None] == segment[None, :]) & (places[None, :] <= place_part[:, None])
    return jnp.where(allowed, scores, -1e30)


def attend_forward(qkv_sums, segment):
    cosine, sine = rotary_tables(segment)
    query_low = rotate(qkv_sums[:, 0], cosine, sine).astype(jnp.bfloat16)
    key_low = rotate(qkv_sums[:, 1], cosine, sine).astype(jnp.bfloat16)
    value_low = qkv_sums[:, 2].astype(jnp.bfloat16)
    length, block_rows, blocks, places = block_masks(segment)

    def one_block(inputs):
        query_part, segment_part, place_part = inputs
        scores = masked_scores(query_part, key_low, segment_part, place_part, segment, places)
        largest = jnp.max(scores, axis=-1, keepdims=True)
        weights = jnp.exp(scores - largest)
        totals = jnp.sum(weights, axis=-1, keepdims=True)
        probs = (weights / totals).astype(jnp.bfloat16)
        outputs = jnp.dot(probs, value_low, preferred_element_type=jnp.float32)
        return (outputs, (largest + jnp.log(totals))[:, 0])

    outputs, log_totals = lax.map(
        one_block,
        (
            query_low.reshape(blocks, block_rows, HEAD),
            segment.reshape(blocks, block_rows),
            places.reshape(blocks, block_rows),
        ),
    )
    return (
        outputs.reshape(length, HEAD),
        log_totals.reshape(length),
        query_low,
        key_low,
        value_low,
        cosine,
        sine,
    )


def attend_backward(grad_low, query_low, key_low, value_low, log_totals, segment):
    length, block_rows, blocks, places = block_masks(segment)

    def one_block(carry, inputs):
        grad_keys, grad_values = carry
        query_part, grad_part, log_part, segment_part, place_part = inputs
        scores = masked_scores(query_part, key_low, segment_part, place_part, segment, places)
        probs = jnp.exp(scores - log_part[:, None])
        grad_probs = jnp.einsum(
            "qe,ke->qk", grad_part, value_low, preferred_element_type=jnp.float32
        )
        inner = jnp.sum(probs * grad_probs, axis=-1, keepdims=True)
        grad_scores = (probs * (grad_probs - inner) * HEAD ** (-0.5)).astype(jnp.bfloat16)
        grad_queries = jnp.dot(grad_scores, key_low, preferred_element_type=jnp.float32)
        grad_keys = grad_keys + jnp.einsum(
            "qk,qe->ke", grad_scores, query_part, preferred_element_type=jnp.float32
        )
        grad_values = grad_values + jnp.einsum(
            "qk,qe->ke", probs.astype(jnp.bfloat16), grad_part, preferred_element_type=jnp.float32
        )
        return ((grad_keys, grad_values), grad_queries)

    zeros_rows = jnp.zeros((length, HEAD), jnp.float32)
    carried, grad_queries = lax.scan(
        one_block,
        (zeros_rows, zeros_rows),
        (
            query_low.reshape(blocks, block_rows, HEAD),
            grad_low.reshape(blocks, block_rows, HEAD),
            log_totals.reshape(blocks, block_rows),
            segment.reshape(blocks, block_rows),
            places.reshape(blocks, block_rows),
        ),
    )
    return (grad_queries.reshape(length, HEAD), carried[0], carried[1])


def adam_update(weight, grad_sum, moment_one, moment_two, clip_factor, step_value):
    clipped = grad_sum * clip_factor
    new_one = beta_first * moment_one + (1.0 - beta_first) * clipped
    new_two = beta_second * moment_two + (1.0 - beta_second) * clipped * clipped
    fix_one = 1.0 - jnp.power(beta_first, step_value)
    fix_two = 1.0 - jnp.power(beta_second, step_value)
    new_weight = weight - learning_rate * (
        new_one / fix_one / (jnp.sqrt(new_two / fix_two) + adam_eps) + weight_decay * weight
    )
    return (new_weight, new_one, new_two)


def body(
    streams,
    cotangent,
    destination,
    segments,
    attention_in,
    feedforward_in,
    attention_out,
    feedforward_out,
    attention_in_moment,
    feedforward_in_moment,
    attention_out_moment,
    feedforward_out_moment,
    attention_in_second,
    feedforward_in_second,
    attention_out_second,
    feedforward_out_second,
    hyper_weights,
    hyper_moment,
    hyper_second,
    step_count,
):
    attention_in_low, feedforward_in_low, attention_out_low, feedforward_out_low = (
        lax.all_gather(attention_in.astype(jnp.bfloat16), "dp", axis=1, tiled=True),
        lax.all_gather(feedforward_in.astype(jnp.bfloat16), "dp", axis=1, tiled=True),
        lax.all_gather(attention_out.astype(jnp.bfloat16), "dp", axis=0, tiled=True),
        lax.all_gather(feedforward_out.astype(jnp.bfloat16), "dp", axis=0, tiled=True),
    )
    orders = jnp.argsort(destination, axis=1)
    sent_streams = jnp.stack(
        [streams[micro_index][:, orders[micro_index]] for micro_index in range(MICRO)]
    )
    sent_cot = jnp.stack(
        [cotangent[micro_index][:, orders[micro_index]] for micro_index in range(MICRO)]
    )
    work_streams, work_cot = (
        lax.all_to_all(sent_streams, "dp", split_axis=2, concat_axis=2, tiled=True),
        lax.all_to_all(sent_cot, "dp", split_axis=2, concat_axis=2, tiled=True),
    )
    local_attention_in = jnp.zeros(attention_in_low.shape, jnp.float32)
    local_feedforward_in = jnp.zeros(feedforward_in_low.shape, jnp.float32)
    local_attention_out = jnp.zeros(attention_out_low.shape, jnp.float32)
    local_feedforward_out = jnp.zeros(feedforward_out_low.shape, jnp.float32)
    hyper_part = jnp.zeros_like(hyper_weights)
    results = []
    stream_grads = []
    for micro_index in range(MICRO):
        streams_zero = work_streams[micro_index]
        segment = segments[micro_index, 0]
        normed_att, inverse_att = norm_forward(mix_in(hyper_weights[0], streams_zero))
        rows_att = gather_tokens(normed_att.astype(jnp.bfloat16))
        qkv_sums = project_units(rows_att, attention_in_low)
        heads_out, log_totals, query_low, key_low, value_low, cosine, sine = attend_forward(
            qkv_sums, segment
        )
        heads_pair = gather_units(heads_out.astype(jnp.bfloat16)[:, None, :])[:, 0]
        branch_att = sum_tokens(heads_pair, attention_out_low, "tu,ud->td")
        streams_one = mix_out(hyper_weights[0], streams_zero, branch_att)
        normed_ffn, inverse_ffn = norm_forward(mix_in(hyper_weights[1], streams_one))
        rows_ffn = gather_tokens(normed_ffn.astype(jnp.bfloat16))
        gate_up = project_units(rows_ffn, feedforward_in_low)
        gate_pre = gate_up[:, 0]
        up_pre = gate_up[:, 1]
        hidden_low = (jax.nn.silu(gate_pre) * up_pre).astype(jnp.bfloat16)
        hidden_pair = gather_units(hidden_low[:, None, :])[:, 0]
        branch_ffn = sum_tokens(hidden_pair, feedforward_out_low, "tu,ud->td")
        results.append(mix_out(hyper_weights[1], streams_one, branch_ffn))
        upstream_two = work_cot[micro_index]
        grad_branch, grad_partial, grad_mix, grad_scale = mix_back(
            hyper_weights[1], streams_one, branch_ffn, upstream_two
        )
        branch_rows = gather_tokens(grad_branch.astype(jnp.bfloat16))
        grad_feedforward_out = jnp.einsum(
            "tu,td->ud", hidden_pair, branch_rows, preferred_element_type=jnp.float32
        )
        grad_hidden = sum_units(
            jnp.einsum(
                "td,ud->tu", branch_rows, feedforward_out_low, preferred_element_type=jnp.float32
            )[:, None, :]
        )[:, 0]
        sigma = jax.nn.sigmoid(gate_pre)
        grad_gate = grad_hidden * up_pre * sigma * (1.0 + gate_pre * (1.0 - sigma))
        grad_up = grad_hidden * jax.nn.silu(gate_pre)
        grad_units = gather_units(jnp.stack([grad_gate, grad_up], axis=1).astype(jnp.bfloat16))
        grad_feedforward_in = jnp.einsum(
            "td,tku->kdu", rows_ffn, grad_units, preferred_element_type=jnp.float32
        )
        grad_normed = sum_tokens(grad_units, feedforward_in_low, "tku,kdu->td")
        grad_input = norm_backward(grad_normed, normed_ffn, inverse_ffn)
        upstream_one, layer_ffn = mix_finish(
            hyper_weights[1], streams_one, grad_partial, grad_input, grad_mix, grad_scale
        )
        grad_branch, grad_partial, grad_mix, grad_scale = mix_back(
            hyper_weights[0], streams_zero, branch_att, upstream_one
        )
        branch_rows = gather_tokens(grad_branch.astype(jnp.bfloat16))
        grad_attention_out = jnp.einsum(
            "tu,td->ud", heads_pair, branch_rows, preferred_element_type=jnp.float32
        )
        grad_heads = sum_units(
            jnp.einsum(
                "td,ud->tu", branch_rows, attention_out_low, preferred_element_type=jnp.float32
            )[:, None, :]
        )[:, 0]
        grad_queries, grad_keys, grad_values = attend_backward(
            grad_heads.astype(jnp.bfloat16), query_low, key_low, value_low, log_totals, segment
        )
        grad_qkv = jnp.stack(
            [rotate(grad_queries, cosine, -sine), rotate(grad_keys, cosine, -sine), grad_values],
            axis=1,
        )
        grad_units = gather_units(grad_qkv.astype(jnp.bfloat16))
        grad_attention_in = jnp.einsum(
            "td,tku->kdu", rows_att, grad_units, preferred_element_type=jnp.float32
        )
        grad_normed = sum_tokens(grad_units, attention_in_low, "tku,kdu->td")
        grad_input = norm_backward(grad_normed, normed_att, inverse_att)
        upstream_zero, layer_att = mix_finish(
            hyper_weights[0], streams_zero, grad_partial, grad_input, grad_mix, grad_scale
        )
        stream_grads.append(upstream_zero)
        hyper_part = hyper_part + jnp.stack([layer_att, layer_ffn])
        local_attention_in = local_attention_in + grad_attention_in
        local_feedforward_in = local_feedforward_in + grad_feedforward_in
        local_attention_out = local_attention_out + grad_attention_out
        local_feedforward_out = local_feedforward_out + grad_feedforward_out
    shard_attention_in, shard_feedforward_in, shard_attention_out, shard_feedforward_out = (
        lax.psum_scatter(local_attention_in, "dp", scatter_dimension=1, tiled=True),
        lax.psum_scatter(local_feedforward_in, "dp", scatter_dimension=1, tiled=True),
        lax.psum_scatter(local_attention_out, "dp", scatter_dimension=0, tiled=True),
        lax.psum_scatter(local_feedforward_out, "dp", scatter_dimension=0, tiled=True),
    )
    square = (
        jnp.sum(shard_attention_in * shard_attention_in)
        + jnp.sum(shard_feedforward_in * shard_feedforward_in)
        + jnp.sum(shard_attention_out * shard_attention_out)
        + jnp.sum(shard_feedforward_out * shard_feedforward_out)
    )
    hyper_grad, square_total = lax.psum((hyper_part, square), ("dp", "row", "col"))
    grad_norm = jnp.sqrt(square_total + jnp.sum(hyper_grad * hyper_grad))
    clip_factor = 1.0 / jnp.maximum(grad_norm, 1.0)
    step_value = step_count[0].astype(jnp.float32)
    attention_in_new = adam_update(
        attention_in,
        shard_attention_in,
        attention_in_moment,
        attention_in_second,
        clip_factor,
        step_value,
    )
    feedforward_in_new = adam_update(
        feedforward_in,
        shard_feedforward_in,
        feedforward_in_moment,
        feedforward_in_second,
        clip_factor,
        step_value,
    )
    attention_out_new = adam_update(
        attention_out,
        shard_attention_out,
        attention_out_moment,
        attention_out_second,
        clip_factor,
        step_value,
    )
    feedforward_out_new = adam_update(
        feedforward_out,
        shard_feedforward_out,
        feedforward_out_moment,
        feedforward_out_second,
        clip_factor,
        step_value,
    )
    hyper_new = adam_update(
        hyper_weights, hyper_grad, hyper_moment, hyper_second, clip_factor, step_value
    )
    back_streams, back_grads = (
        lax.all_to_all(jnp.stack(results), "dp", split_axis=2, concat_axis=2, tiled=True),
        lax.all_to_all(jnp.stack(stream_grads), "dp", split_axis=2, concat_axis=2, tiled=True),
    )
    inverses = jnp.argsort(orders, axis=1)
    streams_out = jnp.stack(
        [back_streams[micro_index][:, inverses[micro_index]] for micro_index in range(MICRO)]
    )
    stream_grad = jnp.stack(
        [back_grads[micro_index][:, inverses[micro_index]] for micro_index in range(MICRO)]
    )
    return (
        streams_out,
        stream_grad,
        grad_norm.reshape(1),
        shard_attention_in,
        shard_feedforward_in,
        shard_attention_out,
        shard_feedforward_out,
        hyper_grad,
        attention_in_new[0],
        feedforward_in_new[0],
        attention_out_new[0],
        feedforward_out_new[0],
        hyper_new[0],
        attention_in_new[1],
        feedforward_in_new[1],
        attention_out_new[1],
        feedforward_out_new[1],
        hyper_new[1],
        attention_in_new[2],
        feedforward_in_new[2],
        attention_out_new[2],
        feedforward_out_new[2],
        hyper_new[2],
    )


def solution(mesh):
    placed = (
        P(None, None, ("dp", "row"), "col"),
        P(None, None, ("dp", "row"), "col"),
        P(None, ("dp", "row")),
        P(None, "dp", None),
        P(None, ("col", "dp"), "row"),
        P(None, ("col", "dp"), "row"),
        P(("row", "dp"), "col"),
        P(("row", "dp"), "col"),
        P(None, ("col", "dp"), "row"),
        P(None, ("col", "dp"), "row"),
        P(("row", "dp"), "col"),
        P(("row", "dp"), "col"),
        P(None, ("col", "dp"), "row"),
        P(None, ("col", "dp"), "row"),
        P(("row", "dp"), "col"),
        P(("row", "dp"), "col"),
        P(),
        P(),
        P(),
        P(),
    )
    return jax.shard_map(
        body,
        mesh=mesh,
        in_specs=placed,
        out_specs=(
            P(None, None, ("dp", "row"), "col"),
            P(None, None, ("dp", "row"), "col"),
            P(),
            P(None, ("col", "dp"), "row"),
            P(None, ("col", "dp"), "row"),
            P(("row", "dp"), "col"),
            P(("row", "dp"), "col"),
            P(),
            P(None, ("col", "dp"), "row"),
            P(None, ("col", "dp"), "row"),
            P(("row", "dp"), "col"),
            P(("row", "dp"), "col"),
            P(),
            P(None, ("col", "dp"), "row"),
            P(None, ("col", "dp"), "row"),
            P(("row", "dp"), "col"),
            P(("row", "dp"), "col"),
            P(),
            P(None, ("col", "dp"), "row"),
            P(None, ("col", "dp"), "row"),
            P(("row", "dp"), "col"),
            P(("row", "dp"), "col"),
            P(),
        ),
        check_vma=False,
    )
```

profile of v0, /device:TPU:0, one launch (start us, length us, event | category | flops | bytes accessed | tf_op | source)
XLA Modules:
  0.0 2738.0 jit_solution(4168186394114907735)
XLA Ops:
  53.6 85.2 %all-to-all-done = f32[2,4,192,1024]{3,1,0,2:T(4,128)} async-done(((f32[2,4,192,1024]{3,1,0,2:T(4,128)}), f32[2,4,192,1024]{3,1,0,2:T(4,128)}, u32[]{:S(2)}, u32[]{:S(2)}) %all-to-all-start) | async-done | bytes 6291488 | tf_op jit(solution)/shard_map/all_to_all | solution.py:257
  162.5 36.6 %all-gather.30.cloned.1.call-done = bf16[1536,1024]{1,0:T(8,128)(2,1)} async-done(((bf16[192,1024]{1,0:T(8,128)(2,1)}), bf16[1536,1024]{1,0:T(8,128)(2,1)}) %all-gather.30.cloned.1.call-update) | async-done | bytes 3145744 | tf_op jit(solution)/shard_map/all_gather | solution.py:64
  216.9 93.3 %while.97 = (s32[]{:T(128)}, u32[1536]{0:T(1024)S(1)}, u32[1536]{0:T(1024)S(1)}, s32[1536]{0:T(1024)S(1)}, s32[]{:T(128)}, /*index=5*/s32[]{:T(128)}, s32[]{}) while((s32[]{:T(128)}, u32[1536]{0:T(1024)S(1)}, u32[1536]{0:T(1024)S(1)}, s32[1536]{0:T(1024)S(1)}, s32[]{:T(128)}, /*index=5*/s32[]{:T(128)}, s32[]{}) %tuple.234), condition=%wide.region_7.8_spmd.clone, body=%wide.region_6.7_spmd.clone.sunk | while | flops 29700 | bytes 115813 | solution.py:26
  318.4 93.3 %while.98 = (s32[]{:T(128)}, u32[1536]{0:T(1024)S(1)}, u32[1536]{0:T(1024)S(1)}, s32[1536]{0:T(1024)S(1)}, s32[]{:T(128)}, /*index=5*/s32[]{:T(128)}, s32[]{}) while((s32[]{:T(128)}, u32[1536]{0:T(1024)S(1)}, u32[1536]{0:T(1024)S(1)}, s32[1536]{0:T(1024)S(1)}, s32[]{:T(128)}, /*index=5*/s32[]{:T(128)}, s32[]{}) %tuple.231), condition=%wide.region_25.26_spmd.clone, body=%wide.region_24.25_spmd.clone.sunk | while | flops 29700 | bytes 115813 | solution.py:26
  555.7 67.1 %all-to-all-done.2 = f32[2,4,192,1024]{3,1,0,2:T(4,128)} async-done(((f32[2,4,192,1024]{3,1,0,2:T(4,128)}), f32[2,4,192,1024]{3,1,0,2:T(4,128)}, u32[]{:S(2)}, u32[]{:S(2)}) %all-to-all-start.2) | async-done | bytes 6291488 | tf_op jit(solution)/shard_map/all_to_all | solution.py:258
  694.9 48.5 %all-gather.24.cloned.1.call-done = bf16[2,1024,1024]{2,1,0:T(8,128)(2,1)} async-done(((bf16[2,512,1024]{2,1,0:T(8,128)(2,1)}), bf16[2,1024,1024]{2,1,0:T(8,128)(2,1)}) %all-gather.24.cloned.1.call-update) | async-done | bytes 4194320 | tf_op jit(solution)/shard_map/all_gather | solution.py:245
  743.3 40.5 %all-gather.22.cloned.1.call-done = bf16[1536,1024]{1,0:T(8,128)(2,1)} async-done(((bf16[192,1024]{1,0:T(8,128)(2,1)}), bf16[1536,1024]{1,0:T(8,128)(2,1)}) %all-gather.22.cloned.1.call-update) | async-done | bytes 3145744 | tf_op jit(solution)/shard_map/all_gather | solution.py:64
  831.9 30.6 %all-gather.32.cloned.1.call-done = bf16[1536,1024]{1,0:T(8,128)(2,1)} async-done(((bf16[192,1024]{1,0:T(8,128)(2,1)}), bf16[1536,1024]{1,0:T(8,128)(2,1)}) %all-gather.32.cloned.1.call-update) | async-done | bytes 3145744 | tf_op jit(solution)/shard_map/all_gather | solution.py:64
  874.9 66.4 %reduce-scatter.37.cloned.1.call-done = f32[1536,1,512]{2,0,1:T(8,128)} async-done(((f32[1536,1,1024]{2,0,1:T(8,128)}), f32[1536,1,512]{2,0,1:T(8,128)}) %reduce-scatter.37.cloned.1.call-update) | async-done | bytes 3145744 | tf_op jit(solution)/shard_map/reduce_scatter | solution.py:68
  941.2 146.8 %reduce-scatter.25.cloned.1.call-done = f32[1536,2,512]{2,0,1:T(8,128)} async-done(((f32[1536,2,1024]{2,0,1:T(8,128)}), f32[1536,2,512]{2,0,1:T(8,128)}) %reduce-scatter.25.cloned.1.call-update) | async-done | bytes 6291472 | tf_op jit(solution)/shard_map/reduce_scatter | solution.py:68
  1095.6 72.3 %reduce-scatter.45.cloned.1.call-done = f32[1536,1,512]{2,0,1:T(8,128)} async-done(((f32[1536,1,1024]{2,0,1:T(8,128)}), f32[1536,1,512]{2,0,1:T(8,128)}) %reduce-scatter.45.cloned.1.call-update) | async-done | bytes 3145744 | tf_op jit(solution)/shard_map/reduce_scatter | solution.py:68
  1167.9 146.6 %reduce-scatter.33.cloned.1.call-done = f32[1536,2,512]{2,0,1:T(8,128)} async-done(((f32[1536,2,1024]{2,0,1:T(8,128)}), f32[1536,2,512]{2,0,1:T(8,128)}) %reduce-scatter.33.cloned.1.call-update) | async-done | bytes 6291472 | tf_op jit(solution)/shard_map/reduce_scatter | solution.py:68
  1322.2 74.8 %all-gather.38.cloned.1.call-done = bf16[1536,2,1024]{2,0,1:T(8,128)(2,1)} async-done(((bf16[1536,2,512]{2,0,1:T(8,128)(2,1)}), bf16[1536,2,1024]{2,0,1:T(8,128)(2,1)}) %all-gather.38.cloned.1.call-update) | async-done | bytes 6291472 | tf_op jit(solution)/shard_map/all_gather | solution.py:72
  1409.0 70.5 %all-gather.46.cloned.1.call-done = bf16[1536,2,1024]{2,0,1:T(8,128)(2,1)} async-done(((bf16[1536,2,512]{2,0,1:T(8,128)(2,1)}), bf16[1536,2,1024]{2,0,1:T(8,128)(2,1)}) %all-gather.46.cloned.1.call-update) | async-done | bytes 6291472 | tf_op jit(solution)/shard_map/all_gather | solution.py:72
  1491.3 60.8 %reduce-scatter.39.cloned.1.call-done = f32[192,1024]{1,0:T(8,128)} async-done(((f32[1536,1024]{1,0:T(8,128)}), f32[192,1024]{1,0:T(8,128)}) %reduce-scatter.39.cloned.1.call-update) | async-done | bytes 786448 | tf_op jit(solution)/shard_map/reduce_scatter | solution.py:82
  1553.6 69.5 %reduce-scatter.47.cloned.1.call-done = f32[192,1024]{1,0:T(8,128)} async-done(((f32[1536,1024]{1,0:T(8,128)}), f32[192,1024]{1,0:T(8,128)}) %reduce-scatter.47.cloned.1.call-update) | async-done | bytes 786448 | tf_op jit(solution)/shard_map/reduce_scatter | solution.py:82
  1687.3 35.3 %all-gather.48.cloned.1.call-done = bf16[1536,1024]{1,0:T(8,128)(2,1)} async-done(((bf16[192,1024]{1,0:T(8,128)(2,1)}), bf16[1536,1024]{1,0:T(8,128)(2,1)}) %all-gather.48.cloned.1.call-update) | async-done | bytes 3145744 | tf_op jit(solution)/shard_map/all_gather | solution.py:64
  1753.0 58.3 %while.99 = (s32[]{:T(128)}, f32[1536,128]{1,0:T(8,128)}, f32[1536,128]{1,0:T(8,128)}, f32[3,512,128]{2,1,0:T(8,128)}, s32[3,512]{1,0:T(4,128)}, /*index=5*/s32[...) while((s32[]{:T(128)}, f32[1536,128]{1,0:T(8,128)}, ...), condition=%wide.region_47.48_spmd.clone, body=%wide.region_45.47_spmd.clone.sunk | while | flops 1017642496 | bytes 79080288 | solution.py:195
  1814.2 52.1 %while.100 = (s32[]{:T(128)}, f32[1536,128]{1,0:T(8,128)}, f32[1536,128]{1,0:T(8,128)}, f32[3,512,128]{2,1,0:T(8,128)}, s32[3,512]{1,0:T(4,128)}, /*index=5*/s32...) while((s32[]{:T(128)}, f32[1536,128]{1,0:T(8,128)}, ...), condition=%wide.region_62.63_spmd.clone, body=%wide.region_60.62_spmd.clone.sunk | while | flops 1017642496 | bytes 79080288 | solution.py:195
  1975.7 50.3 %reduce-scatter.27.cloned.1.call-done = f32[192,1024]{1,0:T(8,128)} async-done(((f32[1536,1024]{1,0:T(8,128)}), f32[192,1024]{1,0:T(8,128)}) %reduce-scatter.27.cloned.1.call-update) | async-done | bytes 786448 | tf_op jit(solution)/shard_map/reduce_scatter | solution.py:82
  2034.3 62.8 %reduce-scatter.35.cloned.1.call-done = f32[192,1024]{1,0:T(8,128)} async-done(((f32[1536,1024]{1,0:T(8,128)}), f32[192,1024]{1,0:T(8,128)}) %reduce-scatter.35.cloned.1.call-update) | async-done | bytes 786448 | tf_op jit(solution)/shard_map/reduce_scatter | solution.py:82
  2387.9 64.0 %reduce-scatter.43.cloned.1.call-done = f32[192,1024]{1,0:T(8,128)} async-done(((f32[1536,1024]{1,0:T(8,128)}), f32[192,1024]{1,0:T(8,128)}) %reduce-scatter.43.cloned.1.call-update) | async-done | bytes 786448 | tf_op jit(solution)/shard_map/reduce_scatter | solution.py:82
  2453.7 68.6 %reduce-scatter.51.cloned.1.call-done = f32[192,1024]{1,0:T(8,128)} async-done(((f32[1536,1024]{1,0:T(8,128)}), f32[192,1024]{1,0:T(8,128)}) %reduce-scatter.51.cloned.1.call-update) | async-done | bytes 786448 | tf_op jit(solution)/shard_map/reduce_scatter | solution.py:82
  2579.0 38.0 %all-reduce = (f32[]{:T(128)}, f32[2,4,6]{2,1,0:T(4,128)S(1)}) all-reduce(f32[]{:T(128)S(6)} %add.430, f32[2,4,6]{2,1,0:T(4,128)S(1)} %maximum_add_fusion), channel_id=1, replica_groups=mesh['dp'=2,'row'=8,'col'=2] {'dp','row','col'}, use_global_device_ids=true, to_apply=%region_76.77 | all-reduce | flops 49 | bytes 392 | tf_op jit(solution)/shard_map/psum | solution.py:359
  (817 shorter events, 1433.2 us)
Async XLA Ops:
  161.6 250.2 %reduce-scatter.29.cloned.1.call-start = ((), (), s32[]{:S(2)}) async-start(), calls=%async_computation.35 | async-start | bytes 7077888 | tf_op jit(solution)/shard_map/reduce_scatter | solution.py:68
  206.2 207.1 %reduce-scatter.21.cloned.1.call-start = ((), (), s32[]{:S(2)}) async-start(), calls=%async_computation.26 | async-start | bytes 7077888 | tf_op jit(solution)/shard_map/reduce_scatter | solution.py:68
  317.0 317.7 %reduce-scatter.23.cloned.1.call-start = ((), (), s32[]{:S(2)}) async-start(), calls=%async_computation.27 | async-start | bytes 7077888 | tf_op jit(solution)/shard_map/reduce_scatter | solution.py:82
  471.7 178.3 %reduce-scatter.31.cloned.1.call-start = ((), (), s32[]{:S(2)}) async-start(), calls=%async_computation.36 | async-start | bytes 7077888 | tf_op jit(solution)/shard_map/reduce_scatter | solution.py:82
  679.6 183.0 %all-gather.32.cloned.1.call-start = ((), (), s32[]{:S(2)}) async-start(), calls=%async_computation.37 | async-start | bytes 3538944 | tf_op jit(solution)/shard_map/all_gather | solution.py:64
  680.7 260.5 %reduce-scatter.37.cloned.1.call-start = ((), (), s32[]{:S(2)}) async-start(), calls=%async_computation.42 | async-start | bytes 9437184 | tf_op jit(solution)/shard_map/reduce_scatter | solution.py:68
  694.8 393.1 %reduce-scatter.25.cloned.1.call-start = ((), (), s32[]{:S(2)}) async-start(), calls=%async_computation.30 | async-start | bytes 18874368 | tf_op jit(solution)/shard_map/reduce_scatter | solution.py:68
  796.3 371.7 %reduce-scatter.45.cloned.1.call-start = ((), (), s32[]{:S(2)}) async-start(), calls=%async_computation.50 | async-start | bytes 9437184 | tf_op jit(solution)/shard_map/reduce_scatter | solution.py:68
  831.9 482.7 %reduce-scatter.33.cloned.1.call-start = ((), (), s32[]{:S(2)}) async-start(), calls=%async_computation.38 | async-start | bytes 18874368 | tf_op jit(solution)/shard_map/reduce_scatter | solution.py:68
  874.8 522.2 %all-gather.38.cloned.1.call-start = ((), (), s32[]{:S(2)}) async-start(), calls=%async_computation.43 | async-start | bytes 9437184 | tf_op jit(solution)/shard_map/all_gather | solution.py:72
  1095.6 383.9 %all-gather.46.cloned.1.call-start = ((), (), s32[]{:S(2)}) async-start(), calls=%async_computation.51 | async-start | bytes 9437184 | tf_op jit(solution)/shard_map/all_gather | solution.py:72
  1322.2 229.9 %reduce-scatter.39.cloned.1.call-start = ((), (), s32[]{:S(2)}) async-start(), calls=%async_computation.44 | async-start | bytes 7077888 | tf_op jit(solution)/shard_map/reduce_scatter | solution.py:82
  1409.0 214.2 %reduce-scatter.47.cloned.1.call-start = ((), (), s32[]{:S(2)}) async-start(), calls=%async_computation.52 | async-start | bytes 7077888 | tf_op jit(solution)/shard_map/reduce_scatter | solution.py:82
  1491.2 191.9 %all-gather.40.cloned.1.call-start = ((), (), s32[]{:S(2)}) async-start(), calls=%async_computation.45 | async-start | bytes 3538944 | tf_op jit(solution)/shard_map/all_gather | solution.py:64
  1726.6 154.6 %all-gather.26.cloned.1.call-start = ((), (), s32[]{:S(2)}) async-start(), calls=%async_computation.31 | async-start | bytes 4718592 | tf_op jit(solution)/shard_map/all_gather | solution.py:72
  1727.2 162.8 %all-gather.34.cloned.1.call-start = ((), (), s32[]{:S(2)}) async-start(), calls=%async_computation.39 | async-start | bytes 4718592 | tf_op jit(solution)/shard_map/all_gather | solution.py:72
  1727.8 210.5 %all-gather.50.cloned.1.call-start = ((), (), s32[]{:S(2)}) async-start(), calls=%async_computation.55 | async-start | bytes 3538944 | tf_op jit(solution)/shard_map/all_gather | solution.py:72
  1889.9 207.1 %reduce-scatter.35.cloned.1.call-start = ((), (), s32[]{:S(2)}) async-start(), calls=%async_computation.40 | async-start | bytes 7077888 | tf_op jit(solution)/shard_map/reduce_scatter | solution.py:82
  1898.8 287.2 %reduce-scatter.59.cloned.1.call-start = ((), (), s32[]{:S(2)}) async-start(), calls=%async_computation.60 | async-start | bytes 6291456 | tf_op jit(solution)/shard_map/reduce_scatter | solution.py:351
  1910.4 449.7 %reduce-scatter.55.cloned.1.call-start = ((), (), s32[]{:S(2)}) async-start(), calls=%async_computation.58 | async-start | bytes 12582912 | tf_op jit(solution)/shard_map/reduce_scatter | solution.py:349
  1932.1 437.3 %reduce-scatter.57.cloned.1.call-start = ((), (), s32[]{:S(2)}) async-start(), calls=%async_computation.59 | async-start | bytes 1572864 | tf_op jit(solution)/shard_map/reduce_scatter | solution.py:350
  1938.2 441.7 %reduce-scatter.53.cloned.1.call-start = ((), (), s32[]{:S(2)}) async-start(), calls=%async_computation.57 | async-start | bytes 4718592 | tf_op jit(solution)/shard_map/reduce_scatter | solution.py:348
  1960.3 491.6 %reduce-scatter.43.cloned.1.call-start = ((), (), s32[]{:S(2)}) async-start(), calls=%async_computation.48 | async-start | bytes 7077888 | tf_op jit(solution)/shard_map/reduce_scatter | solution.py:82
  1968.0 554.2 %reduce-scatter.51.cloned.1.call-start = ((), (), s32[]{:S(2)}) async-start(), calls=%async_computation.56 | async-start | bytes 7077888 | tf_op jit(solution)/shard_map/reduce_scatter | solution.py:82
  (157 other events, 4337.0 us)
Sparse Core Ops, SparseCore 0:
  53.6 47.3 all-gather.19
  160.1 38.8 all-gather.29
  241.1 58.8 reduce-scatter.28
  317.1 58.8 reduce-scatter.20
  471.9 68.6 reduce-scatter.22
  543.4 68.1 reduce-scatter.30
  687.7 55.5 all-gather.23
  865.3 75.8 reduce-scatter.36
  943.5 144.4 reduce-scatter.24
  1090.8 77.0 reduce-scatter.44
  1170.1 144.4 reduce-scatter.32
  1316.5 80.3 all-gather.37
  1399.1 80.3 all-gather.45
  1482.2 69.7 reduce-scatter.38
  1554.9 68.1 reduce-scatter.46
  1781.2 44.9 all-gather.25
  1828.1 44.9 all-gather.33
  1956.1 69.7 reduce-scatter.26
  2028.8 68.1 reduce-scatter.34
  2100.5 85.5 reduce-scatter.58
  2188.3 122.1 reduce-scatter.54
  2336.5 43.3 reduce-scatter.52
  2382.1 69.8 reduce-scatter.42
  2454.1 68.1 reduce-scatter.50
  (13 shorter events, 435.9 us)
where the time goes:
time: 2750 us; the launch traced here: 2740 us
  waiting for transfers between devices  1430 us (52%)
  matrix products  565 us (21%)
  local copies, waits for them, and re-layouts  434 us (16%)
  other arithmetic  162 us (6%)
  blocking collectives  89.5 us (3%)
  starting transfers between devices  28.3 us (1%)
    reduce_scatter x8, waiting for transfers between devices, sum_units(): lax.psum_scatter(partial_sums, 'col', scatter_dimension=2, tiled=True)  454 us
    reduce_scatter x8, waiting for transfers between devices, sum_tokens(): lax.psum_scatter(jnp.einsum(formula, left_side, right_side, preferred_ele...  376 us
    all_gather x8, waiting for transfers between devices, gather_tokens(): return lax.all_gather(rows_low, 'row', axis=0, tiled=True)  195 us
    gather x22, local copies, waits for them, and re-layouts, rotary_tables(): starts = jnp.searchsorted(segment, segment, side='left')  185 us
    all_gather x6, waiting for transfers between devices, gather_units(): return lax.all_gather(units_low, 'col', axis=2, tiled=True)  155 us
    unnamed x201, local copies, waits for them, and re-layouts  88.1 us
    all_to_all x1, waiting for transfers between devices, body(): lax.all_to_all(sent_streams, 'dp', split_axis=2, concat_axis=2, tiled=True)  85.2 us
    all_to_all x1, waiting for transfers between devices, body(): lax.all_to_all(sent_cot, 'dp', split_axis=2, concat_axis=2, tiled=True)  67.1 us
  transfers between devices with their start and end apart: 41, of which 28 were waited for; matrix products, arithmetic and copies ran while one was open for 34% of the time, Pallas kernels for 0%

commit v1 on v0

v1 whole, which is shorter than its diff:
```python
import math

import jax
import jax.numpy as jnp
from jax import lax
from jax.sharding import PartitionSpec as P

D = 2048
HEAD = 128
STREAMS = 4
MICRO = 2


HIGHEST = lax.Precision.HIGHEST
norm_eps = 1e-05
beta_first = 0.9
beta_second = 0.95
adam_eps = 1e-08
learning_rate = 0.05
weight_decay = 0.1


def rotary_tables(segment):
    length = segment.shape[0]
    places = jnp.arange(length, dtype=jnp.int32)
    starts = jnp.sum((segment[None, :] < segment[:, None]).astype(jnp.int32), axis=1)
    offsets = (places - starts).astype(jnp.float32)
    halves = jnp.arange(HEAD // 2, dtype=jnp.float32)
    inverse = jnp.exp(halves * (-2.0 * math.log(10000.0) / HEAD))
    angles = offsets[:, None] * inverse[None, :]
    return (jnp.cos(angles), jnp.sin(angles))


def rotate(values_in, cosine, sine):
    half_width = values_in.shape[-1] // 2
    leading = values_in[..., :half_width]
    trailing = values_in[..., half_width:]
    return jnp.concatenate(
        [leading * cosine - trailing * sine, leading * sine + trailing * cosine], axis=-1
    )


def norm_forward(hidden):
    means = jnp.sum(hidden, axis=-1, keepdims=True) / D
    squares = jnp.sum(hidden * hidden, axis=-1, keepdims=True) / D
    inverse = lax.rsqrt(squares - means * means + norm_eps)
    return ((hidden - means) * inverse, inverse)


def norm_backward(upstream, normed, inverse):
    mean_one = jnp.sum(upstream, axis=-1, keepdims=True) / D
    mean_two = jnp.sum(upstream * normed, axis=-1, keepdims=True) / D
    return inverse * (upstream - mean_one - normed * mean_two)


def gather_tokens(rows_low):
    return lax.all_gather(rows_low, "row", axis=0, tiled=True)


def sum_tokens(partial_sums):
    return lax.psum_scatter(
        partial_sums.astype(jnp.bfloat16), "row", scatter_dimension=0, tiled=True
    ).astype(jnp.float32)


def to_work(home_rows):
    n_dp, n_col = lax.axis_size("dp"), lax.axis_size("col")
    rows, width = home_rows.shape[1:]
    slot = rows // n_dp
    parts = home_rows.reshape(n_col, n_dp, slot, width).transpose(1, 0, 2, 3)
    parts = lax.all_to_all(
        parts.reshape(n_dp * n_col, slot, width),
        ("dp", "col"),
        split_axis=0,
        concat_axis=0,
        tiled=True,
    )
    parts = parts.reshape(n_dp, n_col, slot, width).transpose(0, 2, 1, 3)
    return parts.reshape(rows, n_col * width)


def to_home(work_rows):
    n_dp, n_col = lax.axis_size("dp"), lax.axis_size("col")
    rows, width = work_rows.shape[0], work_rows.shape[1] // n_col
    slot = rows // n_dp
    parts = work_rows.reshape(n_dp, slot, n_col, width).transpose(0, 2, 1, 3)
    parts = lax.all_to_all(
        parts.reshape(n_dp * n_col, slot, width),
        ("dp", "col"),
        split_axis=0,
        concat_axis=0,
        tiled=True,
    )
    parts = parts.reshape(n_dp, n_col, slot, width).transpose(1, 0, 2, 3)
    return parts.reshape(n_col, rows, width)


def gather_in(weight_low):
    return lax.all_gather(weight_low, ("col", "dp"), axis=1, tiled=True)


def gather_out(weight_low):
    return lax.all_gather(
        lax.all_gather(weight_low, "dp", axis=0, tiled=True), "col", axis=1, tiled=True
    )


def scatter_in(grad):
    return lax.psum_scatter(
        grad.astype(jnp.bfloat16), ("col", "dp"), scatter_dimension=1, tiled=True
    ).astype(jnp.float32)


def scatter_out(grad):
    half = lax.psum_scatter(grad.astype(jnp.bfloat16), "col", scatter_dimension=1, tiled=True)
    return lax.psum_scatter(half, "dp", scatter_dimension=0, tiled=True).astype(jnp.float32)


def combine(weights, stream_set):
    total = weights[0] * stream_set[:, 0]
    for index in range(1, STREAMS):
        total = total + weights[index] * stream_set[:, index]
    return total


def mat(left, right):
    return jnp.sum(left[:, :, None] * right[None, :, :], axis=1)


def block_masks(segment):
    length = segment.shape[0]
    block_rows = min(512, length)
    blocks = length // block_rows
    places = jnp.arange(length, dtype=jnp.int32)
    return (length, block_rows, blocks, places)


def masked_scores(query_part, key_low, segment_part, place_part, segment, places):
    scores = jnp.einsum(
        "qe,ke->qk", query_part, key_low, preferred_element_type=jnp.float32
    ) * HEAD ** (-0.5)
    allowed = (segment_part[:, None] == segment[None, :]) & (places[None, :] <= place_part[:, None])
    return jnp.where(allowed, scores, -1e30)


def attend_forward(query_low, key_low, value_low, segment):
    length, block_rows, blocks, places = block_masks(segment)

    def one_block(inputs):
        query_part, segment_part, place_part = inputs
        scores = masked_scores(query_part, key_low, segment_part, place_part, segment, places)
        largest = jnp.max(scores, axis=-1, keepdims=True)
        weights = jnp.exp(scores - largest)
        totals = jnp.sum(weights, axis=-1, keepdims=True)
        probs = (weights / totals).astype(jnp.bfloat16)
        outputs = jnp.dot(probs, value_low, preferred_element_type=jnp.float32)
        return (outputs, (largest + jnp.log(totals))[:, 0])

    outputs, log_totals = lax.map(
        one_block,
        (
            query_low.reshape(blocks, block_rows, HEAD),
            segment.reshape(blocks, block_rows),
            places.reshape(blocks, block_rows),
        ),
    )
    return (outputs.reshape(length, HEAD), log_totals.reshape(length))


def attend_backward(grad_low, query_low, key_low, value_low, log_totals, segment):
    length, block_rows, blocks, places = block_masks(segment)

    def one_block(carry, inputs):
        grad_keys, grad_values = carry
        query_part, grad_part, log_part, segment_part, place_part = inputs
        scores = masked_scores(query_part, key_low, segment_part, place_part, segment, places)
        probs = jnp.exp(scores - log_part[:, None])
        grad_probs = jnp.einsum(
            "qe,ke->qk", grad_part, value_low, preferred_element_type=jnp.float32
        )
        inner = jnp.sum(probs * grad_probs, axis=-1, keepdims=True)
        grad_scores = (probs * (grad_probs - inner) * HEAD ** (-0.5)).astype(jnp.bfloat16)
        grad_queries = jnp.dot(grad_scores, key_low, preferred_element_type=jnp.float32)
        grad_keys = grad_keys + jnp.einsum(
            "qk,qe->ke", grad_scores, query_part, preferred_element_type=jnp.float32
        )
        grad_values = grad_values + jnp.einsum(
            "qk,qe->ke", probs.astype(jnp.bfloat16), grad_part, preferred_element_type=jnp.float32
        )
        return ((grad_keys, grad_values), grad_queries)

    zeros_rows = jnp.zeros((length, HEAD), jnp.float32)
    carried, grad_queries = lax.scan(
        one_block,
        (zeros_rows, zeros_rows),
        (
            query_low.reshape(blocks, block_rows, HEAD),
            grad_low.reshape(blocks, block_rows, HEAD),
            log_totals.reshape(blocks, block_rows),
            segment.reshape(blocks, block_rows),
            places.reshape(blocks, block_rows),
        ),
    )
    return (grad_queries.reshape(length, HEAD), carried[0], carried[1])


def adam_update(weight, grad_sum, moment_one, moment_two, clip_factor, step_value):
    clipped = grad_sum * clip_factor
    new_one = beta_first * moment_one + (1.0 - beta_first) * clipped
    new_two = beta_second * moment_two + (1.0 - beta_second) * clipped * clipped
    fix_one = 1.0 - jnp.power(beta_first, step_value)
    fix_two = 1.0 - jnp.power(beta_second, step_value)
    new_weight = weight - learning_rate * (
        new_one / fix_one / (jnp.sqrt(new_two / fix_two) + adam_eps) + weight_decay * weight
    )
    return (new_weight, new_one, new_two)


def body(
    streams,
    cotangent,
    destination,
    segments,
    attention_in,
    feedforward_in,
    attention_out,
    feedforward_out,
    attention_in_moment,
    feedforward_in_moment,
    attention_out_moment,
    feedforward_out_moment,
    attention_in_second,
    feedforward_in_second,
    attention_out_second,
    feedforward_out_second,
    hyper_weights,
    hyper_moment,
    hyper_second,
    step_count,
):
    low = jnp.bfloat16
    n_dp = lax.axis_size("dp")
    rows = destination.shape[1]
    group_tokens = segments.shape[2]
    slot = rows // n_dp
    home_dp, home_row, col_index = (
        lax.axis_index("dp"),
        lax.axis_index("row"),
        lax.axis_index("col"),
    )
    attention_in_low = gather_in(attention_in.astype(low))
    attention_out_low = gather_out(attention_out.astype(low))
    feedforward_in_low = gather_in(feedforward_in.astype(low))
    feedforward_out_low = gather_out(feedforward_out.astype(low))

    a0, m0, c0 = hyper_weights[0, :, 0], hyper_weights[0, :, 1:5], hyper_weights[0, :, 5]
    a1, m1, c1 = hyper_weights[1, :, 0], hyper_weights[1, :, 1:5], hyper_weights[1, :, 5]
    m01 = mat(m0, m1)
    forward_mix = jnp.sum(m0 * a1[None, :], axis=1)
    forward_branch = jnp.sum(a1 * c0)
    backward_mix = jnp.sum(m1 * c0[:, None], axis=0)
    backward_branch = jnp.sum(c0 * a1)

    group = destination // group_tokens
    sent = (
        group * slot + destination - group * group_tokens - home_row * rows - home_dp * slot
    )
    orders = jnp.argsort(sent, axis=1)

    def sort_rows(values_in):
        return jnp.stack([values_in[index][orders[index]] for index in range(MICRO)])

    def unsort_rows(values_in):
        return jnp.stack([values_in[index][sent[index]] for index in range(MICRO)])

    hidden_att = to_work(sort_rows(combine(a0, streams)))
    hidden_mix = to_work(sort_rows(combine(forward_mix, streams)))
    branch_rows_ffn = to_work(sort_rows(combine(c1, cotangent)).astype(low))
    grad_mix_rows = to_work(sort_rows(combine(backward_mix, cotangent)))
    gram = jnp.stack(
        [
            jnp.stack([jnp.sum(streams[:, i] * cotangent[:, j]) for j in range(STREAMS)])
            for i in range(STREAMS)
        ]
    )

    segment = lax.dynamic_index_in_dim(segments[:, 0], col_index, 0, keepdims=False)
    cosine, sine = rotary_tables(segment)

    normed_att, inverse_att = norm_forward(hidden_att)
    rows_att = gather_tokens(normed_att.astype(low))
    qkv = jnp.einsum("td,kdu->ktu", rows_att, attention_in_low, preferred_element_type=jnp.float32)
    heads = qkv.shape[2] // HEAD
    qkv = qkv.reshape(3, group_tokens, heads, HEAD).transpose(0, 2, 1, 3)
    query_low = rotate(qkv[0], cosine, sine).astype(low)
    key_low = rotate(qkv[1], cosine, sine).astype(low)
    value_low = qkv[2].astype(low)
    heads_out, log_totals = jax.vmap(attend_forward, in_axes=(0, 0, 0, None))(
        query_low, key_low, value_low, segment
    )
    heads_low = heads_out.astype(low).transpose(1, 0, 2).reshape(group_tokens, heads * HEAD)
    branch_att = sum_tokens(
        jnp.dot(heads_low, attention_out_low, preferred_element_type=jnp.float32)
    )

    hidden_ffn = hidden_mix + forward_branch * branch_att
    normed_ffn, inverse_ffn = norm_forward(hidden_ffn)
    rows_ffn = gather_tokens(normed_ffn.astype(low))
    grad_rows_ffn = gather_tokens(branch_rows_ffn)
    gate_pre = jnp.dot(rows_ffn, feedforward_in_low[0], preferred_element_type=jnp.float32)
    up_pre = jnp.dot(rows_ffn, feedforward_in_low[1], preferred_element_type=jnp.float32)
    sigma = jax.nn.sigmoid(gate_pre)
    silu = gate_pre * sigma
    hidden_low = (silu * up_pre).astype(low)
    branch_ffn = sum_tokens(
        jnp.dot(hidden_low, feedforward_out_low, preferred_element_type=jnp.float32)
    )
    grad_hidden = jnp.einsum(
        "td,ud->tu", grad_rows_ffn, feedforward_out_low, preferred_element_type=jnp.float32
    )
    grad_gate = (grad_hidden * up_pre * sigma * (1.0 + gate_pre * (1.0 - sigma))).astype(low)
    grad_up = (grad_hidden * silu).astype(low)
    grad_normed = sum_tokens(
        jnp.einsum(
            "tu,du->td", grad_gate, feedforward_in_low[0], preferred_element_type=jnp.float32
        )
        + jnp.einsum(
            "tu,du->td", grad_up, feedforward_in_low[1], preferred_element_type=jnp.float32
        )
    )
    shard_feedforward_out = scatter_out(
        jnp.einsum("tu,td->ud", hidden_low, grad_rows_ffn, preferred_element_type=jnp.float32)
    )
    shard_feedforward_in = scatter_in(
        jnp.stack(
            [
                jnp.einsum("td,tu->du", rows_ffn, grad, preferred_element_type=jnp.float32)
                for grad in (grad_gate, grad_up)
            ]
        )
    )
    grad_hidden_ffn = norm_backward(grad_normed, normed_ffn, inverse_ffn)
    grad_rows_att = gather_tokens(
        (grad_mix_rows + backward_branch * grad_hidden_ffn).astype(low)
    )
    shard_attention_out = scatter_out(
        jnp.einsum("tu,td->ud", heads_low, grad_rows_att, preferred_element_type=jnp.float32)
    )
    grad_heads = jnp.einsum(
        "td,ud->tu", grad_rows_att, attention_out_low, preferred_element_type=jnp.float32
    ).astype(low)
    grad_heads = grad_heads.reshape(group_tokens, heads, HEAD).transpose(1, 0, 2)
    grad_q, grad_k, grad_v = jax.vmap(attend_backward, in_axes=(0, 0, 0, 0, 0, None))(
        grad_heads, query_low, key_low, value_low, log_totals, segment
    )
    grad_units = (
        jnp.stack([rotate(grad_q, cosine, -sine), rotate(grad_k, cosine, -sine), grad_v])
        .astype(low)
        .transpose(0, 2, 1, 3)
        .reshape(3, group_tokens, heads * HEAD)
    )
    shard_attention_in = scatter_in(
        jnp.einsum("td,ktu->kdu", rows_att, grad_units, preferred_element_type=jnp.float32)
    )
    grad_normed = sum_tokens(
        jnp.einsum("ktu,kdu->td", grad_units, attention_in_low, preferred_element_type=jnp.float32)
    )
    grad_hidden_att = norm_backward(grad_normed, normed_att, inverse_att)

    home_att = unsort_rows(to_home(branch_att.astype(low)))
    home_ffn = unsort_rows(to_home(branch_ffn.astype(low)))
    home_grad_ffn = unsort_rows(to_home(grad_hidden_ffn.astype(low)))
    home_grad_att = unsort_rows(to_home(grad_hidden_att.astype(low)))
    home_att, home_ffn, home_grad_ffn, home_grad_att = (
        value.astype(jnp.float32) for value in (home_att, home_ffn, home_grad_ffn, home_grad_att)
    )
    mix_branch = jnp.sum(m1 * c0[:, None], axis=0)
    streams_out = jnp.stack(
        [
            combine(m01[:, j], streams) + mix_branch[j] * home_att + c1[j] * home_ffn
            for j in range(STREAMS)
        ],
        axis=1,
    )
    mix_grad = jnp.sum(m0 * a1[None, :], axis=1)
    stream_grad = jnp.stack(
        [
            combine(m01[i], cotangent) + mix_grad[i] * home_grad_ffn + a0[i] * home_grad_att
            for i in range(STREAMS)
        ],
        axis=1,
    )
    dots = jnp.concatenate(
        [
            gram.reshape(-1),
            jnp.stack([jnp.sum(cotangent[:, j] * home_att) for j in range(STREAMS)]),
            jnp.stack([jnp.sum(cotangent[:, j] * home_ffn) for j in range(STREAMS)]),
            jnp.stack([jnp.sum(streams[:, i] * home_grad_ffn) for i in range(STREAMS)]),
            jnp.stack([jnp.sum(streams[:, i] * home_grad_att) for i in range(STREAMS)]),
            jnp.sum(home_att * home_grad_ffn)[None],
        ]
    )
    square = (
        jnp.sum(shard_attention_in * shard_attention_in)
        + jnp.sum(shard_feedforward_in * shard_feedforward_in)
        + jnp.sum(shard_attention_out * shard_attention_out)
        + jnp.sum(shard_feedforward_out * shard_feedforward_out)
    )
    totals = lax.psum(jnp.concatenate([dots, square[None]]), ("dp", "row", "col"))
    gram = totals[:16].reshape(STREAMS, STREAMS)
    att_cot, ffn_cot = totals[16:20], totals[20:24]
    streams_ffn, streams_att = totals[24:28], totals[28:32]
    att_ffn, square_total = totals[32], totals[33]
    grad_m1 = mat(m0.T, gram) + c0[:, None] * att_cot[None, :]
    grad_a1 = jnp.sum(m0 * streams_ffn[:, None], axis=0) + c0 * att_ffn
    grad_m0 = mat(gram, m1.T) + streams_ffn[:, None] * a1[None, :]
    grad_c0 = jnp.sum(m1 * att_cot[None, :], axis=1) + a1 * att_ffn
    hyper_grad = jnp.stack(
        [
            jnp.concatenate([streams_att[:, None], grad_m0, grad_c0[:, None]], axis=1),
            jnp.concatenate([grad_a1[:, None], grad_m1, ffn_cot[:, None]], axis=1),
        ]
    )
    grad_norm = jnp.sqrt(square_total + jnp.sum(hyper_grad * hyper_grad))
    clip_factor = 1.0 / jnp.maximum(grad_norm, 1.0)
    step_value = step_count[0].astype(jnp.float32)
    attention_in_new = adam_update(
        attention_in,
        shard_attention_in,
        attention_in_moment,
        attention_in_second,
        clip_factor,
        step_value,
    )
    feedforward_in_new = adam_update(
        feedforward_in,
        shard_feedforward_in,
        feedforward_in_moment,
        feedforward_in_second,
        clip_factor,
        step_value,
    )
    attention_out_new = adam_update(
        attention_out,
        shard_attention_out,
        attention_out_moment,
        attention_out_second,
        clip_factor,
        step_value,
    )
    feedforward_out_new = adam_update(
        feedforward_out,
        shard_feedforward_out,
        feedforward_out_moment,
        feedforward_out_second,
        clip_factor,
        step_value,
    )
    hyper_new = adam_update(
        hyper_weights, hyper_grad, hyper_moment, hyper_second, clip_factor, step_value
    )
    return (
        streams_out,
        stream_grad,
        grad_norm.reshape(1),
        shard_attention_in,
        shard_feedforward_in,
        shard_attention_out,
        shard_feedforward_out,
        hyper_grad,
        attention_in_new[0],
        feedforward_in_new[0],
        attention_out_new[0],
        feedforward_out_new[0],
        hyper_new[0],
        attention_in_new[1],
        feedforward_in_new[1],
        attention_out_new[1],
        feedforward_out_new[1],
        hyper_new[1],
        attention_in_new[2],
        feedforward_in_new[2],
        attention_out_new[2],
        feedforward_out_new[2],
        hyper_new[2],
    )


def solution(mesh):
    placed = (
        P(None, None, ("dp", "row"), "col"),
        P(None, None, ("dp", "row"), "col"),
        P(None, ("dp", "row")),
        P(None, "dp", None),
        P(None, ("col", "dp"), "row"),
        P(None, ("col", "dp"), "row"),
        P(("row", "dp"), "col"),
        P(("row", "dp"), "col"),
        P(None, ("col", "dp"), "row"),
        P(None, ("col", "dp"), "row"),
        P(("row", "dp"), "col"),
        P(("row", "dp"), "col"),
        P(None, ("col", "dp"), "row"),
        P(None, ("col", "dp"), "row"),
        P(("row", "dp"), "col"),
        P(("row", "dp"), "col"),
        P(),
        P(),
        P(),
        P(),
    )
    return jax.shard_map(
        body,
        mesh=mesh,
        in_specs=placed,
        out_specs=(
            P(None, None, ("dp", "row"), "col"),
            P(None, None, ("dp", "row"), "col"),
            P(),
            P(None, ("col", "dp"), "row"),
            P(None, ("col", "dp"), "row"),
            P(("row", "dp"), "col"),
            P(("row", "dp"), "col"),
            P(),
            P(None, ("col", "dp"), "row"),
            P(None, ("col", "dp"), "row"),
            P(("row", "dp"), "col"),
            P(("row", "dp"), "col"),
            P(),
            P(None, ("col", "dp"), "row"),
            P(None, ("col", "dp"), "row"),
            P(("row", "dp"), "col"),
            P(("row", "dp"), "col"),
            P(),
            P(None, ("col", "dp"), "row"),
            P(None, ("col", "dp"), "row"),
            P(("row", "dp"), "col"),
            P(("row", "dp"), "col"),
            P(),
        ),
        check_vma=False,
    )
```

time: 2750 us -> 1300 us (0.47)
  waiting for transfers between devices: 1430 us -> 556 us
  local copies, waits for them, and re-layouts: 434 us -> 108 us
  matrix products: 565 us -> 273 us
  other arithmetic: 162 us -> 194 us
  blocking collectives: 89.5 us -> 121 us
    reduce_scatter x20 -> x10, waiting for transfers between devices: 845 us -> 185 us  [the longest x2 95.6 us: scatter_in(): lax.psum_scatter(grad.astype(jnp.bfloat16), ('col', 'dp'), scatter_dimens...]
    dot_general x52 -> x15, matrix products: 479 us -> 148 us  [the longest x2 21.2 us: body(): jnp.einsum('td,tu->du', rows_ffn, grad, preferred_element_type=jnp.float32)]
    gather x30 -> x16, local copies, waits for them, and re-layouts: 227 us -> 17.9 us  [the longest x8 9.78 us: sort_rows(): values_in[index][orders[index]]]
    all_to_all x4 -> x5, waiting for transfers between devices: 189 us -> 42.1 us  [the longest x1 35 us: to_work(): lax.all_to_all(parts.reshape(n_dp * n_col, slot, width), ('dp', 'col'), s...]
    all_gather x9 -> x5, waiting for transfers between devices: 204 us -> 86 us  [the longest x2 50.5 us: gather_in(): return lax.all_gather(weight_low, ('col', 'dp'), axis=1, tiled=True)]
    all_to_all x0 -> x3, blocking collectives: none -> 74.5 us  [to_work(): lax.all_to_all(parts.reshape(n_dp * n_col, slot, width), ('dp', 'col'), s...]
    add x29 -> x11, other arithmetic: 3.74 us -> 72.6 us  [the longest x4 29.9 us: body(): combine(m01[i], cotangent) + mix_grad[i] * home_grad_ffn]
    unnamed x201 -> x191, local copies, waits for them, and re-layouts: 88.1 us -> 40.3 us
  transfers between devices with their start and end apart: 41 -> 24, of which waited for: 28 -> 14; matrix products, arithmetic and copies ran while one was open for 34% -> 32% of each run, Pallas kernels for 0% -> 0%
where the time goes in v1:
time: 1300 us
  waiting for transfers between devices  556 us (43%)
  matrix products  273 us (21%)
  other arithmetic  194 us (15%)
  blocking collectives  121 us (9%)
  local copies, waits for them, and re-layouts  108 us (8%)
  between operations  22.8 us (2%)
  starting transfers between devices  21.3 us (2%)
    all_gather x4, waiting for transfers between devices, gather_tokens(): return lax.all_gather(rows_low, 'row', axis=0, tiled=True)  240 us
    reduce_scatter x2, waiting for transfers between devices, scatter_in(): lax.psum_scatter(grad.astype(jnp.bfloat16), ('col', 'dp'), scatter_dimens...  95.6 us
    reduce_scatter x4, waiting for transfers between devices, sum_tokens(): lax.psum_scatter(partial_sums.astype(jnp.bfloat16), 'row', scatter_dimens...  77.9 us
    all_to_all x3, blocking collectives, to_work(): lax.all_to_all(parts.reshape(n_dp * n_col, slot, width), ('dp', 'col'), s...  74.5 us
    all_gather x2, waiting for transfers between devices, gather_in(): return lax.all_gather(weight_low, ('col', 'dp'), axis=1, tiled=True)  50.5 us
    unnamed x191, local copies, waits for them, and re-layouts  40.3 us
    psum x1, blocking collectives, body(): lax.psum(jnp.concatenate([dots, square[None]]), ('dp', 'row', 'col'))  39.3 us
    dot_general x3, matrix products, one_block(): jnp.einsum('qk,qe->ke', grad_scores, query_part, preferred_element_type=j...  36.4 us
  transfers between devices with their start and end apart: 24, of which 14 were waited for; matrix products, arithmetic and copies ran while one was open for 32% of the time, Pallas kernels for 0%

profile of v1, /device:TPU:0, one launch (start us, length us, event | category | flops | bytes accessed | tf_op | source)
XLA Modules:
  0.0 1296.4 jit_solution(10073883142513161248)
XLA Ops:
  29.0 37.7 %all_to_all.40 = f32[4,96,1024]{2,1,0:T(8,128)S(1)} all-to-all(f32[4,96,1024]{2,1,0:T(8,128)S(1)} %bitcast.817), channel_id=1, replica_groups=mesh['dp'=2,'row'=8,'col'=2] {'dp','col'}, dimensions={0} | all-to-all | bytes 3145728 | tf_op jit(solution)/shard_map/all_to_all | solution.py:71
  84.3 53.2 %all-gather.10.cloned.1.call-done = bf16[1536,2048]{1,0:T(8,128)(2,1)} async-done(((bf16[192,2048]{1,0:T(8,128)(2,1)}), bf16[1536,2048]{1,0:T(8,128)(2,1)}) %all-gather.10.cloned.1.call-update) | async-done | bytes 6291472 | tf_op jit(solution)/shard_map/all_gather | solution.py:57
  159.0 22.7 %while.30 = (s32[]{:T(128)}, bf16[3,2,512,128]{3,2,0,1:T(8,128)(2,1)S(1)}, f32[3,2,512]{2,1,0:T(2,128)}, s32[3,512]{1,0:T(4,128)S(1)}, s32[1536]{0:T(1024)S(1)},...) while((s32[]{:T(128)}, ...), condition=%wide.region_9.10_spmd.clone.clone, body=%wide.region_6.9_spmd.clone.sunk.clone | while | flops 826539008 | bytes 24431208 | solution.py:159
  206.5 35.0 %all-to-all-done.2 = f32[4,96,1024]{2,1,0:T(8,128)S(1)} async-done(((f32[4,96,1024]{2,1,0:T(8,128)}), f32[4,96,1024]{2,1,0:T(8,128)S(1)}, u32[]{:S(2)}, u32[]{:S(2)}) %all-to-all-start.2) | async-done | bytes 1572896 | tf_op jit(solution)/shard_map/all_to_all | solution.py:71
  243.3 15.7 %reduce-scatter.11.cloned.1.call-done = bf16[192,2048]{1,0:T(8,128)(2,1)} async-done(((bf16[1536,2048]{1,0:T(8,128)(2,1)}), bf16[192,2048]{1,0:T(8,128)(2,1)}) %reduce-scatter.11.cloned.1.call-update) | async-done | bytes 786448 | tf_op jit(solution)/shard_map/reduce_scatter | solution.py:61
  271.6 15.6 %all_to_all.41 = bf16[4,96,1024]{2,1,0:T(8,128)(2,1)S(1)} all-to-all(bf16[4,96,1024]{2,1,0:T(8,128)(2,1)S(1)} %bitcast.833), channel_id=1, replica_groups=mesh['dp'=2,'row'=8,'col'=2] {'dp','col'}, dimensions={0} | all-to-all | bytes 1572864 | tf_op jit(solution)/shard_map/all_to_all | solution.py:71
  289.1 50.5 %all-gather.18.cloned.1.call-done = bf16[2,2048,1024]{2,1,0:T(8,128)(2,1)} async-done(((bf16[2,512,1024]{2,1,0:T(8,128)(2,1)}), bf16[2,2048,1024]{2,1,0:T(8,128)(2,1)}) %all-gather.18.cloned.1.call-update) | async-done | bytes 8388624 | tf_op jit(solution)/shard_map/all_gather | solution.py:99
  339.6 66.7 %all-gather.16.cloned.1.call-done = bf16[1536,2048]{1,0:T(8,128)(2,1)} async-done(((bf16[192,2048]{1,0:T(8,128)(2,1)}), bf16[1536,2048]{1,0:T(8,128)(2,1)}) %all-gather.16.cloned.1.call-update) | async-done | bytes 6291472 | tf_op jit(solution)/shard_map/all_gather | solution.py:57
  406.3 12.6 fusion.65
  427.7 35.4 %all-gather.22.cloned.1.call-done = bf16[1024,2048]{1,0:T(8,128)(2,1)} async-done(((bf16[1024,1024]{1,0:T(8,128)(2,1)}), bf16[1024,2048]{1,0:T(8,128)(2,1)}) %all-gather.22.cloned.1.call-update) | async-done | bytes 4194320 | tf_op jit(solution)/shard_map/all_gather | solution.py:103
  463.2 66.9 %all-gather.24.cloned.1.call-done = bf16[1536,2048]{1,0:T(8,128)(2,1)} async-done(((bf16[192,2048]{1,0:T(8,128)(2,1)}), bf16[1536,2048]{1,0:T(8,128)(2,1)}) %all-gather.24.cloned.1.call-update) | async-done | bytes 6291472 | tf_op jit(solution)/shard_map/all_gather | solution.py:57
  530.0 18.1 %multiply_convert_fusion.1 = (bf16[1536,1024]{1,0:T(8,128)(2,1)}, bf16[1536,1024]{1,0:T(8,128)(2,1)}, bf16[1536,1024]{1,0:T(8,128)(2,1)}) fusion(f32[1536,1024]{1,0:T(8,128)} %fusion.65, f32[1536,1024]{1,0:T(8,128)} %fusion.66, bf16[1536,2048]{1,0:T(8,128)(2,1)} %all-gather.24.cloned.1.call-done, bf16[1024,2048]{1,0:T(8,128)(2,1)} %all-gather.22.cloned.1.call-done), kind=kOutput, calls=%fused_computation.85 | convolution fusion | flops 6466043904 | bytes 32505856 | tf_op jit(solution)/shard_map/td,ud->tu/dot_general | solution.py:318
  557.9 11.4 add_convert_fusion
  575.7 62.2 %reduce-scatter.15.cloned.1.call-done = bf16[192,2048]{1,0:T(8,128)(2,1)} async-done(((bf16[1536,2048]{1,0:T(8,128)(2,1)}), bf16[192,2048]{1,0:T(8,128)(2,1)}) %reduce-scatter.15.cloned.1.call-update) | async-done | bytes 786448 | tf_op jit(solution)/shard_map/reduce_scatter | solution.py:61
  674.5 21.2 %all_to_all.42 = f32[4,96,1024]{2,1,0:T(8,128)S(1)} all-to-all(f32[4,96,1024]{2,1,0:T(8,128)S(1)} %bitcast.818), channel_id=1, replica_groups=mesh['dp'=2,'row'=8,'col'=2] {'dp','col'}, dimensions={0} | all-to-all | bytes 3145728 | tf_op jit(solution)/shard_map/all_to_all | solution.py:71
  711.8 53.7 %all-gather.26.cloned.1.call-done = bf16[1536,2048]{1,0:T(8,128)(2,1)} async-done(((bf16[192,2048]{1,0:T(8,128)(2,1)}), bf16[1536,2048]{1,0:T(8,128)(2,1)}) %all-gather.26.cloned.1.call-update) | async-done | bytes 6291472 | tf_op jit(solution)/shard_map/all_gather | solution.py:57
  792.0 119.5 %while.31 = (s32[]{:T(128)}, f32[2,1536,128]{2,1,0:T(8,128)}, f32[2,1536,128]{2,1,0:T(8,128)S(1)}, f32[3,2,512,128]{3,2,0,1:T(8,128)}, s32[3,512]{1,0:T(4,128)},...) while((s32[]{:T(128)}, f32[2,1536,128]{2,1,0:T(8,128)}, ...), condition=%wide.region_21.22_spmd.clone.clone, body=%wide.region_19.21_spmd.clone.sunk.clone | while | flops 2039223296 | bytes 81035912 | solution.py:193
  814.9 11.8 fusion.281
  854.5 12.3 fusion.281
  894.5 12.3 fusion.281
  1040.8 50.2 %reduce-scatter.21.cloned.1.call-done = bf16[2,512,1024]{2,1,0:T(8,128)(2,1)} async-done(((bf16[2,2048,1024]{2,1,0:T(8,128)(2,1)}), bf16[2,512,1024]{2,1,0:T(8,128)(2,1)}) %reduce-scatter.21.cloned.1.call-update) | async-done | bytes 2097168 | tf_op jit(solution)/shard_map/reduce_scatter | solution.py:109
  1096.3 11.4 reduce-scatter.25.cloned.1.call-done
  1110.1 45.4 %reduce-scatter.19.cloned.1.call-done = bf16[3,512,256]{1,2,0:T(8,128)(2,1)} async-done(((bf16[3,2048,256]{1,2,0:T(8,128)(2,1)}), bf16[3,512,256]{1,2,0:T(8,128)(2,1)}) %reduce-scatter.19.cloned.1.call-update) | async-done | bytes 786448 | tf_op jit(solution)/shard_map/reduce_scatter | solution.py:109
  1178.8 39.3 %psum.7 = f32[34]{0:T(128)S(1)} all-reduce(f32[34]{0:T(128)S(1)} %concatenate.117), channel_id=1, replica_groups=mesh['dp'=2,'row'=8,'col'=2] {'dp','row','col'}, use_global_device_ids=true, to_apply=%region_68.69 | all-reduce | flops 34 | bytes 272 | tf_op jit(solution)/shard_map/psum | solution.py:409
  (451 shorter events, 534.6 us)
Async XLA Ops:
  8.0 76.2 %all-gather.12.cloned.1.call-start = ((), (), s32[]{:S(2)}) async-start(), calls=%async_computation.19 | async-start | bytes 3932160 | tf_op jit(solution)/shard_map/all_gather | solution.py:99
  11.4 126.0 %all-gather.10.cloned.1.call-start = ((), (), s32[]{:S(2)}) async-start(), calls=%async_computation.18 | async-start | bytes 7077888 | tf_op jit(solution)/shard_map/all_gather | solution.py:57
  71.3 113.0 %all-gather.14.cloned.1.call-start = ((), (), s32[]{:S(2)}) async-start(), calls=%async_computation.20 | async-start | bytes 1572864 | tf_op jit(solution)/shard_map/all_gather | solution.py:103
  78.6 180.5 %reduce-scatter.11.cloned.1.call-start = ((), (), s32[]{:S(2)}) async-start(), calls=%async_computation.21 | async-start | bytes 7077888 | tf_op jit(solution)/shard_map/reduce_scatter | solution.py:61
  190.4 72.1 %all-gather.20.cloned.1.call-start = ((), (), s32[]{:S(2)}) async-start(), calls=%async_computation.24 | async-start | bytes 3145728 | tf_op jit(solution)/shard_map/all_gather | solution.py:104
  193.2 146.5 %all-gather.18.cloned.1.call-start = ((), (), s32[]{:S(2)}) async-start(), calls=%async_computation.23 | async-start | bytes 10485760 | tf_op jit(solution)/shard_map/all_gather | solution.py:99
  202.2 39.3 %all-to-all-start.2 = ((f32[4,96,1024]{2,1,0:T(8,128)}), f32[4,96,1024]{2,1,0:T(8,128)S(1)}, u32[]{:S(2)}, u32[]{:S(2)}) async-start(f32[4,96,1024]{2,1,0:T(8,128)} %bitcast.69), calls=%async_computation.3 | async-start | bytes 3145728 | tf_op jit(solution)/shard_map/all_to_all | solution.py:71
  205.7 200.6 %all-gather.16.cloned.1.call-start = ((), (), s32[]{:S(2)}) async-start(), calls=%async_computation.22 | async-start | bytes 7077888 | tf_op jit(solution)/shard_map/all_gather | solution.py:57
  262.5 200.7 %all-gather.22.cloned.1.call-start = ((), (), s32[]{:S(2)}) async-start(), calls=%async_computation.25 | async-start | bytes 6291456 | tf_op jit(solution)/shard_map/all_gather | solution.py:103
  263.2 266.8 %all-gather.24.cloned.1.call-start = ((), (), s32[]{:S(2)}) async-start(), calls=%async_computation.27 | async-start | bytes 7077888 | tf_op jit(solution)/shard_map/all_gather | solution.py:57
  289.1 348.8 %reduce-scatter.15.cloned.1.call-start = ((), (), s32[]{:S(2)}) async-start(), calls=%async_computation.28 | async-start | bytes 7077888 | tf_op jit(solution)/shard_map/reduce_scatter | solution.py:61
  572.1 73.3 %all-to-all-start.1 = ((bf16[4,96,1024]{2,1,0:T(8,128)(2,1)}), bf16[4,96,1024]{2,1,0:T(8,128)(2,1)S(1)}, u32[]{:S(2)}, u32[]{:S(2)}) async-start(bf16[4,96,1024]{2,1,0:T(8,128)(2,1)} %bitcast.45), calls=%async_computation.2 | async-start | bytes 1572864 | tf_op jit(solution)/shard_map/all_to_all | solution.py:87
  645.4 13.3 %all-to-all-start.5 = ((bf16[4,96,1024]{2,1,0:T(8,128)(2,1)}), bf16[4,96,1024]{2,1,0:T(8,128)(2,1)}, u32[]{:S(2)}, u32[]{:S(2)}) async-start(bf16[4,96,1024]{2,1,0:T(8,128)(2,1)} %bitcast.116), calls=%async_computation.8 | async-start | bytes 1572864 | tf_op jit(solution)/shard_map/all_to_all | solution.py:87
  649.6 116.0 %all-gather.26.cloned.1.call-start = ((), (), s32[]{:S(2)}) async-start(), calls=%async_computation.29 | async-start | bytes 7077888 | tf_op jit(solution)/shard_map/all_gather | solution.py:57
  700.5 82.4 %reduce-scatter.27.cloned.1.call-start = ((), (), s32[]{:S(2)}) async-start(), calls=%async_computation.35 | async-start | bytes 6291456 | tf_op jit(solution)/shard_map/reduce_scatter | solution.py:115
  711.7 241.7 %reduce-scatter.23.cloned.1.call-start = ((), (), s32[]{:S(2)}) async-start(), calls=%async_computation.33 | async-start | bytes 1572864 | tf_op jit(solution)/shard_map/reduce_scatter | solution.py:115
  771.3 192.6 %reduce-scatter.13.cloned.1.call-start = ((), (), s32[]{:S(2)}) async-start(), calls=%async_computation.26 | async-start | bytes 7077888 | tf_op jit(solution)/shard_map/reduce_scatter | solution.py:61
  782.7 195.6 %reduce-scatter.29.cloned.1.call-start = ((), (), s32[]{:S(2)}) async-start(), calls=%async_computation.36 | async-start | bytes 3145728 | tf_op jit(solution)/shard_map/reduce_scatter | solution.py:116
  783.5 248.5 %reduce-scatter.17.cloned.1.call-start = ((), (), s32[]{:S(2)}) async-start(), calls=%async_computation.30 | async-start | bytes 7077888 | tf_op jit(solution)/shard_map/reduce_scatter | solution.py:61
  925.8 165.2 %reduce-scatter.21.cloned.1.call-start = ((), (), s32[]{:S(2)}) async-start(), calls=%async_computation.32 | async-start | bytes 10485760 | tf_op jit(solution)/shard_map/reduce_scatter | solution.py:109
  953.4 154.3 %reduce-scatter.25.cloned.1.call-start = ((), (), s32[]{:S(2)}) async-start(), calls=%async_computation.34 | async-start | bytes 786432 | tf_op jit(solution)/shard_map/reduce_scatter | solution.py:116
  953.9 201.6 %reduce-scatter.19.cloned.1.call-start = ((), (), s32[]{:S(2)}) async-start(), calls=%async_computation.31 | async-start | bytes 3932160 | tf_op jit(solution)/shard_map/reduce_scatter | solution.py:109
  967.6 15.1 %all-to-all-start.3 = ((bf16[4,96,1024]{2,1,0:T(8,128)(2,1)}), bf16[4,96,1024]{2,1,0:T(8,128)(2,1)S(1)}, u32[]{:S(2)}, u32[]{:S(2)}) async-start(bf16[4,96,1024]{2,1,0:T(8,128)(2,1)} %bitcast.75), calls=%async_computation.5 | async-start | bytes 1572864 | tf_op jit(solution)/shard_map/all_to_all | solution.py:87
  1036.1 124.0 %all-to-all-start.7 = ((bf16[4,96,1024]{2,1,0:T(8,128)(2,1)}), bf16[4,96,1024]{2,1,0:T(8,128)(2,1)S(1)}, u32[]{:S(2)}, u32[]{:S(2)}) async-start(bf16[4,96,1024]{2,1,0:T(8,128)(2,1)} %bitcast.147), calls=%async_computation.11 | async-start | bytes 1572864 | tf_op jit(solution)/shard_map/all_to_all | solution.py:87
  (89 other events, 1570.5 us)
Sparse Core Ops, SparseCore 0:
  11.3 58.8 all-gather.11
  72.4 64.9 all-gather.9
  139.0 19.9 all-gather.13
  190.6 68.4 reduce-scatter.10
  569.4 68.4 reduce-scatter.14
  711.9 54.6 reduce-scatter.26
  771.4 18.9 reduce-scatter.22
  793.3 69.7 reduce-scatter.12
  865.4 30.1 reduce-scatter.28
  925.9 68.4 reduce-scatter.16
  997.8 93.2 reduce-scatter.20
  1093.1 14.5 reduce-scatter.24
  1111.5 43.9 reduce-scatter.18
Sparse Core Ops, SparseCore 1:
  193.2 47.6 all-gather.19
  243.2 96.3 all-gather.17
  341.7 64.6 all-gather.15
  407.9 55.2 all-gather.21
  465.4 64.6 all-gather.23
  700.6 64.9 all-gather.25

commit v2 on v1

v2 whole, which is shorter than its diff:
```python
import functools
import math

import jax
import jax.numpy as jnp
from jax import lax
from jax.experimental import pallas as pl
from jax.experimental.pallas import tpu as pltpu
from jax.sharding import PartitionSpec as P

D = 2048
HEAD = 128
STREAMS = 4
MICRO = 2


norm_eps = 1e-05
beta_first = 0.9
beta_second = 0.95
adam_eps = 1e-08
learning_rate = 0.05
weight_decay = 0.1

LOW = jnp.bfloat16
FULL = jnp.float32
DMA = pltpu.SemaphoreType.DMA
ANY = pl.BlockSpec(memory_space=pl.ANY)
VMEM = pl.BlockSpec(memory_space=pltpu.VMEM)
SMEM = pl.BlockSpec(memory_space=pltpu.SMEM)
ROOM = 48 * 2**20


def rotary_tables(segment):
    length = segment.shape[0]
    places = jnp.arange(length, dtype=jnp.int32)
    starts = jnp.sum((segment[None, :] < segment[:, None]).astype(jnp.int32), axis=1)
    offsets = (places - starts).astype(jnp.float32)
    halves = jnp.arange(HEAD // 2, dtype=jnp.float32)
    inverse = jnp.exp(halves * (-2.0 * math.log(10000.0) / HEAD))
    angles = offsets[:, None] * inverse[None, :]
    cosine, sine = jnp.cos(angles), jnp.sin(angles)
    return (
        jnp.concatenate([cosine, cosine], axis=1),
        jnp.concatenate([-sine, sine], axis=1),
        starts[:, None],
    )


def norm_forward(hidden):
    means = jnp.sum(hidden, axis=-1, keepdims=True) / D
    squares = jnp.sum(hidden * hidden, axis=-1, keepdims=True) / D
    inverse = lax.rsqrt(squares - means * means + norm_eps)
    return ((hidden - means) * inverse, inverse)


def norm_backward(upstream, hidden):
    normed, inverse = norm_forward(hidden)
    mean_one = jnp.sum(upstream, axis=-1, keepdims=True) / D
    mean_two = jnp.sum(upstream * normed, axis=-1, keepdims=True) / D
    return inverse * (upstream - mean_one - normed * mean_two)


def hyper_parts(hyper):
    width = STREAMS + 2
    parts = []
    for layer in range(2):
        at = [[hyper[(layer * STREAMS + i) * width + k] for k in range(width)] for i in range(STREAMS)]
        parts.append(
            ([row[0] for row in at], [row[1 : STREAMS + 1] for row in at], [row[-1] for row in at])
        )
    return parts


def dot_of(left, right):
    total = left[0] * right[0]
    for a, b in zip(left[1:], right[1:]):
        total = total + a * b
    return total


def column(matrix, index):
    return [row[index] for row in matrix]


def branch_weight(hyper):
    (_, _, c0), (a1, _, _) = hyper_parts(hyper)
    return dot_of(a1, c0)


def combine(weights, stream_set):
    return dot_of(weights, stream_set)


def fold(product):
    rows, width = product.shape
    return jnp.sum(product.reshape(rows // 8, 8, width), axis=0)


def place_rows(match, values_in):
    if values_in.dtype == LOW:
        return jnp.dot(match.astype(LOW), values_in, preferred_element_type=FULL)
    return jnp.dot(
        match.astype(FULL), values_in, precision=lax.Precision.HIGHEST, preferred_element_type=FULL
    )


def prepare_kernel(hyper, streams, cotangent, sent, h_out, mix_out, back_out, gy_out, gram_out):
    rows, width = streams.shape[2:]
    parts, slot = h_out.shape[0], h_out.shape[2]
    (a0, m0, c0), (a1, m1, c1) = hyper_parts(hyper)
    first = [streams[0, i] for i in range(STREAMS)]
    second = [cotangent[0, j] for j in range(STREAMS)]
    match = lax.broadcasted_iota(jnp.int32, (rows, rows), 0) == sent[0]

    def put(out, values_in):
        moved = place_rows(match, values_in)
        for part in range(parts):
            out[part, 0] = moved[part * slot : (part + 1) * slot].astype(out.dtype)

    put(h_out, combine(a0, first))
    put(mix_out, combine([dot_of(row, a1) for row in m0], first))
    put(gy_out, combine(c1, second).astype(LOW))
    put(back_out, combine([dot_of(c0, column(m1, k)) for k in range(STREAMS)], second))

    @pl.when((pl.program_id(0) == 0) & (pl.program_id(1) == 0))
    def _():
        gram_out[...] = jnp.zeros_like(gram_out)

    for i in range(STREAMS):
        for j in range(STREAMS):
            gram_out[i * STREAMS + j] += fold(first[i] * second[j])


def prepare(hyper, streams, cotangent, sent, n_dp, travel):
    micro, _, rows, width = streams.shape
    slot, wide = rows // n_dp, 256
    block = pl.BlockSpec((1, STREAMS, rows, wide), lambda m, f: (m, 0, 0, f))
    home = pl.BlockSpec((n_dp, 1, slot, wide), lambda m, f: (0, m, 0, f))
    shape = (n_dp, micro, slot, width)
    return pl.pallas_call(
        prepare_kernel,
        grid=(micro, width // wide),
        in_specs=[SMEM, block, block, pl.BlockSpec((1, 1, rows), lambda m, f: (m, 0, 0))],
        out_specs=[home] * 4 + [pl.BlockSpec((STREAMS * STREAMS, 8, wide), lambda m, f: (0, 0, 0))],
        out_shape=[jax.ShapeDtypeStruct(shape, FULL)] * 3
        + [
            jax.ShapeDtypeStruct(shape, travel),
            jax.ShapeDtypeStruct((STREAMS * STREAMS, 8, wide), FULL),
        ],
        compiler_params=pltpu.CompilerParams(vmem_limit_bytes=ROOM),
    )(hyper, streams, cotangent, sent[:, None, :])


def finish_kernel(
    hyper, streams, cotangent, sent, y_att, y_ffn, gh_ffn, gh_att, streams_out, grad_out, dots_out
):
    rows, width = streams.shape[2:]
    (a0, m0, c0), (a1, m1, c1) = hyper_parts(hyper)
    first = [streams[0, i] for i in range(STREAMS)]
    second = [cotangent[0, j] for j in range(STREAMS)]
    match = lax.broadcasted_iota(jnp.int32, (rows, rows), 1) == sent[0]
    home_att, home_ffn, back_ffn, back_att = (
        place_rows(match, value[:, 0].reshape(rows, width)) for value in (y_att, y_ffn, gh_ffn, gh_att)
    )
    for j in range(STREAMS):
        mixed = combine([dot_of(m0[k], column(m1, j)) for k in range(STREAMS)], first)
        streams_out[0, j] = mixed + dot_of(c0, column(m1, j)) * home_att + c1[j] * home_ffn
    for i in range(STREAMS):
        mixed = combine([dot_of(m0[i], column(m1, k)) for k in range(STREAMS)], second)
        grad_out[0, i] = mixed + dot_of(m0[i], a1) * back_ffn + a0[i] * back_att

    @pl.when((pl.program_id(0) == 0) & (pl.program_id(1) == 0))
    def _():
        dots_out[...] = jnp.zeros_like(dots_out)

    pairs = (
        [(value, home_att) for value in second]
        + [(value, home_ffn) for value in second]
        + [(value, back_ffn) for value in first]
        + [(value, back_att) for value in first]
        + [(home_att, back_ffn)]
    )
    for index, (left, right) in enumerate(pairs):
        dots_out[index] += fold(left * right)


def finish(hyper, streams, cotangent, sent, homes):
    micro, _, rows, width = streams.shape
    n_dp, _, slot, _ = homes[0].shape
    wide = 256
    block = pl.BlockSpec((1, STREAMS, rows, wide), lambda m, f: (m, 0, 0, f))
    home = pl.BlockSpec((n_dp, 1, slot, wide), lambda m, f: (0, m, 0, f))
    count = 4 * STREAMS + 1
    return pl.pallas_call(
        finish_kernel,
        grid=(micro, width // wide),
        in_specs=[SMEM, block, block, pl.BlockSpec((1, rows, 1), lambda m, f: (m, 0, 0))] + [home] * 4,
        out_specs=[block, block, pl.BlockSpec((count, 8, wide), lambda m, f: (0, 0, 0))],
        out_shape=[
            jax.ShapeDtypeStruct(streams.shape, FULL),
            jax.ShapeDtypeStruct(streams.shape, FULL),
            jax.ShapeDtypeStruct((count, 8, wide), FULL),
        ],
        compiler_params=pltpu.CompilerParams(vmem_limit_bytes=ROOM),
    )(hyper, streams, cotangent, sent[:, :, None], *homes)


def turn(values_in, cosine, sine):
    half = HEAD // 2
    swapped = jnp.concatenate([values_in[:, half:], values_in[:, :half]], axis=1)
    return values_in * cosine + swapped * sine


def dot_last(left, right):
    return lax.dot_general(left, right, (((1,), (1,)), ((), ())), preferred_element_type=jnp.float32)


def dot_first(left, right):
    return lax.dot_general(left, right, (((0,), (0,)), ((), ())), preferred_element_type=jnp.float32)


def allowed_pairs(start_ref, base, block, keys):
    column = lax.broadcasted_iota(jnp.int32, (block, keys), 1)
    row = lax.broadcasted_iota(jnp.int32, (block, keys), 0) + base
    return (column >= start_ref[pl.ds(base, block)]) & (column <= row)


def attend_forward_kernel(
    block, q_in, k_in, v_in, cosine, sine, start, out, log_out, q_out, k_out, v_out
):
    length = q_in.shape[0]
    q_out[...] = turn(q_in[...], cosine[...], sine[...]).astype(jnp.bfloat16)
    k_out[...] = turn(k_in[...], cosine[...], sine[...]).astype(jnp.bfloat16)
    v_out[...] = v_in[...].astype(jnp.bfloat16)
    for base in range(0, length, block):
        keys = base + block
        scores = dot_last(q_out[pl.ds(base, block)], k_out[pl.ds(0, keys)]) * HEAD ** (-0.5)
        scores = jnp.where(allowed_pairs(start, base, block, keys), scores, -1e30)
        largest = jnp.max(scores, axis=1, keepdims=True)
        weights = jnp.exp(scores - largest)
        totals = jnp.sum(weights, axis=1, keepdims=True)
        probs = (weights * (1.0 / totals)).astype(jnp.bfloat16)
        out[pl.ds(base, block)] = jnp.dot(
            probs, v_out[pl.ds(0, keys)], preferred_element_type=jnp.float32
        ).astype(jnp.bfloat16)
        log_out[0, pl.ds(base, block)] = largest + jnp.log(totals)


def attend_backward_kernel(
    block, grad, q, k, v, log_in, cosine, sine, start, q_out, k_out, v_out, k_sum, v_sum
):
    length = q.shape[0]
    k_sum[...] = jnp.zeros_like(k_sum)
    v_sum[...] = jnp.zeros_like(v_sum)
    for base in range(0, length, block):
        keys = base + block
        rows, span = pl.ds(base, block), pl.ds(0, keys)
        scores = dot_last(q[rows], k[span]) * HEAD ** (-0.5)
        probs = jnp.where(
            allowed_pairs(start, base, block, keys), jnp.exp(scores - log_in[0, rows]), 0.0
        )
        grad_probs = dot_last(grad[rows], v[span])
        inner = jnp.sum(probs * grad_probs, axis=1, keepdims=True)
        grad_scores = (probs * (grad_probs - inner) * HEAD ** (-0.5)).astype(jnp.bfloat16)
        grad_query = jnp.dot(grad_scores, k[span], preferred_element_type=jnp.float32)
        q_out[rows] = turn(grad_query, cosine[rows], -sine[rows]).astype(jnp.bfloat16)
        k_sum[span] += dot_first(grad_scores, q[rows])
        v_sum[span] += dot_first(probs.astype(jnp.bfloat16), grad[rows])
    k_out[...] = turn(k_sum[...], cosine[...], -sine[...]).astype(jnp.bfloat16)
    v_out[...] = v_sum[...].astype(jnp.bfloat16)


def attend_forward(qkv, cosine, sine, start):
    length, width = qkv.shape
    heads = width // (3 * HEAD)
    block = min(256, length)

    def part(offset):
        return pl.BlockSpec((length, HEAD), lambda h: (0, offset + h))

    whole = pl.BlockSpec((length, HEAD), lambda h: (0, 0))
    low = jax.ShapeDtypeStruct((length, heads * HEAD), jnp.bfloat16)
    return pl.pallas_call(
        functools.partial(attend_forward_kernel, block),
        grid=(heads,),
        in_specs=[part(0), part(heads), part(2 * heads), whole, whole,
                  pl.BlockSpec((length, 1), lambda h: (0, 0))],
        out_specs=[part(0), pl.BlockSpec((1, length, 1), lambda h: (h, 0, 0)), part(0), part(0), part(0)],
        out_shape=[low, jax.ShapeDtypeStruct((heads, length, 1), jnp.float32), low, low, low],
        compiler_params=pltpu.CompilerParams(vmem_limit_bytes=40 * 2**20),
    )(qkv, qkv, qkv, cosine, sine, start)


def attend_backward(grad, q, k, v, log_totals, cosine, sine, start):
    length, width = q.shape
    heads = width // HEAD
    block = min(256, length)
    part = pl.BlockSpec((length, HEAD), lambda h: (0, h))
    whole = pl.BlockSpec((length, HEAD), lambda h: (0, 0))
    low = jax.ShapeDtypeStruct((length, width), jnp.bfloat16)
    return pl.pallas_call(
        functools.partial(attend_backward_kernel, block),
        grid=(heads,),
        in_specs=[part, part, part, part, pl.BlockSpec((1, length, 1), lambda h: (h, 0, 0)), whole, whole,
                  pl.BlockSpec((length, 1), lambda h: (0, 0))],
        out_specs=[part, part, part],
        out_shape=[low, low, low],
        scratch_shapes=[pltpu.VMEM((length, HEAD), jnp.float32)] * 2,
        compiler_params=pltpu.CompilerParams(vmem_limit_bytes=40 * 2**20),
    )(grad, q, k, v, log_totals, cosine, sine, start)


def remote(source, target, send_sem, recv_sem, device):
    return pltpu.make_async_remote_copy(
        src_ref=source,
        dst_ref=target,
        send_sem=send_sem,
        recv_sem=recv_sem,
        device_id=device,
        device_id_type=pl.DeviceIdType.MESH,
    )


def line_place():
    me = lax.axis_index("row")
    return me, me // 2, me % 2


def greet(pairs, plane=None):
    me, place, side = line_place()
    barrier = pltpu.get_barrier_semaphore()

    def signal(device):
        pl.semaphore_signal(barrier, inc=1, device_id=device, device_id_type=pl.DeviceIdType.MESH)

    signal({"row": me + 1 - 2 * side})

    @pl.when(place < pairs - 1)
    def _():
        signal({"row": me + 2})

    @pl.when(place > 0)
    def _():
        signal({"row": me - 2})

    count = 1
    if plane is not None:
        for offset in offsets(plane):
            signal(peer(plane, offset))
            count += 1
    last = pairs - 1
    neighbours = (place + last) // pairs + (2 * last - place) // pairs
    pl.semaphore_wait(barrier, count + neighbours)


def offsets(plane):
    n_dp, n_col = plane
    return [(d, c) for d in range(n_dp) for c in range(n_col) if (d, c) != (0, 0)]


def peer(plane, offset):
    n_dp, n_col = plane
    return {
        "dp": (lax.axis_index("dp") + offset[0]) % n_dp,
        "col": (lax.axis_index("col") + offset[1]) % n_col,
    }


class Exchange:
    def __init__(self, plane, source_of, target, sends, receives, keep):
        self.plane, self.source_of, self.target = plane, source_of, target
        self.sends, self.receives, self.keep = sends, receives, keep

    def move(self, offset):
        device = peer(self.plane, offset)
        return remote(
            self.source_of(device["dp"], device["col"]),
            self.target,
            self.sends.at[offset[0], offset[1]],
            self.receives.at[offset[0], offset[1]],
            device,
        )

    def stay(self):
        return pltpu.make_async_copy(
            self.source_of(lax.axis_index("dp"), lax.axis_index("col")), self.target, self.keep
        )

    def start(self):
        for offset in offsets(self.plane):
            self.move(offset).start()
        self.stay().start()

    def arrive(self):
        for offset in offsets(self.plane):
            self.move(offset).wait_recv()
        self.stay().wait()

    def leave(self):
        for offset in offsets(self.plane):
            self.move(offset).wait_send()


def exchange_sems(plane, count):
    return [DMA((count,) + plane), DMA((count,) + plane), DMA((count,))]


def work_block(work, slot, width, part, side):
    return work.at[
        pl.ds(pl.multiple_of(part * slot, slot), slot), pl.ds(pl.multiple_of(side * width, width), width)
    ]


def to_work(plane, home, work, sems, index):
    slot, width = home.shape[2:]
    return Exchange(
        plane,
        lambda b, c: home.at[b, c],
        work_block(work, slot, width, lax.axis_index("dp"), lax.axis_index("col")),
        sems[0].at[index],
        sems[1].at[index],
        sems[2].at[index],
    )


def to_home(plane, work, home, sems, index):
    slot, width = home.shape[2:]
    return Exchange(
        plane,
        lambda b, c: work_block(work, slot, width, b, c),
        home.at[lax.axis_index("dp"), lax.axis_index("col")],
        sems[0].at[index],
        sems[1].at[index],
        sems[2].at[index],
    )


class Gather:
    def __init__(self, pairs, cuts, own, out, sems):
        self.pairs, self.cuts, self.own, self.out = pairs, cuts, own, out
        self.right, self.left, self.twin_send, self.line, self.twin_recv, self.keep = sems
        self.height = own.shape[0] // cuts

    def piece(self, ref, cut):
        return ref.at[pl.ds(cut * self.height, self.height)]

    def move(self, row, sends, receives, origin, cut, first):
        _, _, side = line_place()
        block = self.piece(self.out.at[origin * 2 + side], cut)
        return remote(
            self.piece(self.own, cut) if first else block,
            block,
            sends.at[origin, cut],
            receives.at[origin, cut],
            {"row": row},
        )

    def to_twin(self, origin, cut, first=False):
        me, _, side = line_place()
        return self.move(me + 1 - 2 * side, self.twin_send, self.twin_recv, origin, cut, first)

    def to_right(self, origin, cut, first=False):
        return self.move(line_place()[0] + 2, self.right, self.line, origin, cut, first)

    def to_left(self, origin, cut, first=False):
        return self.move(line_place()[0] - 2, self.left, self.line, origin, cut, first)

    def stay(self):
        return pltpu.make_async_copy(self.own, self.out.at[line_place()[0]], self.keep)

    def start(self):
        _, place, _ = line_place()
        for cut in range(self.cuts):
            @pl.when(place < self.pairs - 1)
            def _():
                self.to_right(place, cut, True).start()

            @pl.when(place > 0)
            def _():
                self.to_left(place, cut, True).start()

        for cut in range(self.cuts):
            self.to_twin(place, cut, True).start()
        self.stay().start()

    def step(self, step, cut):
        _, place, _ = line_place()

        @pl.when(place >= step)
        def _():
            origin = place - step
            self.to_right(origin, cut).wait_recv()

            @pl.when(place < self.pairs - 1)
            def _():
                self.to_right(origin, cut).start()

            self.to_twin(origin, cut).start()

        @pl.when(place + step <= self.pairs - 1)
        def _():
            origin = place + step
            self.to_left(origin, cut).wait_recv()

            @pl.when(place > 0)
            def _():
                self.to_left(origin, cut).start()

            self.to_twin(origin, cut).start()

    def finish(self):
        me, place, side = line_place()
        self.stay().wait()
        for origin in range(self.pairs):
            for cut in range(self.cuts):
                self.to_twin(origin, cut).wait_send()
                other = self.piece(self.out.at[origin * 2 + 1 - side], cut)
                remote(
                    other,
                    other,
                    self.twin_send.at[origin, cut],
                    self.twin_recv.at[origin, cut],
                    {"row": me + 1 - 2 * side},
                ).wait_recv()

                @pl.when((place < self.pairs - 1) & (origin <= place))
                def _():
                    self.to_right(origin, cut).wait_send()

                @pl.when((place > 0) & (origin >= place))
                def _():
                    self.to_left(origin, cut).wait_send()


def gather_sems(pairs, cuts):
    return [DMA((pairs, cuts))] * 5 + [DMA]


class Scatter:
    def __init__(self, pairs, cuts, part, buffers, sems):
        self.pairs, self.cuts, self.part = pairs, cuts, part
        self.own, self.twin, self.from_left, self.from_right, self.out_right, self.out_left = buffers
        (
            self.right_send,
            self.left_send,
            self.twin_send,
            self.right_recv,
            self.left_recv,
            self.twin_recv,
            self.loaded,
        ) = sems
        self.height = part.shape[1] // cuts
        self.ready = set()

    def piece(self, ref, dest, cut):
        return ref.at[dest, pl.ds(cut * self.height, self.height)]

    def value(self, ref, dest, cut):
        return ref[dest, pl.ds(cut * self.height, self.height)].astype(FULL)

    def load(self, dest, cut):
        _, _, side = line_place()
        return pltpu.make_async_copy(
            self.piece(self.part, dest * 2 + side, cut),
            self.piece(self.own, dest, cut),
            self.loaded.at[dest, cut],
        )

    def to_twin(self, dest, cut):
        me, _, side = line_place()
        return remote(
            self.piece(self.part, dest * 2 + 1 - side, cut),
            self.piece(self.twin, dest, cut),
            self.twin_send.at[dest, cut],
            self.twin_recv.at[dest, cut],
            {"row": me + 1 - 2 * side},
        )

    def to_right(self, dest, cut):
        return remote(
            self.piece(self.out_right, dest, cut),
            self.piece(self.from_left, dest, cut),
            self.right_send.at[dest, cut],
            self.right_recv.at[dest, cut],
            {"row": line_place()[0] + 2},
        )

    def to_left(self, dest, cut):
        return remote(
            self.piece(self.out_left, dest, cut),
            self.piece(self.from_right, dest, cut),
            self.left_send.at[dest, cut],
            self.left_recv.at[dest, cut],
            {"row": line_place()[0] - 2},
        )

    def start(self):
        order = []
        for step in range(self.pairs):
            for dest in (self.pairs - 1 - step, step):
                if dest not in order:
                    order.append(dest)
        for dest in order:
            for cut in range(self.cuts):
                self.to_twin(dest, cut).start()
                self.load(dest, cut).start()

    def here(self, dest, cut):
        return self.value(self.own, dest, cut) + self.value(self.twin, dest, cut)

    def step(self, step, cut):
        _, place, _ = line_place()
        last = self.pairs - 1
        span = pl.ds(cut * self.height, self.height)
        for dest, sending, first, out, arrived, copy in (
            (last - step, place < last - step, place == 0, self.out_right, self.from_left, self.to_right),
            (step, place > step, place == last, self.out_left, self.from_right, self.to_left),
        ):
            if (dest, cut) not in self.ready:
                self.ready.add((dest, cut))
                self.to_twin(dest, cut).wait_recv()
                self.load(dest, cut).wait()

            @pl.when(sending & first)
            def _():
                out[dest, span] = self.here(dest, cut).astype(out.dtype)
                copy(dest, cut).start()

            @pl.when(sending & jnp.logical_not(first))
            def _():
                copy(dest, cut).wait_recv()
                out[dest, span] = (self.here(dest, cut) + self.value(arrived, dest, cut)).astype(out.dtype)
                copy(dest, cut).start()

    def finish(self, total):
        _, place, _ = line_place()
        last = self.pairs - 1
        for cut in range(self.cuts):
            span = pl.ds(cut * self.height, self.height)
            total[span] = self.here(place, cut)

            @pl.when(place > 0)
            def _():
                self.to_right(place, cut).wait_recv()
                total[span] += self.value(self.from_left, place, cut)

            @pl.when(place < last)
            def _():
                self.to_left(place, cut).wait_recv()
                total[span] += self.value(self.from_right, place, cut)

        for dest in range(self.pairs):
            for cut in range(self.cuts):
                self.to_twin(dest, cut).wait_send()

                @pl.when(place < dest)
                def _():
                    self.to_right(dest, cut).wait_send()

                @pl.when(place > dest)
                def _():
                    self.to_left(dest, cut).wait_send()


def scatter_buffers(pairs, rows, width):
    return [pltpu.VMEM((pairs, rows, width), LOW)] * 6


def scatter_sems(pairs, cuts):
    return [DMA((pairs, cuts))] * 7


CUTS = 2


def call_remote(kernel, collective, **options):
    return pl.pallas_call(
        kernel,
        compiler_params=pltpu.CompilerParams(
            collective_id=collective, has_side_effects=True, vmem_limit_bytes=ROOM
        ),
        **options,
    )


def enter_kernel(plane, pairs, h_home, mix_home, back_home, gy_home, rows_out, h, mix, back, gy, own, *sems):
    plane_sems, line_sems = sems[:3], sems[3:]
    greet(pairs, plane)
    first = to_work(plane, h_home, h, plane_sems, 0)
    others = [
        to_work(plane, home, work, plane_sems, index)
        for index, (home, work) in enumerate(((mix_home, mix), (back_home, back), (gy_home, gy)), 1)
    ]
    first.start()
    first.arrive()
    for other in others:
        other.start()
    own[...] = norm_forward(h[...])[0].astype(LOW)
    gather = Gather(pairs, CUTS, own, rows_out, line_sems)
    gather.start()
    for step in range(1, pairs):
        for cut in range(CUTS):
            gather.step(step, cut)
    gather.finish()
    for other in others:
        other.arrive()
        other.leave()
    first.leave()


def enter(plane, pairs, h_home, mix_home, back_home, gy_home, collective):
    n_dp, n_col, slot, width = h_home.shape
    rows = n_dp * slot
    work = jax.ShapeDtypeStruct((rows, n_col * width), FULL)
    outs = call_remote(
        functools.partial(enter_kernel, plane, pairs),
        collective,
        in_specs=[ANY] * 4,
        out_specs=[ANY, VMEM, ANY, ANY, ANY],
        out_shape=[
            jax.ShapeDtypeStruct((2 * pairs, rows, n_col * width), LOW),
            work,
            work,
            work,
            jax.ShapeDtypeStruct(work.shape, gy_home.dtype),
        ],
        scratch_shapes=[pltpu.VMEM(work.shape, LOW)] + exchange_sems(plane, 4) + gather_sems(pairs, CUTS),
    )(h_home, mix_home, back_home, gy_home)
    return [outs[0].reshape(2 * pairs * rows, n_col * width)] + list(outs[1:])


def duplex_kernel(pairs, part, gathered, rows_out, low_out, total, *scratch):
    scatter = Scatter(pairs, CUTS, part, scratch[:6], scratch[6:13])
    gather = Gather(pairs, CUTS, gathered, rows_out, scratch[13:])
    greet(pairs)
    scatter.start()
    gather.start()
    for step in range(pairs - 1):
        for cut in range(CUTS):
            scatter.step(step, cut)
            gather.step(step + 1, cut)
    scatter.finish(total)
    low_out[...] = total[...].astype(LOW)
    gather.finish()


def duplex(pairs, partial, gathered, collective):
    rows, width = gathered.shape
    whole = jax.ShapeDtypeStruct((2 * pairs, rows, width), LOW)
    outs = call_remote(
        functools.partial(duplex_kernel, pairs),
        collective,
        in_specs=[ANY, ANY],
        out_specs=[ANY, VMEM, VMEM],
        out_shape=[
            whole,
            jax.ShapeDtypeStruct((rows, width), LOW),
            jax.ShapeDtypeStruct((rows, width), FULL),
        ],
        scratch_shapes=scatter_buffers(pairs, rows, width)
        + scatter_sems(pairs, CUTS)
        + gather_sems(pairs, CUTS),
    )(partial.reshape(whole.shape), gathered)
    return [outs[0].reshape(2 * pairs * rows, width)] + list(outs[1:])


def middle_kernel(pairs, hyper, mix, branch, rows_out, h, own, *sems):
    greet(pairs)
    h[...] = mix[...] + branch_weight(hyper) * branch[...]
    own[...] = norm_forward(h[...])[0].astype(LOW)
    gather = Gather(pairs, CUTS, own, rows_out, sems)
    gather.start()
    for step in range(1, pairs):
        for cut in range(CUTS):
            gather.step(step, cut)
    gather.finish()


def middle(pairs, hyper, mix, branch, collective):
    rows, width = mix.shape
    outs = call_remote(
        functools.partial(middle_kernel, pairs),
        collective,
        in_specs=[SMEM, VMEM, VMEM],
        out_specs=[ANY, VMEM],
        out_shape=[
            jax.ShapeDtypeStruct((2 * pairs, rows, width), LOW),
            jax.ShapeDtypeStruct((rows, width), FULL),
        ],
        scratch_shapes=[pltpu.VMEM((rows, width), LOW)] + gather_sems(pairs, CUTS),
    )(hyper, mix, branch)
    return outs[0].reshape(2 * pairs * rows, width), outs[1]


def turn_back_kernel(pairs, hyper, part, h, back, gh_out, gy_out, total, *scratch):
    scatter = Scatter(pairs, CUTS, part, scratch[:6], scratch[6:])
    greet(pairs)
    scatter.start()
    for step in range(pairs - 1):
        for cut in range(CUTS):
            scatter.step(step, cut)
    scatter.finish(total)
    grad = norm_backward(total[...], h[...])
    gh_out[...] = grad.astype(LOW)
    gy_out[...] = (back[...] + branch_weight(hyper) * grad).astype(LOW)


def turn_back(pairs, hyper, partial, h, back, collective):
    rows, width = h.shape
    low = jax.ShapeDtypeStruct((rows, width), LOW)
    return call_remote(
        functools.partial(turn_back_kernel, pairs),
        collective,
        in_specs=[SMEM, ANY, VMEM, VMEM],
        out_specs=[VMEM, VMEM],
        out_shape=[low, low],
        scratch_shapes=[pltpu.VMEM((rows, width), FULL)]
        + scatter_buffers(pairs, rows, width)
        + scatter_sems(pairs, CUTS),
    )(hyper, partial.reshape(2 * pairs, rows, width), h, back)


def leave_kernel(plane, pairs, part, h, y_att, y_ffn, gh_ffn, *rest):
    homes, total, last = rest[:4], rest[4], rest[5]
    plane_sems, scratch = rest[6:9], rest[9:]
    scatter = Scatter(pairs, CUTS, part, scratch[:6], scratch[6:])
    greet(pairs, plane)
    scatter.start()
    ways = [
        to_home(plane, work, home, plane_sems, index)
        for index, (work, home) in enumerate(zip((y_att, y_ffn, gh_ffn, last), homes))
    ]
    for way in ways[:3]:
        way.start()
    for step in range(pairs - 1):
        for cut in range(CUTS):
            scatter.step(step, cut)
    scatter.finish(total)
    last[...] = norm_backward(total[...], h[...]).astype(last.dtype)
    ways[3].start()
    for way in ways:
        way.arrive()
        way.leave()


def leave(plane, pairs, partial, h, works, collective):
    rows, width = h.shape
    n_dp, n_col = plane
    home = jax.ShapeDtypeStruct((n_dp, n_col, rows // n_dp, width // n_col), works[0].dtype)
    return call_remote(
        functools.partial(leave_kernel, plane, pairs),
        collective,
        in_specs=[ANY, VMEM, ANY, ANY, ANY],
        out_specs=[ANY] * 4,
        out_shape=[home] * 4,
        scratch_shapes=[pltpu.VMEM((rows, width), FULL), pltpu.VMEM((rows, width), works[0].dtype)]
        + exchange_sems(plane, 4)
        + scatter_buffers(pairs, rows, width)
        + scatter_sems(pairs, CUTS),
    )(partial.reshape(2 * pairs, rows, width), h, *works)


def total_kernel(plane, count, own, out, line, flat, line_send, line_recv, flat_send, flat_recv):
    n_dp, n_col = plane
    me = lax.axis_index("row")
    here = lax.axis_index("dp") * n_col + lax.axis_index("col")
    barrier = pltpu.get_barrier_semaphore()
    rows = [(me + step) % count for step in range(1, count)]
    for row in rows:
        pl.semaphore_signal(barrier, inc=1, device_id={"row": row}, device_id_type=pl.DeviceIdType.MESH)
    for offset in offsets(plane):
        pl.semaphore_signal(
            barrier, inc=1, device_id=peer(plane, offset), device_id_type=pl.DeviceIdType.MESH
        )
    pl.semaphore_wait(barrier, count - 1 + n_dp * n_col - 1)
    line[me] = own[...]
    copies = [
        remote(line.at[me], line.at[me], line_send.at[step], line_recv.at[step], {"row": row})
        for step, row in enumerate(rows)
    ]
    for copy in copies:
        copy.start()
    for copy in copies:
        copy.wait()
    sums = line[0]
    for row in range(1, count):
        sums = sums + line[row]
    flat[here] = sums
    copies = [
        remote(
            flat.at[here],
            flat.at[here],
            flat_send.at[offset[0], offset[1]],
            flat_recv.at[offset[0], offset[1]],
            peer(plane, offset),
        )
        for offset in offsets(plane)
    ]
    for copy in copies:
        copy.start()
    for copy in copies:
        copy.wait()
    sums = flat[0]
    for index in range(1, n_dp * n_col):
        sums = sums + flat[index]
    out[...] = sums


def sum_everywhere(plane, values_in, collective):
    count = lax.axis_size("row")
    shape = values_in.shape
    return call_remote(
        functools.partial(total_kernel, plane, count),
        collective,
        in_specs=[VMEM],
        out_specs=VMEM,
        out_shape=jax.ShapeDtypeStruct(shape, FULL),
        scratch_shapes=[
            pltpu.VMEM((count,) + shape, FULL),
            pltpu.VMEM((plane[0] * plane[1],) + shape, FULL),
            DMA((count - 1,)),
            DMA((count - 1,)),
            DMA(plane),
            DMA(plane),
        ],
    )(values_in)


def mat(left, right):
    return jnp.sum(left[:, :, None] * right[None, :, :], axis=1)


def gather_blocks(weight_low):
    return lax.all_gather(weight_low, ("col", "dp"), axis=0, tiled=True)


def scatter_blocks(grad_low):
    return lax.psum_scatter(grad_low, ("col", "dp"), scatter_dimension=0, tiled=True).astype(FULL)


def side_by_side(weight):
    return jnp.concatenate([weight[index] for index in range(weight.shape[0])], axis=1)


def apart(weight, count):
    width = weight.shape[1] // count
    return jnp.stack([weight[:, index * width : (index + 1) * width] for index in range(count)])


def whole_out(weight_low, n_dp, n_col):
    rows, width = weight_low.shape
    blocks = gather_blocks(weight_low).reshape(n_col, n_dp, rows, width)
    return blocks.transpose(1, 2, 0, 3).reshape(n_dp * rows, n_col * width)


def own_out(grad, n_dp, n_col):
    rows, width = grad.shape[0] // n_dp, grad.shape[1] // n_col
    blocks = grad.astype(LOW).reshape(n_dp, rows, n_col, width).transpose(2, 0, 1, 3)
    return scatter_blocks(blocks.reshape(n_col * n_dp * rows, width))


def adam_update(weight, grad_sum, moment_one, moment_two, clip_factor, step_value):
    clipped = grad_sum * clip_factor
    new_one = beta_first * moment_one + (1.0 - beta_first) * clipped
    new_two = beta_second * moment_two + (1.0 - beta_second) * clipped * clipped
    fix_one = 1.0 - jnp.power(beta_first, step_value)
    fix_two = 1.0 - jnp.power(beta_second, step_value)
    new_weight = weight - learning_rate * (
        new_one / fix_one / (jnp.sqrt(new_two / fix_two) + adam_eps) + weight_decay * weight
    )
    return (new_weight, new_one, new_two)


def body(
    streams,
    cotangent,
    destination,
    segments,
    attention_in,
    feedforward_in,
    attention_out,
    feedforward_out,
    attention_in_moment,
    feedforward_in_moment,
    attention_out_moment,
    feedforward_out_moment,
    attention_in_second,
    feedforward_in_second,
    attention_out_second,
    feedforward_out_second,
    hyper_weights,
    hyper_moment,
    hyper_second,
    step_count,
):
    n_dp, n_col, count = lax.axis_size("dp"), lax.axis_size("col"), lax.axis_size("row")
    plane, pairs = (n_dp, n_col), count // 2
    rows = destination.shape[1]
    group_tokens = segments.shape[2]
    slot = rows // n_dp
    travel = LOW if slot % 16 == 0 else FULL
    attention_in_low = gather_blocks(side_by_side(attention_in).astype(LOW))
    attention_out_low = whole_out(attention_out.astype(LOW), n_dp, n_col)
    feedforward_in_low = gather_blocks(side_by_side(feedforward_in).astype(LOW))
    feedforward_out_low = whole_out(feedforward_out.astype(LOW), n_dp, n_col)

    group = destination // group_tokens
    sent = (
        group * slot
        + (destination - group * group_tokens)
        - lax.axis_index("row") * rows
        - lax.axis_index("dp") * slot
    )
    hyper = hyper_weights.reshape(-1)
    h_home, mix_home, back_home, gy_home, gram = prepare(
        hyper, streams, cotangent, sent, n_dp, travel
    )
    segment = lax.dynamic_index_in_dim(segments[:, 0], lax.axis_index("col"), 0, keepdims=False)
    cosine, sine, start = rotary_tables(segment)

    rows_att, hidden_att, mix_work, back_work, gy_work = enter(
        plane, pairs, h_home, mix_home, back_home, gy_home, 1
    )
    qkv = jnp.dot(rows_att, attention_in_low, preferred_element_type=FULL)
    heads_low, log_totals, query_low, key_low, value_low = attend_forward(qkv, cosine, sine, start)
    partial_att = jnp.dot(heads_low, attention_out_low, preferred_element_type=FULL).astype(LOW)
    grad_rows_ffn, branch_low, branch_att = duplex(pairs, partial_att, gy_work.astype(LOW), 2)
    rows_ffn, hidden_ffn = middle(pairs, hyper, mix_work, branch_att, 3)

    gate_up = jnp.dot(rows_ffn, feedforward_in_low, preferred_element_type=FULL)
    units = gate_up.shape[1] // 2
    gate_pre, up_pre = gate_up[:, :units], gate_up[:, units:]
    sigma = jax.nn.sigmoid(gate_pre)
    silu = gate_pre * sigma
    hidden_low = (silu * up_pre).astype(LOW)
    grad_hidden = jnp.einsum("td,ud->tu", grad_rows_ffn, feedforward_out_low, preferred_element_type=FULL)
    grad_gate = (grad_hidden * up_pre * sigma * (1.0 + gate_pre * (1.0 - sigma))).astype(LOW)
    grad_up = (grad_hidden * silu).astype(LOW)
    grad_units = jnp.concatenate([grad_gate, grad_up], axis=1)
    partial_grad = jnp.einsum(
        "tu,du->td", grad_units, feedforward_in_low, preferred_element_type=FULL
    ).astype(LOW)
    grad_hidden_ffn, grad_branch = turn_back(pairs, hyper, partial_grad, hidden_ffn, back_work, 4)
    partial_ffn = jnp.dot(hidden_low, feedforward_out_low, preferred_element_type=FULL).astype(LOW)
    shard_feedforward_in = apart(
        scatter_blocks(
            jnp.einsum("td,tu->du", rows_ffn, grad_units, preferred_element_type=FULL).astype(LOW)
        ),
        2,
    )
    shard_feedforward_out = own_out(
        jnp.einsum("tu,td->ud", hidden_low, grad_rows_ffn, preferred_element_type=FULL), n_dp, n_col
    )
    grad_rows_att, branch_ffn, _ = duplex(pairs, partial_ffn, grad_branch, 5)

    shard_attention_out = own_out(
        jnp.einsum("tu,td->ud", heads_low, grad_rows_att, preferred_element_type=FULL), n_dp, n_col
    )
    grad_heads = jnp.einsum(
        "td,ud->tu", grad_rows_att, attention_out_low, preferred_element_type=FULL
    ).astype(LOW)
    grad_units_att = jnp.concatenate(
        attend_backward(grad_heads, query_low, key_low, value_low, log_totals, cosine, sine, start),
        axis=1,
    )
    shard_attention_in = apart(
        scatter_blocks(
            jnp.einsum("td,tu->du", rows_att, grad_units_att, preferred_element_type=FULL).astype(LOW)
        ),
        3,
    )
    partial_grad = jnp.einsum(
        "tu,du->td", grad_units_att, attention_in_low, preferred_element_type=FULL
    ).astype(LOW)
    homes = leave(
        plane,
        pairs,
        partial_grad,
        hidden_att,
        [value.astype(travel) for value in (branch_low, branch_ffn, grad_hidden_ffn)],
        6,
    )
    streams_out, stream_grad, dots = finish(hyper, streams, cotangent, sent, homes)
    square = (
        jnp.sum(shard_attention_in * shard_attention_in)
        + jnp.sum(shard_feedforward_in * shard_feedforward_in)
        + jnp.sum(shard_attention_out * shard_attention_out)
        + jnp.sum(shard_feedforward_out * shard_feedforward_out)
    )
    dots = jnp.concatenate([jnp.sum(gram, axis=(1, 2)), jnp.sum(dots, axis=(1, 2)), square[None]])
    totals = sum_everywhere(plane, jnp.pad(dots, (0, 128 - dots.shape[0])).reshape(1, 128), 7)[0]
    a0, m0, c0 = hyper_weights[0, :, 0], hyper_weights[0, :, 1:5], hyper_weights[0, :, 5]
    a1, m1, c1 = hyper_weights[1, :, 0], hyper_weights[1, :, 1:5], hyper_weights[1, :, 5]
    gram = totals[:16].reshape(STREAMS, STREAMS)
    att_cot, ffn_cot = totals[16:20], totals[20:24]
    streams_ffn, streams_att = totals[24:28], totals[28:32]
    att_ffn, square_total = totals[32], totals[33]
    grad_m1 = mat(m0.T, gram) + c0[:, None] * att_cot[None, :]
    grad_a1 = jnp.sum(m0 * streams_ffn[:, None], axis=0) + c0 * att_ffn
    grad_m0 = mat(gram, m1.T) + streams_ffn[:, None] * a1[None, :]
    grad_c0 = jnp.sum(m1 * att_cot[None, :], axis=1) + a1 * att_ffn
    hyper_grad = jnp.stack(
        [
            jnp.concatenate([streams_att[:, None], grad_m0, grad_c0[:, None]], axis=1),
            jnp.concatenate([grad_a1[:, None], grad_m1, ffn_cot[:, None]], axis=1),
        ]
    )
    grad_norm = jnp.sqrt(square_total + jnp.sum(hyper_grad * hyper_grad))
    clip_factor = 1.0 / jnp.maximum(grad_norm, 1.0)
    step_value = step_count[0].astype(jnp.float32)
    attention_in_new = adam_update(
        attention_in,
        shard_attention_in,
        attention_in_moment,
        attention_in_second,
        clip_factor,
        step_value,
    )
    feedforward_in_new = adam_update(
        feedforward_in,
        shard_feedforward_in,
        feedforward_in_moment,
        feedforward_in_second,
        clip_factor,
        step_value,
    )
    attention_out_new = adam_update(
        attention_out,
        shard_attention_out,
        attention_out_moment,
        attention_out_second,
        clip_factor,
        step_value,
    )
    feedforward_out_new = adam_update(
        feedforward_out,
        shard_feedforward_out,
        feedforward_out_moment,
        feedforward_out_second,
        clip_factor,
        step_value,
    )
    hyper_new = adam_update(
        hyper_weights, hyper_grad, hyper_moment, hyper_second, clip_factor, step_value
    )
    return (
        streams_out,
        stream_grad,
        grad_norm.reshape(1),
        shard_attention_in,
        shard_feedforward_in,
        shard_attention_out,
        shard_feedforward_out,
        hyper_grad,
        attention_in_new[0],
        feedforward_in_new[0],
        attention_out_new[0],
        feedforward_out_new[0],
        hyper_new[0],
        attention_in_new[1],
        feedforward_in_new[1],
        attention_out_new[1],
        feedforward_out_new[1],
        hyper_new[1],
        attention_in_new[2],
        feedforward_in_new[2],
        attention_out_new[2],
        feedforward_out_new[2],
        hyper_new[2],
    )


def solution(mesh):
    placed = (
        P(None, None, ("dp", "row"), "col"),
        P(None, None, ("dp", "row"), "col"),
        P(None, ("dp", "row")),
        P(None, "dp", None),
        P(None, ("col", "dp"), "row"),
        P(None, ("col", "dp"), "row"),
        P(("row", "dp"), "col"),
        P(("row", "dp"), "col"),
        P(None, ("col", "dp"), "row"),
        P(None, ("col", "dp"), "row"),
        P(("row", "dp"), "col"),
        P(("row", "dp"), "col"),
        P(None, ("col", "dp"), "row"),
        P(None, ("col", "dp"), "row"),
        P(("row", "dp"), "col"),
        P(("row", "dp"), "col"),
        P(),
        P(),
        P(),
        P(),
    )
    return jax.shard_map(
        body,
        mesh=mesh,
        in_specs=placed,
        out_specs=(
            P(None, None, ("dp", "row"), "col"),
            P(None, None, ("dp", "row"), "col"),
            P(),
            P(None, ("col", "dp"), "row"),
            P(None, ("col", "dp"), "row"),
            P(("row", "dp"), "col"),
            P(("row", "dp"), "col"),
            P(),
            P(None, ("col", "dp"), "row"),
            P(None, ("col", "dp"), "row"),
            P(("row", "dp"), "col"),
            P(("row", "dp"), "col"),
            P(),
            P(None, ("col", "dp"), "row"),
            P(None, ("col", "dp"), "row"),
            P(("row", "dp"), "col"),
            P(("row", "dp"), "col"),
            P(),
            P(None, ("col", "dp"), "row"),
            P(None, ("col", "dp"), "row"),
            P(("row", "dp"), "col"),
            P(("row", "dp"), "col"),
            P(),
        ),
        check_vma=False,
    )
```

time: 1300 us -> 871 us (0.67)
  Pallas kernels: 0 us -> 542 us
  waiting for transfers between devices: 556 us -> 66.3 us
  other arithmetic: 194 us -> 51.2 us
  matrix products: 273 us -> 133 us
  blocking collectives: 121 us -> 0 us
  local copies, waits for them, and re-layouts: 108 us -> 46.9 us
  starting transfers between devices: 21.3 us -> 0.97 us
    pallas_call x0 -> x11, Pallas kernels: none -> 542 us  [the longest x2 193 us: duplex(): call_remote(functools.partial(duplex_kernel, pairs), collective, in_specs...]
    all_gather x9 -> x4, waiting for transfers between devices: 326 us -> 0.03 us  [gather_blocks(): return lax.all_gather(weight_low, ('col', 'dp'), axis=0, tiled=True)]
    dot_general x32 -> x8, matrix products: 232 us -> 95.1 us  [the longest x1 19.5 us: body(): jnp.einsum('td,tu->du', rows_ffn, grad_units, preferred_element_type=FULL)]
    reduce_scatter x10 -> x4, waiting for transfers between devices: 185 us -> 66.1 us  [scatter_blocks(): lax.psum_scatter(grad_low, ('col', 'dp'), scatter_dimension=0, tiled=True)]
    all_to_all x3 -> x0, blocking collectives: 74.5 us -> none  [to_work(): lax.all_to_all(parts.reshape(n_dp * n_col, slot, width), ('dp', 'col'), s...]
    add x10 -> x0, other arithmetic: 71.8 us -> none  [the longest x4 29.9 us: body(): combine(m01[i], cotangent) + mix_grad[i] * home_grad_ffn]
    all_to_all x5 -> x0, waiting for transfers between devices: 42.1 us -> none  [the longest x1 35 us: to_work(): lax.all_to_all(parts.reshape(n_dp * n_col, slot, width), ('dp', 'col'), s...]
    psum x1 -> x0, blocking collectives: 39.3 us -> none  [body(): lax.psum(jnp.concatenate([dots, square[None]]), ('dp', 'row', 'col'))]
  transfers between devices with their start and end apart: 24 -> 8, of which waited for: 14 -> 1; matrix products, arithmetic and copies ran while one was open for 32% -> 14% of each run, Pallas kernels for 0% -> 43%
where the time goes in v2:
time: 871 us; the launch traced here: 862 us
  Pallas kernels  542 us (62%)
  matrix products  133 us (15%)
  waiting for transfers between devices  66.3 us (8%)
  other arithmetic  51.2 us (6%)
  local copies, waits for them, and re-layouts  46.9 us (5%)
  between operations  21.2 us (2%)
    pallas_call x2, Pallas kernels, duplex(): call_remote(functools.partial(duplex_kernel, pairs), collective, in_specs...  193 us
    pallas_call x1, Pallas kernels, enter(): call_remote(functools.partial(enter_kernel, plane, pairs), collective, in...  91.8 us
    pallas_call x1, Pallas kernels, leave(): call_remote(functools.partial(leave_kernel, plane, pairs), collective, in...  81.4 us
    reduce_scatter x4, waiting for transfers between devices, scatter_blocks(): lax.psum_scatter(grad_low, ('col', 'dp'), scatter_dimension=0, tiled=True)  66.1 us
    pallas_call x1, Pallas kernels, turn_back(): call_remote(functools.partial(turn_back_kernel, pairs), collective, in_sp...  61.6 us
    pallas_call x1, Pallas kernels, middle(): call_remote(functools.partial(middle_kernel, pairs), collective, in_specs...  57.4 us
    sub x5, other arithmetic, adam_update(): weight - learning_rate * (new_one / fix_one / (jnp.sqrt(new_two / fix_two...  20.4 us
    dot_general x1, matrix products, body(): jnp.einsum('td,tu->du', rows_ffn, grad_units, preferred_element_type=FULL)  19.5 us
  transfers between devices with their start and end apart: 8, of which 1 were waited for; matrix products, arithmetic and copies ran while one was open for 14% of the time, Pallas kernels for 43%

profile of v2, /device:TPU:0, one launch (start us, length us, event | category | flops | bytes accessed | tf_op | source)
XLA Modules:
  0.0 861.6 jit_solution(2720408992144446338)
XLA Ops:
  18.9 11.3 %shard_map.371 = (f32[2,2,96,1024]{3,2,1,0:T(8,128)S(1)}, f32[2,2,96,1024]{3,2,1,0:T(8,128)S(1)}, f32[2,2,96,1024]{3,2,1,0:T(8,128)S(1)}, bf16[2,2,96,1024]{3,2,1,0:T(8,128)(2,1)S(1)}, f32[16,8,256]{2,1,0:T(8,128)S(1)}) custom-call(f32[48]{0:T(128)S(1)} %reshape.189.hyper, f32[2,4,192,1024]{3,2,1,0:T(8,128)} %streams.3, f32[2,4,192,1024]{3,2,1,0:T(8,128)} %cotangent.3, ...), custom_call_target="tpu_custom_call" | custom-call | tf_op jit(solution)/shard_map/pallas_call | solution.py:140
  33.6 91.8 %shard_map.372 = (bf16[8,192,2048]{2,1,0:T(8,128)(2,1)}, f32[192,2048]{1,0:T(8,128)S(1)}, f32[192,2048]{1,0:T(8,128)S(1)}, f32[192,2048]{1,0:T(8,128)}, bf16[192,2048]{1,0:T(8,128)(2,1)S(1)}) custom-call(f32[2,2,96,1024]{3,2,1,0:T(8,128)} %copy-done.10, f32[2,2,96,1024]{3,2,1,0:T(8,128)} %copy-done.11, f32[2,2,96,1024]{3,2,1,0:T(8,128)} %copy-done.12, ...), custom_call_target="tpu_custom_call" | custom-call | tf_op jit(solution)/shard_map/pallas_call | solution.py:715
  133.6 8.1 fusion.18.q_in.k_in.v_in
  141.7 10.4 %shard_map.373 = (bf16[1536,256]{1,0:T(8,128)(2,1)S(1)}, f32[2,1536,1]{2,1,0:T(8,128)S(1)}, bf16[1536,256]{1,0:T(8,128)(2,1)S(1)}, bf16[1536,256]{1,0:T(8,128)(2,1)S(1)}, bf16[1536,256]{1,0:T(8,128)(2,1)S(1)}) custom-call(f32[1536,768]{1,0:T(8,128)S(1)} %fusion.18.q_in.k_in.v_in, f32[1536,768]{1,0:T(8,128)S(1)} %fusion.18.q_in.k_in.v_in, ...), custom_call_target="tpu_custom_call" | custom-call | tf_op jit(solution)/shard_map/pallas_call | solution.py:283
  156.7 94.7 %shard_map.374 = (bf16[8,192,2048]{2,1,0:T(8,128)(2,1)}, bf16[192,2048]{1,0:T(8,128)(2,1)S(1)}, f32[192,2048]{1,0:T(8,128)S(1)}) custom-call(bf16[8,192,2048]{2,1,0:T(8,128)(2,1)} %bitcast.106, bf16[192,2048]{1,0:T(8,128)(2,1)S(1)} %copy-done.26), custom_call_target="tpu_custom_call" | custom-call | tf_op jit(solution)/shard_map/pallas_call | solution.py:750
  252.3 57.4 %shard_map.375 = (bf16[8,192,2048]{2,1,0:T(8,128)(2,1)}, f32[192,2048]{1,0:T(8,128)S(1)}) custom-call(f32[48]{0:T(128)S(1)} %reshape.189.hyper, f32[192,2048]{1,0:T(8,128)S(1)} %copy-done.9, f32[192,2048]{1,0:T(8,128)S(1)} %get-tuple-element.65.branch), custom_call_target="tpu_custom_call" | custom-call | tf_op jit(solution)/shard_map/pallas_call | solution.py:781
  310.9 8.5 copy.73
  325.0 19.3 %fusion.19 = f32[1536,2048]{1,0:T(8,128)} fusion(bf16[1536,2048]{1,0:T(8,128)(2,1)} %bitcast.130, bf16[2048,2048]{1,0:T(8,128)(2,1)} %all-gather.9.cloned.1.call-done), kind=kOutput, calls=%fused_computation.98 | convolution fusion | flops 12884901888 | bytes 27262976 | tf_op jit(solution)/shard_map/dot_general | solution.py:1030
  344.3 16.2 %multiply_convert_fusion.1 = (bf16[1536,1024]{1,0:T(8,128)(2,1)}, bf16[1536,1024]{1,0:T(8,128)(2,1)}, bf16[1536,1024]{1,0:T(8,128)(2,1)S(1)}) fusion(f32[1536,2048]{1,0:T(8,128)} %fusion.19, bf16[1536,2048]{1,0:T(8,128)(2,1)} %bitcast.132, bf16[1024,2048]{1,0:T(8,128)(2,1)S(1)} %bitcast.118), kind=kOutput, calls=%fused_computation.9 | convolution fusion | flops 6466043904 | bytes 32505856 | tf_op jit(solution)/shard_map/td,ud->tu/dot_general | solution.py:1036
  360.4 8.7 %convolution_convert_fusion.4 = bf16[1536,2048]{1,0:T(8,128)(2,1)} fusion(bf16[1536,1024]{1,0:T(8,128)(2,1)S(1)} %get-tuple-element.124, bf16[1024,2048]{1,0:T(8,128)(2,1)S(1)} %bitcast.119), kind=kOutput, calls=%fused_computation.5 | convolution fusion | flops 6445596672 | bytes 13631488 | tf_op jit(solution)/shard_map/dot_general | solution.py:1044
  369.1 19.3 %convolution_convert_fusion.3 = bf16[1536,2048]{1,0:T(8,128)(2,1)} fusion(bf16[2048,2048]{1,0:T(8,128)(2,1)} %all-gather.9.cloned.1.call-done, bf16[1536,1024]{1,0:T(8,128)(2,1)} %get-tuple-element.123, bf16[1536,1024]{1,0:T(8,128)(2,1)} %get-tuple-element.122), kind=kOutput, calls=%fused_computation.4 | convolution fusion | flops 12900630528 | bytes 20971520 | tf_op jit(solution)/shard_map/tu,du->td/dot_general | solution.py:1040
  388.4 61.6 %shard_map.376 = (bf16[192,2048]{1,0:T(8,128)(2,1)S(1)}, bf16[192,2048]{1,0:T(8,128)(2,1)S(1)}) custom-call(f32[48]{0:T(128)S(1)} %reshape.189.hyper, bf16[8,192,2048]{2,1,0:T(8,128)(2,1)} %bitcast.114, f32[192,2048]{1,0:T(8,128)S(1)} %copy-done.7, f32[192,2048]{1,0:T(8,128)S(1)} %copy-done.3), custom_call_target="tpu_custom_call" | custom-call | tf_op jit(solution)/shard_map/pallas_call | solution.py:811
  450.9 98.3 %shard_map.377 = (bf16[8,192,2048]{2,1,0:T(8,128)(2,1)}, bf16[192,2048]{1,0:T(8,128)(2,1)S(1)}, f32[192,2048]{1,0:T(8,128)}) custom-call(bf16[8,192,2048]{2,1,0:T(8,128)(2,1)} %bitcast.112, bf16[192,2048]{1,0:T(8,128)(2,1)S(1)} %get-tuple-element.70.gathered), custom_call_target="tpu_custom_call" | custom-call | tf_op jit(solution)/shard_map/pallas_call | solution.py:750
  564.5 12.6 %shard_map.378 = (bf16[1536,256]{1,0:T(8,128)(2,1)S(1)}, bf16[1536,256]{1,0:T(8,128)(2,1)S(1)}, bf16[1536,256]{1,0:T(8,128)(2,1)S(1)}) custom-call(bf16[1536,256]{1,0:T(8,128)(2,1)S(1)} %convolution_convert_fusion.8.grad, bf16[1536,256]{1,0:T(8,128)(2,1)S(1)} %copy-done.20, bf16[1536,256]{1,0:T(8,128)(2,1)S(1)} %copy-done.22, ...), custom_call_target="tpu_custom_call" | custom-call | tf_op jit(solution)/shard_map/pallas_call | solution.py:301
  577.3 6.7 convolution_convert_fusion.6
  584.3 11.3 %convolution_convert_fusion.5 = bf16[1024,2048]{1,0:T(8,128)(2,1)} fusion(bf16[1536,1024]{1,0:T(8,128)(2,1)} %copy-done.48, bf16[1536,2048]{1,0:T(8,128)(2,1)} %bitcast.133), kind=kOutput, calls=%fused_computation.18 | convolution fusion | flops 6444548096 | bytes 13631488 | tf_op jit(solution)/shard_map/tu,td->ud/dot_general | solution.py:1052
  595.6 8.0 reshape.204
  609.3 19.5 %convolution_convert_fusion.2 = bf16[2048,2048]{1,0:T(8,128)(2,1)} fusion(bf16[1536,2048]{1,0:T(8,128)(2,1)} %bitcast.131, bf16[1536,1024]{1,0:T(8,128)(2,1)} %get-tuple-element.123, bf16[1536,1024]{1,0:T(8,128)(2,1)} %get-tuple-element.122), kind=kOutput, calls=%fused_computation.3 | convolution fusion | flops 12901679104 | bytes 20971520 | tf_op jit(solution)/shard_map/td,tu->du/dot_general | solution.py:1047
  631.0 9.1 %convolution_convert_fusion = bf16[1536,2048]{1,0:T(8,128)(2,1)} fusion(bf16[1536,768]{1,0:T(8,128)(2,1)S(1)} %constant_dynamic-update-slice_fusion, bf16[2048,768]{1,0:T(8,128)(2,1)} %all-gather.5.cloned.1.call-done), kind=kOutput, calls=%fused_computation.1 | convolution fusion | flops 4834983936 | bytes 11796480 | tf_op jit(solution)/shard_map/tu,du->td/dot_general | solution.py:1072
  640.1 81.4 %shard_map.379 = (bf16[2,2,96,1024]{3,2,1,0:T(8,128)(2,1)S(1)}, bf16[2,2,96,1024]{3,2,1,0:T(8,128)(2,1)S(1)}, bf16[2,2,96,1024]{3,2,1,0:T(8,128)(2,1)S(1)}, bf16[2,2,96,1024]{3,2,1,0:T(8,128)(2,1)S(1)}) custom-call(bf16[8,192,2048]{2,1,0:T(8,128)(2,1)} %bitcast.113, f32[192,2048]{1,0:T(8,128)} %copy-done.2, bf16[192,2048]{1,0:T(8,128)(2,1)S(1)} %copy-done.14, ...), custom_call_target="tpu_custom_call" | custom-call | tf_op jit(solution)/shard_map/pallas_call | solution.py:850
  721.6 12.8 %shard_map.380 = (f32[2,4,192,1024]{3,2,1,0:T(8,128)}, f32[2,4,192,1024]{3,2,1,0:T(8,128)}, f32[17,8,256]{2,1,0:T(8,128)S(1)}) custom-call(f32[48]{0:T(128)S(1)} %reshape.189.hyper, f32[2,4,192,1024]{3,2,1,0:T(8,128)} %streams.3, f32[2,4,192,1024]{3,2,1,0:T(8,128)} %cotangent.3, s32[2,192,1]{2,1,0:T(8,128)S(1)} %copy.77.sent, ...), custom_call_target="tpu_custom_call" | custom-call | tf_op jit(solution)/shard_map/pallas_call | solution.py:194
  743.6 66.1 %reduce-scatter.7.cloned.1.call-done = bf16[512,2048]{1,0:T(8,128)(2,1)} async-done(((bf16[2048,2048]{1,0:T(8,128)(2,1)}), bf16[512,2048]{1,0:T(8,128)(2,1)}) %reduce-scatter.7.cloned.1.call-update) | async-done | bytes 2097168 | tf_op jit(solution)/shard_map/reduce_scatter | solution.py:938
  818.8 9.6 %shard_map.381 = f32[1,128]{1,0:T(1,128)S(1)} custom-call(f32[1,128]{1,0:T(1,128)S(1)} %fusion.9.own), custom_call_target="tpu_custom_call" | custom-call | tf_op jit(solution)/shard_map/pallas_call | solution.py:912
  833.3 7.3 multiply_subtract_fusion.1
  (191 shorter events, 90.6 us)
Async XLA Ops:
  7.2 122.7 %all-gather.7.cloned.1.call-start = ((), (), s32[]{:S(2)}) async-start(), calls=%async_computation.5 | async-start | bytes 1310720 | tf_op jit(solution)/shard_map/all_gather | solution.py:934
  9.1 124.5 %all-gather.5.cloned.1.call-start = ((), (), s32[]{:S(2)}) async-start(), calls=%async_computation.4 | async-start | bytes 3932160 | tf_op jit(solution)/shard_map/all_gather | solution.py:934
  11.8 299.1 %all-gather.11.cloned.1.call-start = ((), (), s32[]{:S(2)}) async-start(), calls=%async_computation.7 | async-start | bytes 5242880 | tf_op jit(solution)/shard_map/all_gather | solution.py:934
  13.0 312.0 %all-gather.9.cloned.1.call-start = ((), (), s32[]{:S(2)}) async-start(), calls=%async_computation.6 | async-start | bytes 10485760 | tf_op jit(solution)/shard_map/all_gather | solution.py:934
  17.3 717.3 %reduce-scatter.9.cloned.1.call-start = ((), (), s32[]{:S(2)}) async-start(), calls=%async_computation.10 | async-start | bytes 1310720 | tf_op jit(solution)/shard_map/reduce_scatter | solution.py:938
  141.7 10.4 %copy-start.35 = (bf16[32,8,2,1024]{3,1,2,0:T(8,128)(2,1)S(1)}, bf16[32,8,2,1024]{3,1,2,0:T(8,128)(2,1)}, u32[]{:S(2)}) copy-start(bf16[32,8,2,1024]{3,1,2,0:T(8,128)(2,1)} %copy.89) | copy-start | bytes 3145732
  156.7 95.6 %copy-start.9 = (f32[192,2048]{1,0:T(8,128)S(1)}, f32[192,2048]{1,0:T(8,128)}, u32[]{:S(2)}) copy-start(f32[192,2048]{1,0:T(8,128)} %copy-done.8) | copy-start | bytes 4718596
  325.0 19.3 %copy-start.36 = (bf16[128,8,2,1024]{3,1,2,0:T(8,128)(2,1)S(1)}, bf16[128,8,2,1024]{3,1,2,0:T(8,128)(2,1)}, u32[]{:S(2)}) copy-start(bf16[128,8,2,1024]{3,1,2,0:T(8,128)(2,1)} %copy.90) | copy-start | bytes 12582916
  369.1 19.3 %copy-start.3 = (f32[192,2048]{1,0:T(8,128)S(1)}, f32[192,2048]{1,0:T(8,128)}, u32[]{:S(2)}) copy-start(f32[192,2048]{1,0:T(8,128)} %get-tuple-element.69.back) | copy-start | bytes 4718596
  369.1 19.3 %copy-start.7 = (f32[192,2048]{1,0:T(8,128)S(1)}, f32[192,2048]{1,0:T(8,128)}, u32[]{:S(2)}) copy-start(f32[192,2048]{1,0:T(8,128)} %copy-done.6) | copy-start | bytes 4718596
  558.8 177.5 %reduce-scatter.5.cloned.1.call-start = ((), (), s32[]{:S(2)}) async-start(), calls=%async_computation.8 | async-start | bytes 3932160 | tf_op jit(solution)/shard_map/reduce_scatter | solution.py:938
  564.4 12.9 %slice-start = ((s8[6291456]{0:T(1024)(128)(4,1)}), s8[4194304]{0:T(1024)(128)(4,1)S(1)}, s32[]{:S(2)}) async-start(s8[6291456]{0:T(1024)(128)(4,1)} %bitcast.127), calls=%async_computation.12 | async-start | bytes 8388608
  564.4 12.8 %slice-start.1 = ((s8[6291456]{0:T(1024)(128)(4,1)}), s8[2097152]{0:T(1024)(128)(4,1)S(1)}, s32[]{:S(2)}) async-start(s8[6291456]{0:T(1024)(128)(4,1)} %bitcast.127), calls=%async_computation.13 | async-start | bytes 4194304
  584.1 155.9 %reduce-scatter.11.cloned.1.call-start = ((), (), s32[]{:S(2)}) async-start(), calls=%async_computation.11 | async-start | bytes 5242880 | tf_op jit(solution)/shard_map/reduce_scatter | solution.py:938
  609.2 200.5 %reduce-scatter.7.cloned.1.call-start = ((), (), s32[]{:S(2)}) async-start(), calls=%async_computation.9 | async-start | bytes 10485760 | tf_op jit(solution)/shard_map/reduce_scatter | solution.py:938
  736.3 104.3 %copy-start.38 = (f32[128,1024]{1,0:T(8,128)}, f32[128,1024]{1,0:T(8,128)S(1)}, u32[]{:S(2)}) copy-start(f32[128,1024]{1,0:T(8,128)S(1)} %get-tuple-element.117) | copy-start | bytes 1572868
  812.4 20.2 %copy-start.46 = (f32[2,4,6]{2,1,0:T(4,128)S(1)}, f32[2,4,6]{2,1,0:T(4,128)}, u32[]{:S(2)}) copy-start(f32[2,4,6]{2,1,0:T(4,128)} %param.38) | copy-start | bytes 580
  812.4 20.2 %copy-start.47 = (f32[2,4,6]{2,1,0:T(4,128)S(1)}, f32[2,4,6]{2,1,0:T(4,128)}, u32[]{:S(2)}) copy-start(f32[2,4,6]{2,1,0:T(4,128)} %param.37) | copy-start | bytes 580
  812.4 20.8 %copy-start.30 = (f32[512,1024]{1,0:T(8,128)S(1)}, f32[512,1024]{1,0:T(8,128)}, u32[]{:S(2)}) copy-start(f32[512,1024]{1,0:T(8,128)} %param.27) | copy-start | bytes 6291460
  812.5 28.1 %copy-start.37 = (f32[128,1024]{1,0:T(8,128)S(1)}, f32[128,1024]{1,0:T(8,128)}, u32[]{:S(2)}) copy-start(f32[128,1024]{1,0:T(8,128)} %param.26) | copy-start | bytes 1572868
  833.3 10.8 %copy-start.27 = (f32[2,512,1024]{2,1,0:T(8,128)S(1)}, f32[2,512,1024]{2,1,0:T(8,128)}, u32[]{:S(2)}) copy-start(f32[2,512,1024]{2,1,0:T(8,128)} %param.25) | copy-start | bytes 12582916
  833.3 10.8 %copy-start.28 = (f32[2,512,1024]{2,1,0:T(8,128)S(1)}, f32[2,512,1024]{2,1,0:T(8,128)}, u32[]{:S(2)}) copy-start(f32[2,512,1024]{2,1,0:T(8,128)} %get-tuple-element.119) | copy-start | bytes 12582916
  833.3 10.8 %copy-start.33 = (f32[2,512,1024]{2,1,0:T(8,128)S(1)}, f32[2,512,1024]{2,1,0:T(8,128)}, u32[]{:S(2)}) copy-start(f32[2,512,1024]{2,1,0:T(8,128)} %param.33) | copy-start | bytes 12582916
  833.3 10.8 %copy-start.34 = (f32[2,512,1024]{2,1,0:T(8,128)S(1)}, f32[2,512,1024]{2,1,0:T(8,128)}, u32[]{:S(2)}) copy-start(f32[2,512,1024]{2,1,0:T(8,128)} %param.29) | copy-start | bytes 12582916
  (35 other events, 148.1 us)
Sparse Core Ops, SparseCore 0:
  10.5 29.8 all-gather.6
  42.8 79.1 all-gather.4
  124.4 52.4 all-gather.10
  179.1 87.5 all-gather.8
  558.9 27.7 reduce-scatter.8
  589.9 43.9 reduce-scatter.4
  637.6 81.4 reduce-scatter.10
  722.2 87.4 reduce-scatter.6

commit v3 on v2

--- a/solution.py
+++ b/solution.py
@@ -27,7 +27,7 @@
 ANY = pl.BlockSpec(memory_space=pl.ANY)
 VMEM = pl.BlockSpec(memory_space=pltpu.VMEM)
 SMEM = pl.BlockSpec(memory_space=pltpu.SMEM)
-ROOM = 48 * 2**20
+ROOM = 60 * 2**20
 
 
 def rotary_tables(segment):
@@ -508,20 +508,29 @@
 
             self.to_twin(origin, cut).start()
 
+    def twin_arrive(self, origin):
+        me, _, side = line_place()
+        for cut in range(self.cuts):
+            other = self.piece(self.out.at[origin * 2 + 1 - side], cut)
+            remote(
+                other,
+                other,
+                self.twin_send.at[origin, cut],
+                self.twin_recv.at[origin, cut],
+                {"row": me + 1 - 2 * side},
+            ).wait_recv()
+
     def finish(self):
-        me, place, side = line_place()
         self.stay().wait()
+        for origin in range(self.pairs):
+            self.twin_arrive(origin)
+        self.leave()
+
+    def leave(self):
+        _, place, _ = line_place()
         for origin in range(self.pairs):
             for cut in range(self.cuts):
                 self.to_twin(origin, cut).wait_send()
-                other = self.piece(self.out.at[origin * 2 + 1 - side], cut)
-                remote(
-                    other,
-                    other,
-                    self.twin_send.at[origin, cut],
-                    self.twin_recv.at[origin, cut],
-                    {"row": me + 1 - 2 * side},
-                ).wait_recv()
 
                 @pl.when((place < self.pairs - 1) & (origin <= place))
                 def _():
@@ -668,6 +677,93 @@
 
 def scatter_sems(pairs, cuts):
     return [DMA((pairs, cuts))] * 7
+
+
+class PlaneScatter:
+    def __init__(self, block_of, out, buffers, sems):
+        self.block_of, self.out = block_of, out
+        self.arrived, self.mine, self.onward, self.final = buffers
+        self.send, self.recv, self.loaded, self.send_on, self.recv_on = sems
+        self.height = out.shape[0] // 2
+
+    def places(self, half, index):
+        d, c = lax.axis_index("dp"), lax.axis_index("col")
+        if half == 0:
+            there = 1 - c if index == 0 else c
+            return {"dp": 1 - d}, self.block_of(there, 1 - d, 0), self.block_of(there, d, 0)
+        there = 1 - d if index == 0 else d
+        return {"col": 1 - c}, self.block_of(1 - c, there, 1), self.block_of(c, there, 1)
+
+    def move(self, half, index):
+        device, block, _ = self.places(half, index)
+        return remote(
+            block, self.arrived.at[half, index], self.send.at[half, index], self.recv.at[half, index], device
+        )
+
+    def load(self, half, index):
+        _, _, block = self.places(half, index)
+        return pltpu.make_async_copy(block, self.mine.at[half, index], self.loaded.at[half, index])
+
+    def move_on(self, half):
+        device = (
+            {"col": 1 - lax.axis_index("col")} if half == 0 else {"dp": 1 - lax.axis_index("dp")}
+        )
+        return remote(
+            self.onward.at[half], self.final.at[half], self.send_on.at[half], self.recv_on.at[half], device
+        )
+
+    def start(self):
+        for index in range(2):
+            for half in range(2):
+                self.move(half, index).start()
+                self.load(half, index).start()
+
+    def sum_of(self, half, index):
+        self.move(half, index).wait_recv()
+        self.load(half, index).wait()
+        return self.mine[half, index].astype(FULL) + self.arrived[half, index].astype(FULL)
+
+    def forward(self):
+        for half in range(2):
+            self.onward[half] = self.sum_of(half, 0).astype(LOW)
+            self.move_on(half).start()
+
+    def finish(self):
+        for half in range(2):
+            total = self.sum_of(half, 1)
+            self.move_on(half).wait_recv()
+            self.out[pl.ds(half * self.height, self.height)] = total + self.final[half].astype(FULL)
+        for half in range(2):
+            for index in range(2):
+                self.move(half, index).wait_send()
+            self.move_on(half).wait_send()
+
+
+def by_rows(part, height):
+    half_height = height // 2
+    return lambda c, d, half: part.at[pl.ds((c * 2 + d) * height + half * half_height, half_height)]
+
+
+def by_tiles(part, height, width):
+    half_height = height // 2
+    return lambda c, d, half: part.at[
+        pl.ds(d * height + half * half_height, half_height), pl.ds(pl.multiple_of(c * width, width), width)
+    ]
+
+
+def plane_scratch(rows, width):
+    half = (rows // 2, width)
+    return [
+        pltpu.VMEM((2, 2) + half, LOW),
+        pltpu.VMEM((2, 2) + half, LOW),
+        pltpu.VMEM((2,) + half, LOW),
+        pltpu.VMEM((2,) + half, LOW),
+        DMA((2, 2)),
+        DMA((2, 2)),
+        DMA((2, 2)),
+        DMA((2,)),
+        DMA((2,)),
+    ]
 
 
 CUTS = 2
@@ -729,103 +825,340 @@
     return [outs[0].reshape(2 * pairs * rows, n_col * width)] + list(outs[1:])
 
 
-def duplex_kernel(pairs, part, gathered, rows_out, low_out, total, *scratch):
+def duplex_kernel(pairs, plane, count, part, gathered, *rest):
+    grads, rest = rest[:count], rest[count:]
+    (rows_out, low_out), rest = rest[:2], rest[2:]
+    sums, rest = rest[:count], rest[count:]
+    total, scratch, rest = rest[0], rest[1:], rest[20:]
     scatter = Scatter(pairs, CUTS, part, scratch[:6], scratch[6:13])
-    gather = Gather(pairs, CUTS, gathered, rows_out, scratch[13:])
-    greet(pairs)
+    gather = Gather(pairs, CUTS, gathered, rows_out, scratch[13:19])
+    planes = plane_sums(grads, sums, rest)
+    greet(pairs, plane if count else None)
     scatter.start()
     gather.start()
+    for one in planes:
+        one.start()
     for step in range(pairs - 1):
         for cut in range(CUTS):
             scatter.step(step, cut)
             gather.step(step + 1, cut)
+        if 0 < step <= len(planes):
+            planes[step - 1].forward()
     scatter.finish(total)
     low_out[...] = total[...].astype(LOW)
     gather.finish()
-
-
-def duplex(pairs, partial, gathered, collective):
+    for one in planes:
+        one.finish()
+
+
+def plane_sums(grads, sums, scratch):
+    planes = []
+    for index, (grad, total) in enumerate(zip(grads, sums)):
+        rows, width = total.shape
+        block_of = by_rows(grad, rows) if grad.shape[1] == width else by_tiles(grad, rows, width)
+        planes.append(
+            PlaneScatter(
+                block_of, total, scratch[9 * index : 9 * index + 4], scratch[9 * index + 4 : 9 * index + 9]
+            )
+        )
+    return planes
+
+
+def owned_shape(grad):
+    rows, width = grad.shape
+    return (rows // 4, width) if rows == D else (rows // 2, width // 2)
+
+
+def duplex(pairs, plane, partial, gathered, grads, collective):
     rows, width = gathered.shape
     whole = jax.ShapeDtypeStruct((2 * pairs, rows, width), LOW)
+    owned = [owned_shape(grad) for grad in grads]
     outs = call_remote(
-        functools.partial(duplex_kernel, pairs),
+        functools.partial(duplex_kernel, pairs, plane, len(grads)),
         collective,
-        in_specs=[ANY, ANY],
-        out_specs=[ANY, VMEM, VMEM],
-        out_shape=[
-            whole,
-            jax.ShapeDtypeStruct((rows, width), LOW),
-            jax.ShapeDtypeStruct((rows, width), FULL),
-        ],
+        in_specs=[ANY] * (2 + len(grads)),
+        out_specs=[ANY] + [VMEM] * (2 + len(grads)),
+        out_shape=[whole, jax.ShapeDtypeStruct((rows, width), LOW)]
+        + [jax.ShapeDtypeStruct(shape, FULL) for shape in owned]
+        + [jax.ShapeDtypeStruct((rows, width), FULL)],
         scratch_shapes=scatter_buffers(pairs, rows, width)
         + scatter_sems(pairs, CUTS)
-        + gather_sems(pairs, CUTS),
-    )(partial.reshape(whole.shape), gathered)
-    return [outs[0].reshape(2 * pairs * rows, width)] + list(outs[1:])
-
-
-def middle_kernel(pairs, hyper, mix, branch, rows_out, h, own, *sems):
+        + gather_sems(pairs, CUTS)
+        + sum([plane_scratch(*shape) for shape in owned], []),
+    )(partial.reshape(whole.shape), gathered, *grads)
+    return outs[0].reshape(2 * pairs * rows, width), outs[1], outs[-1], outs[2:-1]
+
+
+def arrival(place, pairs, step):
+    chosen = jnp.int32(0)
+    for here in range(pairs):
+        order = sorted(range(pairs), key=lambda there: abs(there - here))
+        chosen = jnp.where(place == here, order[step], chosen)
+    return chosen
+
+
+UNIT = 256
+
+
+def ffn_kernel(
+    pairs, hyper, mix, branch, back, w_in, w_out, gy_rows,
+    rows_out, hid_out, units_out, y_out, h, gh_out, gy_out,
+    own, x, wd, gy, hid, units, y, part, twin, from_left, from_right, total, upstream,
+    load_sem, gy_sem, hid_sem, units_sem, y_sem, x_sem,
+    twin_send, twin_recv, right_send, right_recv, left_send, left_recv, *line_sems,
+):
+    me, place, side = line_place()
+    last = pairs - 1
+    rows = own.shape[0]
+    height = rows // CUTS
+    n_col, n_dp, owned, width = w_out.shape
+    half = units.shape[2] // 2
     greet(pairs)
-    h[...] = mix[...] + branch_weight(hyper) * branch[...]
+    loads = [
+        pltpu.make_async_copy(mix, h, load_sem.at[0]),
+        pltpu.make_async_copy(branch, total, load_sem.at[1]),
+        pltpu.make_async_copy(back, upstream, load_sem.at[2]),
+    ]
+    for load in loads:
+        load.start()
+    tiles = [
+        pltpu.make_async_copy(
+            w_out.at[c, d],
+            wd.at[pl.ds(d * owned, owned), pl.ds(c * width, width)],
+            load_sem.at[3 + c * n_dp + d],
+        )
+        for c in range(n_col)
+        for d in range(n_dp)
+    ]
+    for tile in tiles:
+        tile.start()
+    order = [arrival(place, pairs, step) for step in range(pairs)]
+
+    def load_gy(step):
+        return pltpu.make_async_copy(gy_rows.at[order[step]], gy.at[step % 2], gy_sem.at[step % 2])
+
+    load_gy(0).start()
+    loads[0].wait()
+    loads[1].wait()
+    h[...] = h[...] + branch_weight(hyper) * total[...]
     own[...] = norm_forward(h[...])[0].astype(LOW)
-    gather = Gather(pairs, CUTS, own, rows_out, sems)
+    gather = Gather(pairs, CUTS, own, x, line_sems)
     gather.start()
-    for step in range(1, pairs):
+    for tile in tiles:
+        tile.wait()
+
+    def saves(step):
+        slot = step % 2
+        return [
+            pltpu.make_async_copy(hid.at[slot], hid_out.at[order[step]], hid_sem.at[slot]),
+            pltpu.make_async_copy(units.at[slot], units_out.at[order[step]], units_sem.at[slot]),
+            pltpu.make_async_copy(y.at[slot], y_out.at[order[step]], y_sem.at[slot]),
+        ]
+
+    def save_x(step):
+        return pltpu.make_async_copy(
+            x.at[pl.ds(order[step] * 2, 2)], rows_out.at[pl.ds(order[step] * 2, 2)], x_sem.at[step]
+        )
+
+    def work(step):
+        slot = step % 2
+        x_block = x.at[pl.ds(order[step] * 2, 2)]
+
+        @pl.loop(0, half // UNIT)
+        def _(unit):
+            at = pl.multiple_of(unit * UNIT, UNIT)
+            rows_in = x_block[...].reshape(2 * rows, -1)
+            gate = jnp.dot(rows_in, w_in[:, pl.ds(at, UNIT)], preferred_element_type=FULL)
+            up = jnp.dot(rows_in, w_in[:, pl.ds(half + at, UNIT)], preferred_element_type=FULL)
+            grad = dot_last(gy[slot], wd[pl.ds(at, UNIT)])
+            sigma = 1.0 / (1.0 + jnp.exp(-gate))
+            silu = gate * sigma
+            hid[slot, :, pl.ds(at, UNIT)] = (silu * up).astype(LOW)
+            units[slot, :, pl.ds(at, UNIT)] = (
+                grad * up * sigma * (1.0 + gate * (1.0 - sigma))
+            ).astype(LOW)
+            units[slot, :, pl.ds(half + at, UNIT)] = (grad * silu).astype(LOW)
+
+        @pl.loop(0, D // UNIT)
+        def _(unit):
+            at = pl.multiple_of(unit * UNIT, UNIT)
+            y_tile = jnp.dot(hid[slot], wd[:, pl.ds(at, UNIT)], preferred_element_type=FULL)
+            y[slot, :, pl.ds(at, UNIT)] = y_tile.astype(LOW)
+            tile = dot_last(units[slot], w_in[pl.ds(at, UNIT)]).astype(LOW)
+            part[pl.ds(order[step] * 2, 2), :, pl.ds(at, UNIT)] = tile.reshape(2, rows, UNIT)
+
+    def to_twin(dest):
+        return remote(
+            part.at[dest * 2 + 1 - side],
+            twin.at[dest],
+            twin_send.at[dest],
+            twin_recv.at[dest],
+            {"row": me + 1 - 2 * side},
+        )
+
+    def line(dest, cut, rightward):
+        span = pl.ds(cut * height, height)
+        return remote(
+            part.at[dest * 2 + side, span],
+            (from_left if rightward else from_right).at[dest, span],
+            (right_send if rightward else left_send).at[dest, cut],
+            (right_recv if rightward else left_recv).at[dest, cut],
+            {"row": me + 2 if rightward else me - 2},
+        )
+
+    def here(dest, span):
+        return part[dest * 2 + side, span].astype(FULL) + twin[dest, span].astype(FULL)
+
+    def send_first(step):
+        dest = order[step]
+        to_twin(dest).wait_recv()
+        for at_end, rightward in ((place == 0, True), (place == last, False)):
+            @pl.when(at_end & (dest != place))
+            def _():
+                for cut in range(CUTS):
+                    span = pl.ds(cut * height, height)
+                    part[dest * 2 + side, span] = here(dest, span).astype(LOW)
+                    line(dest, cut, rightward).start()
+
+    for step in range(pairs):
+        if step > 0:
+            for cut in range(CUTS):
+                gather.step(step, cut)
+        else:
+            gather.stay().wait()
+        if step + 1 < pairs:
+            load_gy(step + 1).start()
+        gather.twin_arrive(order[step])
+        save_x(step).start()
+        load_gy(step).wait()
+        if step >= 2:
+            for save in saves(step - 2):
+                save.wait()
+        work(step)
+        to_twin(order[step]).start()
+        for save in saves(step):
+            save.start()
+        if step > 0:
+            send_first(step - 1)
+    send_first(pairs - 1)
+
+    def pass_on(dest, rightward):
+        arrived = from_left if rightward else from_right
         for cut in range(CUTS):
-            gather.step(step, cut)
-    gather.finish()
-
-
-def middle(pairs, hyper, mix, branch, collective):
+            span = pl.ds(cut * height, height)
+            line(dest, cut, rightward).wait_recv()
+            part[dest * 2 + side, span] = (here(dest, span) + arrived[dest, span].astype(FULL)).astype(LOW)
+            line(dest, cut, rightward).start()
+
+    for reach in range(2, pairs):
+        rightward, leftward = (place > 0) & (place < reach), (place < last) & (place > last - reach)
+        pl.when(rightward & (place < pairs // 2))(functools.partial(pass_on, reach, True))
+        pl.when(leftward)(functools.partial(pass_on, last - reach, False))
+        pl.when(rightward & (place >= pairs // 2))(functools.partial(pass_on, reach, True))
+
+    for cut in range(CUTS):
+        span = pl.ds(cut * height, height)
+        total[span] = here(place, span)
+
+        @pl.when(place > 0)
+        def _():
+            line(place, cut, True).wait_recv()
+            total[span] += from_left[place, span].astype(FULL)
+
+        @pl.when(place < last)
+        def _():
+            line(place, cut, False).wait_recv()
+            total[span] += from_right[place, span].astype(FULL)
+
+    loads[2].wait()
+    grad = norm_backward(total[...], h[...])
+    gh_out[...] = grad.astype(LOW)
+    gy_out[...] = (upstream[...] + branch_weight(hyper) * grad).astype(LOW)
+
+    gather.leave()
+    for step in range(pairs):
+        save_x(step).wait()
+    for step in range(pairs - 2, pairs):
+        for save in saves(step):
+            save.wait()
+    for dest in range(pairs):
+        to_twin(dest).wait_send()
+        for cut in range(CUTS):
+            @pl.when(place < dest)
+            def _():
+                line(dest, cut, True).wait_send()
+
+            @pl.when(place > dest)
+            def _():
+                line(dest, cut, False).wait_send()
+
+
+def feed_forward(pairs, hyper, mix, branch, back, w_in, w_out, gy_rows, collective):
     rows, width = mix.shape
+    units = w_in.shape[1]
+    half = units // 2
+    n_col, n_dp = w_out.shape[:2]
+    low = jax.ShapeDtypeStruct((rows, width), LOW)
+
+    def by_pair(last_width):
+        return jax.ShapeDtypeStruct((pairs, 2 * rows, last_width), LOW)
+
+    blocks = pltpu.VMEM((pairs, rows, width), LOW)
+    full = pltpu.VMEM((rows, width), FULL)
     outs = call_remote(
-        functools.partial(middle_kernel, pairs),
+        functools.partial(ffn_kernel, pairs),
         collective,
-        in_specs=[SMEM, VMEM, VMEM],
-        out_specs=[ANY, VMEM],
+        in_specs=[SMEM, ANY, ANY, ANY, VMEM, ANY, ANY],
+        out_specs=[ANY, ANY, ANY, ANY, VMEM, VMEM, VMEM],
         out_shape=[
             jax.ShapeDtypeStruct((2 * pairs, rows, width), LOW),
+            by_pair(half),
+            by_pair(units),
+            by_pair(width),
             jax.ShapeDtypeStruct((rows, width), FULL),
+            low,
+            low,
         ],
-        scratch_shapes=[pltpu.VMEM((rows, width), LOW)] + gather_sems(pairs, CUTS),
-    )(hyper, mix, branch)
-    return outs[0].reshape(2 * pairs * rows, width), outs[1]
-
-
-def turn_back_kernel(pairs, hyper, part, h, back, gh_out, gy_out, total, *scratch):
+        scratch_shapes=[
+            pltpu.VMEM((rows, width), LOW),
+            pltpu.VMEM((2 * pairs, rows, width), LOW),
+            pltpu.VMEM((half, width), LOW),
+            pltpu.VMEM((2, 2 * rows, width), LOW),
+            pltpu.VMEM((2, 2 * rows, half), LOW),
+            pltpu.VMEM((2, 2 * rows, units), LOW),
+            pltpu.VMEM((2, 2 * rows, width), LOW),
+            pltpu.VMEM((2 * pairs, rows, width), LOW),
+            blocks,
+            blocks,
+            blocks,
+            full,
+            full,
+            DMA((3 + n_col * n_dp,)),
+            DMA((2,)),
+            DMA((2,)),
+            DMA((2,)),
+            DMA((2,)),
+            DMA((pairs,)),
+            DMA((pairs,)),
+            DMA((pairs,)),
+        ]
+        + [DMA((pairs, CUTS))] * 4
+        + gather_sems(pairs, CUTS),
+    )(hyper, mix, branch, back, w_in, w_out, gy_rows.reshape(pairs, 2 * rows, width))
+    tokens = 2 * pairs * rows
+    return [value.reshape(tokens, -1) for value in outs[:4]] + list(outs[5:])
+
+
+def leave_kernel(plane, pairs, count, part, h, y_att, y_ffn, gh_ffn, *rest):
+    grads, rest = rest[:count], rest[count:]
+    homes, sums, rest = rest[:4], rest[4 : 4 + count], rest[4 + count :]
+    (total, last), plane_sems, scratch, rest = rest[:2], rest[2:5], rest[5:18], rest[18:]
     scatter = Scatter(pairs, CUTS, part, scratch[:6], scratch[6:])
-    greet(pairs)
-    scatter.start()
-    for step in range(pairs - 1):
-        for cut in range(CUTS):
-            scatter.step(step, cut)
-    scatter.finish(total)
-    grad = norm_backward(total[...], h[...])
-    gh_out[...] = grad.astype(LOW)
-    gy_out[...] = (back[...] + branch_weight(hyper) * grad).astype(LOW)
-
-
-def turn_back(pairs, hyper, partial, h, back, collective):
-    rows, width = h.shape
-    low = jax.ShapeDtypeStruct((rows, width), LOW)
-    return call_remote(
-        functools.partial(turn_back_kernel, pairs),
-        collective,
-        in_specs=[SMEM, ANY, VMEM, VMEM],
-        out_specs=[VMEM, VMEM],
-        out_shape=[low, low],
-        scratch_shapes=[pltpu.VMEM((rows, width), FULL)]
-        + scatter_buffers(pairs, rows, width)
-        + scatter_sems(pairs, CUTS),
-    )(hyper, partial.reshape(2 * pairs, rows, width), h, back)
-
-
-def leave_kernel(plane, pairs, part, h, y_att, y_ffn, gh_ffn, *rest):
-    homes, total, last = rest[:4], rest[4], rest[5]
-    plane_sems, scratch = rest[6:9], rest[9:]
-    scatter = Scatter(pairs, CUTS, part, scratch[:6], scratch[6:])
+    planes = plane_sums(grads, sums, rest)
     greet(pairs, plane)
     scatter.start()
+    for one in planes:
+        one.start()
     ways = [
         to_home(plane, work, home, plane_sems, index)
         for index, (work, home) in enumerate(zip((y_att, y_ffn, gh_ffn, last), homes))
@@ -835,29 +1168,36 @@
     for step in range(pairs - 1):
         for cut in range(CUTS):
             scatter.step(step, cut)
+        if 0 < step <= len(planes):
+            planes[step - 1].forward()
     scatter.finish(total)
     last[...] = norm_backward(total[...], h[...]).astype(last.dtype)
     ways[3].start()
+    for one in planes:
+        one.finish()
     for way in ways:
         way.arrive()
         way.leave()
 
 
-def leave(plane, pairs, partial, h, works, collective):
+def leave(plane, pairs, partial, h, works, grads, collective):
     rows, width = h.shape
     n_dp, n_col = plane
     home = jax.ShapeDtypeStruct((n_dp, n_col, rows // n_dp, width // n_col), works[0].dtype)
-    return call_remote(
-        functools.partial(leave_kernel, plane, pairs),
+    owned = [owned_shape(grad) for grad in grads]
+    outs = call_remote(
+        functools.partial(leave_kernel, plane, pairs, len(grads)),
         collective,
-        in_specs=[ANY, VMEM, ANY, ANY, ANY],
-        out_specs=[ANY] * 4,
-        out_shape=[home] * 4,
+        in_specs=[ANY, VMEM, ANY, ANY, ANY] + [ANY] * len(grads),
+        out_specs=[ANY] * 4 + [VMEM] * len(grads),
+        out_shape=[home] * 4 + [jax.ShapeDtypeStruct(shape, FULL) for shape in owned],
         scratch_shapes=[pltpu.VMEM((rows, width), FULL), pltpu.VMEM((rows, width), works[0].dtype)]
         + exchange_sems(plane, 4)
         + scatter_buffers(pairs, rows, width)
-        + scatter_sems(pairs, CUTS),
-    )(partial.reshape(2 * pairs, rows, width), h, *works)
+        + scatter_sems(pairs, CUTS)
+        + sum([plane_scratch(*shape) for shape in owned], []),
+    )(partial.reshape(2 * pairs, rows, width), h, *works, *grads)
+    return outs[:4], outs[4:]
 
 
 def total_kernel(plane, count, own, out, line, flat, line_send, line_recv, flat_send, flat_recv):
@@ -1002,7 +1342,9 @@
     attention_in_low = gather_blocks(side_by_side(attention_in).astype(LOW))
     attention_out_low = whole_out(attention_out.astype(LOW), n_dp, n_col)
     feedforward_in_low = gather_blocks(side_by_side(feedforward_in).astype(LOW))
-    feedforward_out_low = whole_out(feedforward_out.astype(LOW), n_dp, n_col)
+    feedforward_out_low = gather_blocks(feedforward_out.astype(LOW)).reshape(
+        n_col, n_dp, *feedforward_out.shape
+    )
 
     group = destination // group_tokens
     sent = (
@@ -1024,38 +1366,29 @@
     qkv = jnp.dot(rows_att, attention_in_low, preferred_element_type=FULL)
     heads_low, log_totals, query_low, key_low, value_low = attend_forward(qkv, cosine, sine, start)
     partial_att = jnp.dot(heads_low, attention_out_low, preferred_element_type=FULL).astype(LOW)
-    grad_rows_ffn, branch_low, branch_att = duplex(pairs, partial_att, gy_work.astype(LOW), 2)
-    rows_ffn, hidden_ffn = middle(pairs, hyper, mix_work, branch_att, 3)
-
-    gate_up = jnp.dot(rows_ffn, feedforward_in_low, preferred_element_type=FULL)
-    units = gate_up.shape[1] // 2
-    gate_pre, up_pre = gate_up[:, :units], gate_up[:, units:]
-    sigma = jax.nn.sigmoid(gate_pre)
-    silu = gate_pre * sigma
-    hidden_low = (silu * up_pre).astype(LOW)
-    grad_hidden = jnp.einsum("td,ud->tu", grad_rows_ffn, feedforward_out_low, preferred_element_type=FULL)
-    grad_gate = (grad_hidden * up_pre * sigma * (1.0 + gate_pre * (1.0 - sigma))).astype(LOW)
-    grad_up = (grad_hidden * silu).astype(LOW)
-    grad_units = jnp.concatenate([grad_gate, grad_up], axis=1)
-    partial_grad = jnp.einsum(
-        "tu,du->td", grad_units, feedforward_in_low, preferred_element_type=FULL
-    ).astype(LOW)
-    grad_hidden_ffn, grad_branch = turn_back(pairs, hyper, partial_grad, hidden_ffn, back_work, 4)
-    partial_ffn = jnp.dot(hidden_low, feedforward_out_low, preferred_element_type=FULL).astype(LOW)
-    shard_feedforward_in = apart(
-        scatter_blocks(
-            jnp.einsum("td,tu->du", rows_ffn, grad_units, preferred_element_type=FULL).astype(LOW)
-        ),
-        2,
-    )
-    shard_feedforward_out = own_out(
-        jnp.einsum("tu,td->ud", hidden_low, grad_rows_ffn, preferred_element_type=FULL), n_dp, n_col
-    )
-    grad_rows_att, branch_ffn, _ = duplex(pairs, partial_ffn, grad_branch, 5)
-
-    shard_attention_out = own_out(
-        jnp.einsum("tu,td->ud", heads_low, grad_rows_att, preferred_element_type=FULL), n_dp, n_col
-    )
+    grad_rows_ffn, branch_low, branch_att, _ = duplex(
+        pairs, plane, partial_att, gy_work.astype(LOW), [], 2
+    )
+    rows_ffn, hidden_low, grad_units, partial_ffn, grad_hidden_ffn, grad_branch = feed_forward(
+        pairs,
+        hyper,
+        mix_work,
+        branch_att,
+        back_work,
+        feedforward_in_low,
+        feedforward_out_low,
+        grad_rows_ffn,
+        3,
+    )
+    in_kernel = plane == (2, 2)
+    grads_ffn = [
+        jnp.einsum("td,tu->du", rows_ffn, grad_units, preferred_element_type=FULL).astype(LOW),
+        jnp.einsum("tu,td->ud", hidden_low, grad_rows_ffn, preferred_element_type=FULL).astype(LOW),
+    ]
+    grad_rows_att, branch_ffn, _, sums_ffn = duplex(
+        pairs, plane, partial_ffn, grad_branch, grads_ffn if in_kernel else [], 5
+    )
+
     grad_heads = jnp.einsum(
         "td,ud->tu", grad_rows_att, attention_out_low, preferred_element_type=FULL
     ).astype(LOW)
@@ -1063,23 +1396,28 @@
         attend_backward(grad_heads, query_low, key_low, value_low, log_totals, cosine, sine, start),
         axis=1,
     )
-    shard_attention_in = apart(
-        scatter_blocks(
-            jnp.einsum("td,tu->du", rows_att, grad_units_att, preferred_element_type=FULL).astype(LOW)
-        ),
-        3,
-    )
+    grads_att = [
+        jnp.einsum("td,tu->du", rows_att, grad_units_att, preferred_element_type=FULL).astype(LOW),
+        jnp.einsum("tu,td->ud", heads_low, grad_rows_att, preferred_element_type=FULL).astype(LOW),
+    ]
     partial_grad = jnp.einsum(
         "tu,du->td", grad_units_att, attention_in_low, preferred_element_type=FULL
     ).astype(LOW)
-    homes = leave(
+    homes, sums_att = leave(
         plane,
         pairs,
         partial_grad,
         hidden_att,
         [value.astype(travel) for value in (branch_low, branch_ffn, grad_hidden_ffn)],
+        grads_att if in_kernel else [],
         6,
     )
+    if not in_kernel:
+        sums_ffn, sums_att = (
+            [scatter_blocks(grads[0]), own_out(grads[1], n_dp, n_col)] for grads in (grads_ffn, grads_att)
+        )
+    shard_feedforward_in, shard_feedforward_out = apart(sums_ffn[0], 2), sums_ffn[1]
+    shard_attention_in, shard_attention_out = apart(sums_att[0], 3), sums_att[1]
     streams_out, stream_grad, dots = finish(hyper, streams, cotangent, sent, homes)
     square = (
         jnp.sum(shard_attention_in * shard_attention_in)

time: 871 us -> 752 us (0.86)
  matrix products: 133 us -> 62 us
  waiting for transfers between devices: 66.3 us -> 16.5 us
  Pallas kernels: 542 us -> 577 us
  local copies, waits for them, and re-layouts: 46.9 us -> 19.5 us
    reduce_scatter x4 -> x0, waiting for transfers between devices: 66.1 us -> none  [scatter_blocks(): lax.psum_scatter(grad_low, ('col', 'dp'), scatter_dimension=0, tiled=True)]
    dot_general x4 -> x0, matrix products: 63.4 us -> none  [the longest x1 19.3 us: body(): jnp.einsum('tu,du->td', grad_units, feedforward_in_low, preferred_element...]
    pallas_call x5 -> x4, Pallas kernels: 393 us -> 416 us  [the longest x2 205 us: duplex(): call_remote(functools.partial(duplex_kernel, pairs, plane, len(grads)), c...]
    all_gather x4, waiting for transfers between devices: 0.03 us -> 16.5 us  [gather_blocks(): return lax.all_gather(weight_low, ('col', 'dp'), axis=0, tiled=True)]
    unnamed x106 -> x83, local copies, waits for them, and re-layouts: 16.2 us -> 5.92 us
    reshape x2 -> x0, local copies, waits for them, and re-layouts: 9.78 us -> none  [own_out(): grad.astype(LOW).reshape(n_dp, rows, n_col, width).transpose(2, 0, 1, 3)]
    pallas_call x1, Pallas kernels: 9.56 us -> 19.3 us  [sum_everywhere(): call_remote(functools.partial(total_kernel, plane, count), collective, in...]
  transfers between devices with their start and end apart: 8 -> 4, of which waited for: 1 -> 1; matrix products, arithmetic and copies ran while one was open for 14% -> 4% of each run, Pallas kernels for 43% -> 28%
where the time goes in v3:
time: 752 us; the launch traced here: 744 us
  Pallas kernels  577 us (77%)
  matrix products  62 us (8%)
  other arithmetic  48.5 us (6%)
  between operations  20.4 us (3%)
  local copies, waits for them, and re-layouts  19.5 us (3%)
  waiting for transfers between devices  16.5 us (2%)
    pallas_call x2, Pallas kernels, duplex(): call_remote(functools.partial(duplex_kernel, pairs, plane, len(grads)), c...  205 us
    pallas_call x1, Pallas kernels, feed_forward(): call_remote(functools.partial(ffn_kernel, pairs), collective, in_specs=[S...  135 us
    pallas_call x1, Pallas kernels, enter(): call_remote(functools.partial(enter_kernel, plane, pairs), collective, in...  92.4 us
    pallas_call x1, Pallas kernels, leave(): call_remote(functools.partial(leave_kernel, plane, pairs, len(grads)), co...  76.1 us
    sub x5, other arithmetic, adam_update(): weight - learning_rate * (new_one / fix_one / (jnp.sqrt(new_two / fix_two...  20.2 us
    pallas_call x1, Pallas kernels, sum_everywhere(): call_remote(functools.partial(total_kernel, plane, count), collective, in...  19.3 us
    all_gather x4, waiting for transfers between devices, gather_blocks(): return lax.all_gather(weight_low, ('col', 'dp'), axis=0, tiled=True)  16.5 us
    dot_general x1, matrix products, body(): jnp.einsum('td,tu->du', rows_ffn, grad_units, preferred_element_type=FULL)  15.9 us
  transfers between devices with their start and end apart: 4, of which 1 were waited for; matrix products, arithmetic and copies ran while one was open for 4% of the time, Pallas kernels for 28%

profile of v3, /device:TPU:0, one launch (start us, length us, event | category | flops | bytes accessed | tf_op | source)
XLA Modules:
  0.0 744.3 jit_solution(6698312299094774431)
XLA Ops:
  22.4 12.7 %shard_map.371 = (f32[2,2,96,1024]{3,2,1,0:T(8,128)}, f32[2,2,96,1024]{3,2,1,0:T(8,128)}, f32[2,2,96,1024]{3,2,1,0:T(8,128)}, bf16[2,2,96,1024]{3,2,1,0:T(8,128)(2,1)}, f32[16,8,256]{2,1,0:T(8,128)}) custom-call(f32[48]{0:T(128)} %reshape.174.hyper, f32[2,4,192,1024]{3,2,1,0:T(8,128)} %streams.3, f32[2,4,192,1024]{3,2,1,0:T(8,128)} %cotangent.3, ...), custom_call_target="tpu_custom_call" | custom-call | tf_op jit(solution)/shard_map/pallas_call | solution.py:140
  36.3 92.4 %shard_map.372 = (bf16[8,192,2048]{2,1,0:T(8,128)(2,1)}, f32[192,2048]{1,0:T(8,128)}, f32[192,2048]{1,0:T(8,128)}, f32[192,2048]{1,0:T(8,128)}, bf16[192,2048]{1,0:T(8,128)(2,1)}) custom-call(f32[2,2,96,1024]{3,2,1,0:T(8,128)} %get-tuple-element.63.h_home, f32[2,2,96,1024]{3,2,1,0:T(8,128)} %get-tuple-element.64.mix_home, ...), custom_call_target="tpu_custom_call" | custom-call | tf_op jit(solution)/shard_map/pallas_call | solution.py:811
  128.9 2.8 fusion.4
  135.8 8.9 %fusion.15.q_in.k_in.v_in = f32[1536,768]{1,0:T(8,128)S(1)} fusion(bf16[1536,2048]{1,0:T(8,128)(2,1)} %bitcast.108, bf16[2048,768]{1,0:T(8,128)(2,1)} %all-gather.5.cloned.1.call-done), kind=kOutput, calls=%fused_computation.87 | convolution fusion | flops 4831838208 | bytes 14155776 | tf_op jit(solution)/shard_map/dot_general | solution.py:1366
  144.7 10.3 %shard_map.373 = (bf16[1536,256]{1,0:T(8,128)(2,1)S(1)}, f32[2,1536,1]{2,1,0:T(8,128)S(1)}, bf16[1536,256]{1,0:T(8,128)(2,1)S(1)}, bf16[1536,256]{1,0:T(8,128)(2,1)S(1)}, bf16[1536,256]{1,0:T(8,128)(2,1)S(1)}) custom-call(f32[1536,768]{1,0:T(8,128)S(1)} %fusion.15.q_in.k_in.v_in, f32[1536,768]{1,0:T(8,128)S(1)} %fusion.15.q_in.k_in.v_in, ...), custom_call_target="tpu_custom_call" | custom-call | tf_op jit(solution)/shard_map/pallas_call | solution.py:283
  155.0 4.6 convolution_convert_fusion.1
  159.6 96.3 %shard_map.374 = (bf16[8,192,2048]{2,1,0:T(8,128)(2,1)}, bf16[192,2048]{1,0:T(8,128)(2,1)}, f32[192,2048]{1,0:T(8,128)}) custom-call(bf16[8,192,2048]{2,1,0:T(8,128)(2,1)} %bitcast.94, bf16[192,2048]{1,0:T(8,128)(2,1)} %get-tuple-element.70.gathered), custom_call_target="tpu_custom_call" | custom-call | tf_op jit(solution)/shard_map/pallas_call | solution.py:876
  255.9 16.4 %all-gather.9.cloned.1.call-done.w_in = bf16[2048,2048]{1,0:T(8,128)(2,1)} async-done(((bf16[512,2048]{1,0:T(8,128)(2,1)}), bf16[2048,2048]{1,0:T(8,128)(2,1)}) %all-gather.9.cloned.1.call-update) | async-done | bytes 8388624 | tf_op jit(solution)/shard_map/all_gather | solution.py:1274
  272.4 134.5 %shard_map.375 = (bf16[8,192,2048]{2,1,0:T(8,128)(2,1)}, bf16[4,384,1024]{2,1,0:T(8,128)(2,1)}, bf16[4,384,2048]{2,1,0:T(8,128)(2,1)}, bf16[4,384,2048]{2,1,0:T(...) custom-call(f32[48]{0:T(128)} %reshape.174.hyper, ...), custom_call_target="tpu_custom_call" | custom-call | tf_op jit(solution)/shard_map/pallas_call | solution.py:1108
  406.9 11.3 %convolution_convert_fusion.3.rest_1_ = bf16[1024,2048]{1,0:T(8,128)(2,1)} fusion(bf16[1536,1024]{1,0:T(8,128)(2,1)} %bitcast.114, bf16[1536,2048]{1,0:T(8,128)(2,1)} %bitcast.99), kind=kOutput, calls=%fused_computation.10 | convolution fusion | flops 6444548096 | bytes 13631488 | tf_op jit(solution)/shard_map/tu,td->ud/dot_general | solution.py:1386
  418.3 15.9 %convolution_convert_fusion.2.rest_0_ = bf16[2048,2048]{1,0:T(8,128)(2,1)} fusion(bf16[1536,2048]{1,0:T(8,128)(2,1)S(1)} %bitcast.112, bf16[1536,2048]{1,0:T(8,128)(2,1)S(1)} %bitcast.113), kind=kOutput, calls=%fused_computation.3 | convolution fusion | flops 12889096192 | bytes 20971520 | tf_op jit(solution)/shard_map/td,tu->du/dot_general | solution.py:1385
  434.2 109.1 %shard_map.376 = (bf16[8,192,2048]{2,1,0:T(8,128)(2,1)}, bf16[192,2048]{1,0:T(8,128)(2,1)}, f32[512,2048]{1,0:T(8,128)}, f32[512,1024]{1,0:T(8,128)}, f32[192,2048]{1,0:T(8,128)}) custom-call(bf16[8,192,2048]{2,1,0:T(8,128)(2,1)} %bitcast.100, bf16[192,2048]{1,0:T(8,128)(2,1)} %get-tuple-element.75.gathered, ...), custom_call_target="tpu_custom_call" | custom-call | tf_op jit(solution)/shard_map/pallas_call | solution.py:876
  543.3 5.7 convolution_convert_fusion.5.rest_1_
  554.8 13.2 %shard_map.377 = (bf16[1536,256]{1,0:T(8,128)(2,1)S(1)}, bf16[1536,256]{1,0:T(8,128)(2,1)S(1)}, bf16[1536,256]{1,0:T(8,128)(2,1)S(1)}) custom-call(bf16[1536,256]{1,0:T(8,128)(2,1)S(1)} %convolution_convert_fusion.6.grad, bf16[1536,256]{1,0:T(8,128)(2,1)S(1)} %copy-done.5, bf16[1536,256]{1,0:T(8,128)(2,1)S(1)} %copy-done.7, bf16[1536,256]{1,0:T(8,128)(2,1)S(1)} %copy-done.9, ...), custom_call_target="tpu_custom_call" | custom-call | tf_op jit(solution)/shard_map/pallas_call | solution.py:301
  568.2 6.7 convolution_convert_fusion.4.rest_0_
  574.9 7.0 convolution_convert_fusion
  581.9 76.1 %shard_map.378 = (bf16[2,2,96,1024]{3,2,1,0:T(8,128)(2,1)}, bf16[2,2,96,1024]{3,2,1,0:T(8,128)(2,1)}, bf16[2,2,96,1024]{3,2,1,0:T(8,128)(2,1)}, bf16[2,2,96,1024...) custom-call(bf16[8,192,2048]{2,1,0:T(8,128)(2,1)} %bitcast.97, f32[192,2048]{1,0:T(8,128)} %get-tuple-element.87.h, ...), custom_call_target="tpu_custom_call" | custom-call | tf_op jit(solution)/shard_map/pallas_call | solution.py:1188
  662.5 13.5 %shard_map.379 = (f32[2,4,192,1024]{3,2,1,0:T(8,128)}, f32[2,4,192,1024]{3,2,1,0:T(8,128)}, f32[17,8,256]{2,1,0:T(8,128)}) custom-call(f32[48]{0:T(128)} %reshape.174.hyper, f32[2,4,192,1024]{3,2,1,0:T(8,128)} %streams.3, f32[2,4,192,1024]{3,2,1,0:T(8,128)} %cotangent.3, s32[2,192,1]{2,1,0:T(8,128)} %copy.65.sent, ...), custom_call_target="tpu_custom_call" | custom-call | tf_op jit(solution)/shard_map/pallas_call | solution.py:194
  677.1 6.0 multiply_reduce_fusion
  688.4 19.3 %shard_map.380 = f32[1,128]{1,0:T(1,128)} custom-call(f32[1,128]{1,0:T(1,128)} %fusion.8.own), custom_call_target="tpu_custom_call" | custom-call | tf_op jit(solution)/shard_map/pallas_call | solution.py:1252
  714.0 7.0 multiply_subtract_fusion.1
  721.1 3.5 multiply_subtract_fusion.3
  725.3 6.0 multiply_subtract_fusion
  731.3 3.0 multiply_subtract_fusion.2
  (144 shorter events, 41.7 us)
Async XLA Ops:
  7.2 12.0 %copy-start = (s32[2,1,1536]{2,1,0:T(1,128)S(1)}, s32[2,1,1536]{2,1,0:T(1,128)}, u32[]{:S(2)}) copy-start(s32[2,1,1536]{2,1,0:T(1,128)} %param.23) | copy-start | bytes 36868
  7.2 125.0 %all-gather.7.cloned.1.call-start = ((), (), s32[]{:S(2)}) async-start(), calls=%async_computation.1 | async-start | bytes 1310720 | tf_op jit(solution)/shard_map/all_gather | solution.py:1274
  9.1 126.7 %all-gather.5.cloned.1.call-start = ((), (), s32[]{:S(2)}) async-start(), calls=%async_computation | async-start | bytes 3932160 | tf_op jit(solution)/shard_map/all_gather | solution.py:1274
  11.6 244.3 %all-gather.11.cloned.1.call-start = ((), (), s32[]{:S(2)}) async-start(), calls=%async_computation.3 | async-start | bytes 5242880 | tf_op jit(solution)/shard_map/all_gather | solution.py:1274
  13.6 258.7 %all-gather.9.cloned.1.call-start = ((), (), s32[]{:S(2)}) async-start(), calls=%async_computation.2 | async-start | bytes 10485760 | tf_op jit(solution)/shard_map/all_gather | solution.py:1274
  144.6 10.4 %copy-start.20 = (bf16[32,8,2,1024]{3,1,2,0:T(8,128)(2,1)S(1)}, bf16[32,8,2,1024]{3,1,2,0:T(8,128)(2,1)}, u32[]{:S(2)}) copy-start(bf16[32,8,2,1024]{3,1,2,0:T(8,128)(2,1)} %copy.74) | copy-start | bytes 3145732
  406.9 11.3 %copy-start.34 = (bf16[8,192,2048]{2,1,0:T(8,128)(2,1)S(1)}, bf16[8,192,2048]{2,1,0:T(8,128)(2,1)}, u32[]{:S(2)}) copy-start(bf16[8,192,2048]{2,1,0:T(8,128)(2,1)} %get-tuple-element.76) | copy-start | bytes 18874372
  406.9 11.3 %copy-start.35 = (bf16[4,384,2048]{2,1,0:T(8,128)(2,1)S(1)}, bf16[4,384,2048]{2,1,0:T(8,128)(2,1)}, u32[]{:S(2)}) copy-start(bf16[4,384,2048]{2,1,0:T(8,128)(2,1)} %get-tuple-element.77) | copy-start | bytes 18874372
  551.2 16.9 %slice-start = ((s8[6291456]{0:T(1024)(128)(4,1)}), s8[4194304]{0:T(1024)(128)(4,1)S(1)}, s32[]{:S(2)}) async-start(s8[6291456]{0:T(1024)(128)(4,1)} %bitcast.109), calls=%async_computation.4 | async-start | bytes 8388608
  554.8 13.4 %slice-start.1 = ((s8[6291456]{0:T(1024)(128)(4,1)}), s8[2097152]{0:T(1024)(128)(4,1)S(1)}, s32[]{:S(2)}) async-start(s8[6291456]{0:T(1024)(128)(4,1)} %bitcast.109), calls=%async_computation.5 | async-start | bytes 4194304
  568.1 6.7 copy-start.36
  677.1 6.0 copy-start.24
  677.1 6.0 copy-start.25
  677.1 6.0 copy-start.26
  683.2 37.9 %copy-start.23 = (f32[128,1024]{1,0:T(8,128)S(1)}, f32[128,1024]{1,0:T(8,128)}, u32[]{:S(2)}) copy-start(f32[128,1024]{1,0:T(8,128)} %param.26) | copy-start | bytes 1572868
  712.6 12.0 %copy-start.30 = (f32[2,4,6]{2,1,0:T(4,128)}, f32[2,4,6]{2,1,0:T(4,128)S(1)}, u32[]{:S(2)}) copy-start(f32[2,4,6]{2,1,0:T(4,128)S(1)} %get-tuple-element.187) | copy-start | bytes 580
  714.0 11.2 %copy-start.12 = (f32[2,512,1024]{2,1,0:T(8,128)S(1)}, f32[2,512,1024]{2,1,0:T(8,128)}, u32[]{:S(2)}) copy-start(f32[2,512,1024]{2,1,0:T(8,128)} %param.25) | copy-start | bytes 12582916
  714.0 11.2 %copy-start.13 = (f32[2,512,1024]{2,1,0:T(8,128)S(1)}, f32[2,512,1024]{2,1,0:T(8,128)}, u32[]{:S(2)}) copy-start(f32[2,512,1024]{2,1,0:T(8,128)} %get-tuple-element.184) | copy-start | bytes 12582916
  714.0 11.2 %copy-start.18 = (f32[2,512,1024]{2,1,0:T(8,128)S(1)}, f32[2,512,1024]{2,1,0:T(8,128)}, u32[]{:S(2)}) copy-start(f32[2,512,1024]{2,1,0:T(8,128)} %param.33) | copy-start | bytes 12582916
  714.0 11.2 %copy-start.19 = (f32[2,512,1024]{2,1,0:T(8,128)S(1)}, f32[2,512,1024]{2,1,0:T(8,128)}, u32[]{:S(2)}) copy-start(f32[2,512,1024]{2,1,0:T(8,128)} %param.29) | copy-start | bytes 12582916
  725.3 6.0 copy-start.15
  725.3 6.0 copy-start.16
  725.3 6.0 copy-start.27
  725.3 6.0 copy-start.28
  (19 other events, 65.0 us)
Sparse Core Ops, SparseCore 0:
  10.5 29.3 all-gather.6
  42.2 82.6 all-gather.4
  127.3 55.0 all-gather.10
  184.7 87.5 all-gather.8

commit v4 on v3

--- a/solution.py
+++ b/solution.py
@@ -27,7 +27,7 @@
 ANY = pl.BlockSpec(memory_space=pl.ANY)
 VMEM = pl.BlockSpec(memory_space=pltpu.VMEM)
 SMEM = pl.BlockSpec(memory_space=pltpu.SMEM)
-ROOM = 60 * 2**20
+ROOM = 63 * 2**20
 
 
 def rotary_tables(segment):
@@ -225,89 +225,45 @@
     return (column >= start_ref[pl.ds(base, block)]) & (column <= row)
 
 
-def attend_forward_kernel(
-    block, q_in, k_in, v_in, cosine, sine, start, out, log_out, q_out, k_out, v_out
-):
-    length = q_in.shape[0]
-    q_out[...] = turn(q_in[...], cosine[...], sine[...]).astype(jnp.bfloat16)
-    k_out[...] = turn(k_in[...], cosine[...], sine[...]).astype(jnp.bfloat16)
-    v_out[...] = v_in[...].astype(jnp.bfloat16)
+def attend_head(head, q, k, v, start, out, log_out):
+    length = q.shape[0]
+    block = min(256, length)
+    at = pl.ds(head * HEAD, HEAD)
     for base in range(0, length, block):
         keys = base + block
-        scores = dot_last(q_out[pl.ds(base, block)], k_out[pl.ds(0, keys)]) * HEAD ** (-0.5)
+        rows, span = pl.ds(base, block), pl.ds(0, keys)
+        scores = dot_last(q[rows, at], k[span, at]) * HEAD ** (-0.5)
         scores = jnp.where(allowed_pairs(start, base, block, keys), scores, -1e30)
         largest = jnp.max(scores, axis=1, keepdims=True)
         weights = jnp.exp(scores - largest)
         totals = jnp.sum(weights, axis=1, keepdims=True)
-        probs = (weights * (1.0 / totals)).astype(jnp.bfloat16)
-        out[pl.ds(base, block)] = jnp.dot(
-            probs, v_out[pl.ds(0, keys)], preferred_element_type=jnp.float32
-        ).astype(jnp.bfloat16)
-        log_out[0, pl.ds(base, block)] = largest + jnp.log(totals)
-
-
-def attend_backward_kernel(
-    block, grad, q, k, v, log_in, cosine, sine, start, q_out, k_out, v_out, k_sum, v_sum
-):
-    length = q.shape[0]
+        probs = (weights * (1.0 / totals)).astype(LOW)
+        out[rows, at] = jnp.dot(probs, v[span, at], preferred_element_type=FULL).astype(LOW)
+        log_out[rows, pl.ds(head, 1)] = largest + jnp.log(totals)
+
+
+def attend_head_back(head, grad, q, k, v, log_in, cosine, sine, start, units, k_sum, v_sum):
+    length, width = q.shape
+    block = min(256, length)
+    at = pl.ds(head * HEAD, HEAD)
     k_sum[...] = jnp.zeros_like(k_sum)
     v_sum[...] = jnp.zeros_like(v_sum)
     for base in range(0, length, block):
         keys = base + block
         rows, span = pl.ds(base, block), pl.ds(0, keys)
-        scores = dot_last(q[rows], k[span]) * HEAD ** (-0.5)
+        scores = dot_last(q[rows, at], k[span, at]) * HEAD ** (-0.5)
         probs = jnp.where(
-            allowed_pairs(start, base, block, keys), jnp.exp(scores - log_in[0, rows]), 0.0
-        )
-        grad_probs = dot_last(grad[rows], v[span])
+            allowed_pairs(start, base, block, keys), jnp.exp(scores - log_in[rows, pl.ds(head, 1)]), 0.0
+        )
+        grad_probs = dot_last(grad[rows, at], v[span, at])
         inner = jnp.sum(probs * grad_probs, axis=1, keepdims=True)
-        grad_scores = (probs * (grad_probs - inner) * HEAD ** (-0.5)).astype(jnp.bfloat16)
-        grad_query = jnp.dot(grad_scores, k[span], preferred_element_type=jnp.float32)
-        q_out[rows] = turn(grad_query, cosine[rows], -sine[rows]).astype(jnp.bfloat16)
-        k_sum[span] += dot_first(grad_scores, q[rows])
-        v_sum[span] += dot_first(probs.astype(jnp.bfloat16), grad[rows])
-    k_out[...] = turn(k_sum[...], cosine[...], -sine[...]).astype(jnp.bfloat16)
-    v_out[...] = v_sum[...].astype(jnp.bfloat16)
-
-
-def attend_forward(qkv, cosine, sine, start):
-    length, width = qkv.shape
-    heads = width // (3 * HEAD)
-    block = min(256, length)
-
-    def part(offset):
-        return pl.BlockSpec((length, HEAD), lambda h: (0, offset + h))
-
-    whole = pl.BlockSpec((length, HEAD), lambda h: (0, 0))
-    low = jax.ShapeDtypeStruct((length, heads * HEAD), jnp.bfloat16)
-    return pl.pallas_call(
-        functools.partial(attend_forward_kernel, block),
-        grid=(heads,),
-        in_specs=[part(0), part(heads), part(2 * heads), whole, whole,
-                  pl.BlockSpec((length, 1), lambda h: (0, 0))],
-        out_specs=[part(0), pl.BlockSpec((1, length, 1), lambda h: (h, 0, 0)), part(0), part(0), part(0)],
-        out_shape=[low, jax.ShapeDtypeStruct((heads, length, 1), jnp.float32), low, low, low],
-        compiler_params=pltpu.CompilerParams(vmem_limit_bytes=40 * 2**20),
-    )(qkv, qkv, qkv, cosine, sine, start)
-
-
-def attend_backward(grad, q, k, v, log_totals, cosine, sine, start):
-    length, width = q.shape
-    heads = width // HEAD
-    block = min(256, length)
-    part = pl.BlockSpec((length, HEAD), lambda h: (0, h))
-    whole = pl.BlockSpec((length, HEAD), lambda h: (0, 0))
-    low = jax.ShapeDtypeStruct((length, width), jnp.bfloat16)
-    return pl.pallas_call(
-        functools.partial(attend_backward_kernel, block),
-        grid=(heads,),
-        in_specs=[part, part, part, part, pl.BlockSpec((1, length, 1), lambda h: (h, 0, 0)), whole, whole,
-                  pl.BlockSpec((length, 1), lambda h: (0, 0))],
-        out_specs=[part, part, part],
-        out_shape=[low, low, low],
-        scratch_shapes=[pltpu.VMEM((length, HEAD), jnp.float32)] * 2,
-        compiler_params=pltpu.CompilerParams(vmem_limit_bytes=40 * 2**20),
-    )(grad, q, k, v, log_totals, cosine, sine, start)
+        grad_scores = (probs * (grad_probs - inner) * HEAD ** (-0.5)).astype(LOW)
+        grad_query = jnp.dot(grad_scores, k[span, at], preferred_element_type=FULL)
+        units[rows, at] = turn(grad_query, cosine[rows], -sine[rows]).astype(LOW)
+        k_sum[span] += dot_first(grad_scores, q[rows, at])
+        v_sum[span] += dot_first(probs.astype(LOW), grad[rows, at])
+    units[:, pl.ds(width + head * HEAD, HEAD)] = turn(k_sum[...], cosine[...], -sine[...]).astype(LOW)
+    units[:, pl.ds(2 * width + head * HEAD, HEAD)] = v_sum[...].astype(LOW)
 
 
 def remote(source, target, send_sem, recv_sem, device):
@@ -545,10 +501,20 @@
     return [DMA((pairs, cuts))] * 5 + [DMA]
 
 
+def inner_order(pairs, cuts, inner):
+    near = [(True, dest, cut) for dest in range(pairs - 1, inner, -1) for cut in range(cuts)]
+    far = [(False, dest, cut) for dest in range(inner) for cut in range(cuts)]
+    hops = pairs - 1 - 2 * inner
+    timed = [(index, 0) + one for index, one in enumerate(near)]
+    timed += [(index + hops, 1) + one for index, one in enumerate(far)]
+    return [one[2:] for one in sorted(timed, key=lambda one: one[:2])]
+
+
 class Scatter:
     def __init__(self, pairs, cuts, part, buffers, sems):
         self.pairs, self.cuts, self.part = pairs, cuts, part
-        self.own, self.twin, self.from_left, self.from_right, self.out_right, self.out_left = buffers
+        self.twin, self.from_left, self.from_right = buffers[:3]
+        self.own = buffers[3] if len(buffers) > 3 else None
         (
             self.right_send,
             self.left_send,
@@ -559,27 +525,27 @@
             self.loaded,
         ) = sems
         self.height = part.shape[1] // cuts
-        self.ready = set()
-
-    def piece(self, ref, dest, cut):
-        return ref.at[dest, pl.ds(cut * self.height, self.height)]
-
-    def value(self, ref, dest, cut):
-        return ref[dest, pl.ds(cut * self.height, self.height)].astype(FULL)
+
+    def span(self, cut):
+        return pl.ds(cut * self.height, self.height)
+
+    def mine(self, dest, cut):
+        _, _, side = line_place()
+        if self.own is None:
+            return self.part.at[dest * 2 + side, self.span(cut)]
+        return self.own.at[dest, self.span(cut)]
 
     def load(self, dest, cut):
         _, _, side = line_place()
         return pltpu.make_async_copy(
-            self.piece(self.part, dest * 2 + side, cut),
-            self.piece(self.own, dest, cut),
-            self.loaded.at[dest, cut],
+            self.part.at[dest * 2 + side, self.span(cut)], self.mine(dest, cut), self.loaded.at[dest, cut]
         )
 
     def to_twin(self, dest, cut):
         me, _, side = line_place()
         return remote(
-            self.piece(self.part, dest * 2 + 1 - side, cut),
-            self.piece(self.twin, dest, cut),
+            self.part.at[dest * 2 + 1 - side, self.span(cut)],
+            self.twin.at[dest, self.span(cut)],
             self.twin_send.at[dest, cut],
             self.twin_recv.at[dest, cut],
             {"row": me + 1 - 2 * side},
@@ -587,8 +553,8 @@
 
     def to_right(self, dest, cut):
         return remote(
-            self.piece(self.out_right, dest, cut),
-            self.piece(self.from_left, dest, cut),
+            self.mine(dest, cut),
+            self.from_left.at[dest, self.span(cut)],
             self.right_send.at[dest, cut],
             self.right_recv.at[dest, cut],
             {"row": line_place()[0] + 2},
@@ -596,8 +562,8 @@
 
     def to_left(self, dest, cut):
         return remote(
-            self.piece(self.out_left, dest, cut),
-            self.piece(self.from_right, dest, cut),
+            self.mine(dest, cut),
+            self.from_right.at[dest, self.span(cut)],
             self.left_send.at[dest, cut],
             self.left_recv.at[dest, cut],
             {"row": line_place()[0] - 2},
@@ -612,51 +578,81 @@
         for dest in order:
             for cut in range(self.cuts):
                 self.to_twin(dest, cut).start()
-                self.load(dest, cut).start()
+                if self.own is not None:
+                    self.load(dest, cut).start()
 
     def here(self, dest, cut):
-        return self.value(self.own, dest, cut) + self.value(self.twin, dest, cut)
-
-    def step(self, step, cut):
+        return self.mine(dest, cut)[...].astype(FULL) + self.twin[dest, self.span(cut)].astype(FULL)
+
+    def flows(self, step, place):
+        last = self.pairs - 1
+        return (
+            (last - step, place < last - step, place == 0, self.from_left, self.to_right),
+            (step, place > step, place == last, self.from_right, self.to_left),
+        )
+
+    def begin(self):
+        _, place, _ = line_place()
+        ready = []
+        for step in range(self.pairs - 1):
+            for dest, sending, first, _, copy in self.flows(step, place):
+                for cut in range(self.cuts):
+                    if (dest, cut) not in ready:
+                        ready.append((dest, cut))
+                        self.to_twin(dest, cut).wait_recv()
+                        if self.own is not None:
+                            self.load(dest, cut).wait()
+
+                    @pl.when(sending & first)
+                    def _():
+                        self.mine(dest, cut)[...] = self.here(dest, cut).astype(LOW)
+                        copy(dest, cut).start()
+
+    def pass_on(self, dest, cut, rightward):
+        copy, arrived = (self.to_right, self.from_left) if rightward else (self.to_left, self.from_right)
+        copy(dest, cut).wait_recv()
+        self.mine(dest, cut)[...] = (
+            self.here(dest, cut) + arrived[dest, self.span(cut)].astype(FULL)
+        ).astype(LOW)
+        copy(dest, cut).start()
+
+    def poll(self, index):
         _, place, _ = line_place()
         last = self.pairs - 1
-        span = pl.ds(cut * self.height, self.height)
-        for dest, sending, first, out, arrived, copy in (
-            (last - step, place < last - step, place == 0, self.out_right, self.from_left, self.to_right),
-            (step, place > step, place == last, self.out_left, self.from_right, self.to_left),
-        ):
-            if (dest, cut) not in self.ready:
-                self.ready.add((dest, cut))
-                self.to_twin(dest, cut).wait_recv()
-                self.load(dest, cut).wait()
-
-            @pl.when(sending & first)
-            def _():
-                out[dest, span] = self.here(dest, cut).astype(out.dtype)
-                copy(dest, cut).start()
-
-            @pl.when(sending & jnp.logical_not(first))
-            def _():
-                copy(dest, cut).wait_recv()
-                out[dest, span] = (self.here(dest, cut) + self.value(arrived, dest, cut)).astype(out.dtype)
-                copy(dest, cut).start()
+        for inner in range(1, self.pairs // 2):
+            order = inner_order(self.pairs, self.cuts, inner)
+            if index < len(order):
+                near, dest, cut = order[index]
+
+                @pl.when(place == inner)
+                def _():
+                    self.pass_on(dest, cut, near)
+
+                @pl.when(place == last - inner)
+                def _():
+                    self.pass_on(last - dest, cut, not near)
+
+    def polls(self):
+        return max(
+            len(inner_order(self.pairs, self.cuts, inner)) for inner in range(1, self.pairs // 2)
+        )
 
     def finish(self, total):
         _, place, _ = line_place()
         last = self.pairs - 1
         for cut in range(self.cuts):
-            span = pl.ds(cut * self.height, self.height)
+            span = self.span(cut)
             total[span] = self.here(place, cut)
 
             @pl.when(place > 0)
             def _():
                 self.to_right(place, cut).wait_recv()
-                total[span] += self.value(self.from_left, place, cut)
+                total[span] += self.from_left[place, span].astype(FULL)
 
             @pl.when(place < last)
             def _():
                 self.to_left(place, cut).wait_recv()
-                total[span] += self.value(self.from_right, place, cut)
+                total[span] += self.from_right[place, span].astype(FULL)
 
         for dest in range(self.pairs):
             for cut in range(self.cuts):
@@ -671,8 +667,8 @@
                     self.to_left(dest, cut).wait_send()
 
 
-def scatter_buffers(pairs, rows, width):
-    return [pltpu.VMEM((pairs, rows, width), LOW)] * 6
+def scatter_buffers(pairs, rows, width, loaded=True):
+    return [pltpu.VMEM((pairs, rows, width), LOW)] * (4 if loaded else 3)
 
 
 def scatter_sems(pairs, cuts):
@@ -680,11 +676,11 @@
 
 
 class PlaneScatter:
-    def __init__(self, block_of, out, buffers, sems):
-        self.block_of, self.out = block_of, out
+    def __init__(self, block_of, out, square, buffers, sems):
+        self.block_of, self.out, self.square = block_of, out, square
         self.arrived, self.mine, self.onward, self.final = buffers
         self.send, self.recv, self.loaded, self.send_on, self.recv_on = sems
-        self.height = out.shape[0] // 2
+        self.height = out.shape[-2] // 2
 
     def places(self, half, index):
         d, c = lax.axis_index("dp"), lax.axis_index("col")
@@ -716,12 +712,18 @@
         for index in range(2):
             for half in range(2):
                 self.move(half, index).start()
-                self.load(half, index).start()
+                if self.mine is not None:
+                    self.load(half, index).start()
 
     def sum_of(self, half, index):
         self.move(half, index).wait_recv()
-        self.load(half, index).wait()
-        return self.mine[half, index].astype(FULL) + self.arrived[half, index].astype(FULL)
+        if self.mine is None:
+            _, _, block = self.places(half, index)
+            mine = block[...]
+        else:
+            self.load(half, index).wait()
+            mine = self.mine[half, index]
+        return mine.astype(FULL) + self.arrived[half, index].astype(FULL)
 
     def forward(self):
         for half in range(2):
@@ -732,16 +734,87 @@
         for half in range(2):
             total = self.sum_of(half, 1)
             self.move_on(half).wait_recv()
-            self.out[pl.ds(half * self.height, self.height)] = total + self.final[half].astype(FULL)
+            total = total + self.final[half].astype(FULL)
+            width = self.out.shape[-1]
+            for index in range(self.out.shape[0]):
+                self.out[index, pl.ds(half * self.height, self.height)] = total[
+                    :, index * width : (index + 1) * width
+                ]
+            self.square[half] = fold(total * total)
         for half in range(2):
             for index in range(2):
                 self.move(half, index).wait_send()
             self.move_on(half).wait_send()
 
 
+class PlaneGather:
+    def __init__(self, own, block_of, sems):
+        self.own, self.block_of = own, block_of
+        self.send, self.recv, self.send_on, self.recv_on, self.keep = sems
+        self.height = own.shape[0] // 2
+
+    def direct(self, axis, half):
+        d, c = lax.axis_index("dp"), lax.axis_index("col")
+        return remote(
+            self.own.at[pl.ds(half * self.height, self.height)],
+            self.block_of(c, d, half),
+            self.send.at[axis, half],
+            self.recv.at[axis, half],
+            {"dp": 1 - d} if axis == 0 else {"col": 1 - c},
+        )
+
+    def onward(self, half):
+        d, c = lax.axis_index("dp"), lax.axis_index("col")
+        block = self.block_of(c, 1 - d, 0) if half == 0 else self.block_of(1 - c, d, 1)
+        return remote(
+            block,
+            block,
+            self.send_on.at[half],
+            self.recv_on.at[half],
+            {"col": 1 - c} if half == 0 else {"dp": 1 - d},
+        )
+
+    def stay(self, half):
+        d, c = lax.axis_index("dp"), lax.axis_index("col")
+        return pltpu.make_async_copy(
+            self.own.at[pl.ds(half * self.height, self.height)], self.block_of(c, d, half), self.keep.at[half]
+        )
+
+    def start(self):
+        for swap in range(2):
+            for half in range(2):
+                self.direct(half ^ swap, half).start()
+        for half in range(2):
+            self.stay(half).start()
+
+    def forward(self):
+        for half in range(2):
+            self.direct(half, half).wait_recv()
+            self.onward(half).start()
+
+    def finish(self):
+        for half in range(2):
+            self.direct(1 - half, half).wait_recv()
+            self.onward(half).wait_recv()
+            self.stay(half).wait()
+        for half in range(2):
+            for axis in range(2):
+                self.direct(axis, half).wait_send()
+            self.onward(half).wait_send()
+
+
+def plane_gather_sems():
+    return [DMA((2, 2)), DMA((2, 2)), DMA((2,)), DMA((2,)), DMA((2,))]
+
+
 def by_rows(part, height):
     half_height = height // 2
     return lambda c, d, half: part.at[pl.ds((c * 2 + d) * height + half * half_height, half_height)]
+
+
+def by_owner(part, height):
+    half_height = height // 2
+    return lambda c, d, half: part.at[c, d, pl.ds(half * half_height, half_height)]
 
 
 def by_tiles(part, height, width):
@@ -751,22 +824,8 @@
     ]
 
 
-def plane_scratch(rows, width):
-    half = (rows // 2, width)
-    return [
-        pltpu.VMEM((2, 2) + half, LOW),
-        pltpu.VMEM((2, 2) + half, LOW),
-        pltpu.VMEM((2,) + half, LOW),
-        pltpu.VMEM((2,) + half, LOW),
-        DMA((2, 2)),
-        DMA((2, 2)),
-        DMA((2, 2)),
-        DMA((2,)),
-        DMA((2,)),
-    ]
-
-
 CUTS = 2
+SUM_CUTS = 4
 
 
 def call_remote(kernel, collective, **options):
@@ -779,114 +838,318 @@
     )
 
 
-def enter_kernel(plane, pairs, h_home, mix_home, back_home, gy_home, rows_out, h, mix, back, gy, own, *sems):
-    plane_sems, line_sems = sems[:3], sems[3:]
+def block_view(whole, rows, width):
+    return by_rows(whole, rows) if whole.shape[1] == width else by_tiles(whole, rows, width)
+
+
+def plane_gathers(weights, wholes, sems):
+    return [
+        PlaneGather(weight, block_view(whole, *weight.shape), sems[5 * index : 5 * index + 5])
+        for index, (weight, whole) in enumerate(zip(weights, wholes))
+    ]
+
+
+def whole_shapes(weights):
+    return [
+        jax.ShapeDtypeStruct((4 * rows, width) if width != D // 2 else (2 * rows, 2 * width), LOW)
+        for rows, width in (weight.shape for weight in weights)
+    ]
+
+
+def enter_kernel(plane, pairs, count, h_home, gy_home, *rest):
+    weights, rest = rest[:count], rest[count:]
+    (rows_out, h, gy), rest = rest[:3], rest[3:]
+    wholes, rest = rest[:count], rest[count:]
+    own, plane_sems, line_sems, rest = rest[0], rest[1:4], rest[4:10], rest[10:]
+    gathers = plane_gathers(weights, wholes, rest)
     greet(pairs, plane)
     first = to_work(plane, h_home, h, plane_sems, 0)
-    others = [
-        to_work(plane, home, work, plane_sems, index)
-        for index, (home, work) in enumerate(((mix_home, mix), (back_home, back), (gy_home, gy)), 1)
-    ]
+    second = to_work(plane, gy_home, gy, plane_sems, 1)
     first.start()
     first.arrive()
-    for other in others:
-        other.start()
+    for one in gathers:
+        one.start()
     own[...] = norm_forward(h[...])[0].astype(LOW)
     gather = Gather(pairs, CUTS, own, rows_out, line_sems)
     gather.start()
     for step in range(1, pairs):
         for cut in range(CUTS):
             gather.step(step, cut)
+        if step == 1:
+            second.start()
+        if step == 2:
+            for one in gathers:
+                one.forward()
     gather.finish()
-    for other in others:
-        other.arrive()
-        other.leave()
+    for one in gathers:
+        one.finish()
+    second.arrive()
+    second.leave()
     first.leave()
 
 
-def enter(plane, pairs, h_home, mix_home, back_home, gy_home, collective):
+def enter(plane, pairs, h_home, gy_home, weights, collective):
     n_dp, n_col, slot, width = h_home.shape
     rows = n_dp * slot
     work = jax.ShapeDtypeStruct((rows, n_col * width), FULL)
     outs = call_remote(
-        functools.partial(enter_kernel, plane, pairs),
+        functools.partial(enter_kernel, plane, pairs, len(weights)),
         collective,
-        in_specs=[ANY] * 4,
-        out_specs=[ANY, VMEM, ANY, ANY, ANY],
+        in_specs=[ANY] * (2 + len(weights)),
+        out_specs=[ANY, VMEM, ANY] + [ANY] * len(weights),
         out_shape=[
             jax.ShapeDtypeStruct((2 * pairs, rows, n_col * width), LOW),
             work,
-            work,
-            work,
             jax.ShapeDtypeStruct(work.shape, gy_home.dtype),
-        ],
-        scratch_shapes=[pltpu.VMEM(work.shape, LOW)] + exchange_sems(plane, 4) + gather_sems(pairs, CUTS),
-    )(h_home, mix_home, back_home, gy_home)
-    return [outs[0].reshape(2 * pairs * rows, n_col * width)] + list(outs[1:])
-
-
-def duplex_kernel(pairs, plane, count, part, gathered, *rest):
-    grads, rest = rest[:count], rest[count:]
-    (rows_out, low_out), rest = rest[:2], rest[2:]
-    sums, rest = rest[:count], rest[count:]
-    total, scratch, rest = rest[0], rest[1:], rest[20:]
-    scatter = Scatter(pairs, CUTS, part, scratch[:6], scratch[6:13])
-    gather = Gather(pairs, CUTS, gathered, rows_out, scratch[13:19])
-    planes = plane_sums(grads, sums, rest)
-    greet(pairs, plane if count else None)
+        ]
+        + whole_shapes(weights),
+        scratch_shapes=[pltpu.VMEM(work.shape, LOW)]
+        + exchange_sems(plane, 2)
+        + gather_sems(pairs, CUTS)
+        + plane_gather_sems() * len(weights),
+    )(h_home, gy_home, *weights)
+    return outs[0].reshape(2 * pairs * rows, n_col * width), outs[1], outs[2], outs[3:]
+
+
+def attend_kernel(
+    plane, pairs, count, x_in, w_in, w_out, cosine, sine, start, gathered, mix_home,
+    *rest,
+):
+    weights, rest = rest[:count], rest[count:]
+    (rows_out, mix, heads_out, log_out, q, k, v, low_out, total), rest = rest[:9], rest[9:]
+    wholes, rest = rest[:count], rest[count:]
+    (x, part, load_sem), plane_sems, scratch, line_sems = rest[:3], rest[3:6], rest[6:16], rest[16:22]
+    scatter = Scatter(pairs, SUM_CUTS, part, scratch[:3], scratch[3:])
+    gather = Gather(pairs, CUTS, gathered, rows_out, line_sems)
+    gathers = plane_gathers(weights, wholes, rest[22:])
+    load = pltpu.make_async_copy(x_in, x, load_sem)
+    load.start()
+    greet(pairs, plane)
+    gather.start()
+    exchange = to_work(plane, mix_home, mix, plane_sems, 0)
+    for one in gathers:
+        one.start()
+    exchange.start()
+    load.wait()
+    width = q.shape[1]
+    heads = width // HEAD
+    for index, out in enumerate((q, k, v)):
+        value = jnp.dot(x[...], w_in[:, index * width : (index + 1) * width], preferred_element_type=FULL)
+        for head in range(heads):
+            at = slice(head * HEAD, (head + 1) * HEAD)
+            one = value[:, at]
+            out[:, at] = (one if index == 2 else turn(one, cosine[...], sine[...])).astype(LOW)
+    for head in range(heads):
+        attend_head(head, q, k, v, start, heads_out, log_out)
+        if head == 0:
+            for cut in range(CUTS):
+                gather.step(1, cut)
+    rows = total.shape[0]
+    for owner in range(2 * pairs):
+        part[owner] = jnp.dot(
+            heads_out[pl.ds(owner * rows, rows)], w_out[...], preferred_element_type=FULL
+        ).astype(LOW)
     scatter.start()
-    gather.start()
-    for one in planes:
-        one.start()
-    for step in range(pairs - 1):
+    scatter.begin()
+    polls = list(range(scatter.polls()))
+    for step in range(2, pairs):
         for cut in range(CUTS):
-            scatter.step(step, cut)
-            gather.step(step + 1, cut)
-        if 0 < step <= len(planes):
-            planes[step - 1].forward()
+            gather.step(step, cut)
+            for index in polls[:2]:
+                scatter.poll(index)
+            polls = polls[2:]
+        if step == 2:
+            for one in gathers:
+                one.forward()
+    for index in polls:
+        scatter.poll(index)
     scatter.finish(total)
     low_out[...] = total[...].astype(LOW)
     gather.finish()
-    for one in planes:
+    for one in gathers:
         one.finish()
-
-
-def plane_sums(grads, sums, scratch):
-    planes = []
-    for index, (grad, total) in enumerate(zip(grads, sums)):
-        rows, width = total.shape
-        block_of = by_rows(grad, rows) if grad.shape[1] == width else by_tiles(grad, rows, width)
-        planes.append(
-            PlaneScatter(
-                block_of, total, scratch[9 * index : 9 * index + 4], scratch[9 * index + 4 : 9 * index + 9]
-            )
-        )
-    return planes
-
-
-def owned_shape(grad):
-    rows, width = grad.shape
-    return (rows // 4, width) if rows == D else (rows // 2, width // 2)
-
-
-def duplex(pairs, plane, partial, gathered, grads, collective):
+    exchange.arrive()
+    exchange.leave()
+
+
+def attend(plane, pairs, x, w_in, w_out, cosine, sine, start, gathered, mix_home, weights, collective):
+    tokens, width = x.shape
+    rows = tokens // (2 * pairs)
+    local = w_out.shape[0]
+    low = jax.ShapeDtypeStruct((tokens, local), LOW)
+    full = jax.ShapeDtypeStruct((rows, width), FULL)
+    outs = call_remote(
+        functools.partial(attend_kernel, plane, pairs, len(weights)),
+        collective,
+        in_specs=[ANY, VMEM, VMEM, VMEM, VMEM, VMEM, ANY, ANY] + [ANY] * len(weights),
+        out_specs=[ANY, ANY] + [VMEM] * 7 + [ANY] * len(weights),
+        out_shape=[
+            jax.ShapeDtypeStruct((2 * pairs, rows, width), LOW),
+            full,
+            low,
+            jax.ShapeDtypeStruct((tokens, local // HEAD), FULL),
+            low,
+            low,
+            low,
+            jax.ShapeDtypeStruct((rows, width), LOW),
+            full,
+        ]
+        + whole_shapes(weights),
+        scratch_shapes=[pltpu.VMEM(x.shape, LOW), pltpu.VMEM((2 * pairs, rows, width), LOW), DMA]
+        + exchange_sems(plane, 1)
+        + scatter_buffers(pairs, rows, width, False)
+        + scatter_sems(pairs, SUM_CUTS)
+        + gather_sems(pairs, CUTS)
+        + plane_gather_sems() * len(weights),
+    )(x, w_in, w_out, cosine, sine, start, gathered, mix_home, *weights)
+    return [outs[0].reshape(tokens, width)] + list(outs[1:9]), outs[9:]
+
+
+def back_kernel(
+    pairs, plane, gathered, part, x_in, units_in, hid_in, gy_in,
+    rows_out, low_out, out_grad, in_sum, square,
+    total, left, right, grad, arrived, onward, final, load_sem,
+    send, recv, loaded, send_on, recv_on, *rest,
+):
+    d, c = lax.axis_index("dp"), lax.axis_index("col")
+    scatter = Scatter(pairs, SUM_CUTS, part, rest[:4], rest[4:11])
+    gather = Gather(pairs, CUTS, gathered, rows_out, rest[11:])
+    height = in_sum.shape[1]
+    one = PlaneScatter(
+        by_rows(grad, height),
+        in_sum,
+        square,
+        (arrived, None, onward, final),
+        (send, recv, loaded, send_on, recv_on),
+    )
+    narrow = hid_in.shape[1]
+    loads = [
+        pltpu.make_async_copy(x_in, left, load_sem.at[0]),
+        pltpu.make_async_copy(units_in, right, load_sem.at[1]),
+        pltpu.make_async_copy(hid_in, left.at[:, pl.ds(0, narrow)], load_sem.at[2]),
+        pltpu.make_async_copy(gy_in, right, load_sem.at[3]),
+    ]
+    loads[0].start()
+    loads[1].start()
+    greet(pairs, plane)
+    gather.start()
+    scatter.start()
+
+    def in_block(there, across):
+        @pl.loop(0, height // UNIT)
+        def _(index):
+            at = pl.multiple_of((there * 2 + across) * height + index * UNIT, UNIT)
+            grad[pl.ds(at, UNIT)] = dot_first(left[:, pl.ds(at, UNIT)], right[...]).astype(LOW)
+
+    owned, width = out_grad.shape[2:]
+
+    def out_block(part):
+        @pl.loop(0, owned // UNIT)
+        def _(index):
+            at = pl.multiple_of(part * owned + index * UNIT, UNIT)
+            tile = dot_first(left[:, pl.ds(at, UNIT)], right[...]).astype(LOW)
+            for side in range(2):
+                out_grad[side, part, pl.ds(pl.multiple_of(index * UNIT, UNIT), UNIT)] = tile[
+                    :, side * width : (side + 1) * width
+                ]
+
+    each = -(-scatter.polls() // (CUTS * (pairs - 1)))
+
+    def both(step):
+        for cut in range(CUTS):
+            gather.step(step + 1, cut)
+            for index in range(each):
+                scatter.poll((step * CUTS + cut) * each + index)
+
+    scatter.begin()
+    loads[0].wait()
+    loads[1].wait()
+    in_block(1 - c, 1 - d)
+    one.move(0, 0).start()
+    one.move(1, 0).start()
+    in_block(c, 1 - d)
+    one.move(0, 1).start()
+    in_block(1 - c, d)
+    one.move(1, 1).start()
+    both(0)
+    in_block(c, d)
+    loads[2].start()
+    loads[3].start()
+    both(1)
+    loads[2].wait()
+    loads[3].wait()
+    out_block(0)
+    one.forward()
+    out_block(1)
+    for step in range(2, pairs - 1):
+        both(step)
+    scatter.finish(total)
+    low_out[...] = total[...].astype(LOW)
+    gather.finish()
+    one.finish()
+
+
+def back_gather(pairs, plane, gathered, partial, x, units, hid, gy, collective):
     rows, width = gathered.shape
+    wide, narrow = units.shape[1], hid.shape[1]
+    height = width // 4
+    half = (height // 2, wide)
     whole = jax.ShapeDtypeStruct((2 * pairs, rows, width), LOW)
-    owned = [owned_shape(grad) for grad in grads]
     outs = call_remote(
-        functools.partial(duplex_kernel, pairs, plane, len(grads)),
+        functools.partial(back_kernel, pairs, plane),
         collective,
-        in_specs=[ANY] * (2 + len(grads)),
-        out_specs=[ANY] + [VMEM] * (2 + len(grads)),
-        out_shape=[whole, jax.ShapeDtypeStruct((rows, width), LOW)]
-        + [jax.ShapeDtypeStruct(shape, FULL) for shape in owned]
-        + [jax.ShapeDtypeStruct((rows, width), FULL)],
-        scratch_shapes=scatter_buffers(pairs, rows, width)
-        + scatter_sems(pairs, CUTS)
-        + gather_sems(pairs, CUTS)
-        + sum([plane_scratch(*shape) for shape in owned], []),
-    )(partial.reshape(whole.shape), gathered, *grads)
-    return outs[0].reshape(2 * pairs * rows, width), outs[1], outs[-1], outs[2:-1]
+        in_specs=[ANY] * 6,
+        out_specs=[ANY, VMEM, VMEM, VMEM, VMEM],
+        out_shape=[
+            whole,
+            jax.ShapeDtypeStruct((rows, width), LOW),
+            jax.ShapeDtypeStruct((2, 2, narrow // 2, width // 2), LOW),
+            jax.ShapeDtypeStruct((2, height, wide // 2), FULL),
+            jax.ShapeDtypeStruct((2, 8, wide), FULL),
+        ],
+        scratch_shapes=[
+            pltpu.VMEM((rows, width), FULL),
+            pltpu.VMEM(x.shape, LOW),
+            pltpu.VMEM(units.shape, LOW),
+            pltpu.VMEM((width, wide), LOW),
+            pltpu.VMEM((2, 2) + half, LOW),
+            pltpu.VMEM((2,) + half, LOW),
+            pltpu.VMEM((2,) + half, LOW),
+            DMA((4,)),
+            DMA((2, 2)),
+            DMA((2, 2)),
+            DMA((2, 2)),
+            DMA((2,)),
+            DMA((2,)),
+        ]
+        + scatter_buffers(pairs, rows, width)
+        + scatter_sems(pairs, SUM_CUTS)
+        + gather_sems(pairs, CUTS),
+    )(gathered, partial.reshape(whole.shape), x, units, hid, gy)
+    return [outs[0].reshape(2 * pairs * rows, width)] + list(outs[1:])
+
+
+def row_gather_kernel(pairs, gathered, rows_out, *line_sems):
+    gather = Gather(pairs, CUTS, gathered, rows_out, line_sems)
+    greet(pairs)
+    gather.start()
+    for step in range(1, pairs):
+        for cut in range(CUTS):
+            gather.step(step, cut)
+    gather.finish()
+
+
+def row_gather(pairs, gathered, collective):
+    rows, width = gathered.shape
+    out = call_remote(
+        functools.partial(row_gather_kernel, pairs),
+        collective,
+        in_specs=[ANY],
+        out_specs=ANY,
+        out_shape=jax.ShapeDtypeStruct((2 * pairs, rows, width), LOW),
+        scratch_shapes=gather_sems(pairs, CUTS),
+    )(gathered)
+    return out.reshape(2 * pairs * rows, width)
 
 
 def arrival(place, pairs, step):
@@ -901,37 +1164,39 @@
 
 
 def ffn_kernel(
-    pairs, hyper, mix, branch, back, w_in, w_out, gy_rows,
+    plane, pairs, hyper, mix, branch, back_home, w_in, w_out, gy_rows,
     rows_out, hid_out, units_out, y_out, h, gh_out, gy_out,
     own, x, wd, gy, hid, units, y, part, twin, from_left, from_right, total, upstream,
     load_sem, gy_sem, hid_sem, units_sem, y_sem, x_sem,
-    twin_send, twin_recv, right_send, right_recv, left_send, left_recv, *line_sems,
+    twin_send, twin_recv, right_send, right_recv, left_send, left_recv, *rest,
 ):
+    plane_sems, line_sems = rest[:3], rest[3:]
     me, place, side = line_place()
     last = pairs - 1
     rows = own.shape[0]
-    height = rows // CUTS
+    height = rows // SUM_CUTS
+    half = units.shape[2] // 2
     n_col, n_dp, owned, width = w_out.shape
-    half = units.shape[2] // 2
-    greet(pairs)
-    loads = [
-        pltpu.make_async_copy(mix, h, load_sem.at[0]),
-        pltpu.make_async_copy(branch, total, load_sem.at[1]),
-        pltpu.make_async_copy(back, upstream, load_sem.at[2]),
-    ]
-    for load in loads:
-        load.start()
     tiles = [
         pltpu.make_async_copy(
             w_out.at[c, d],
             wd.at[pl.ds(d * owned, owned), pl.ds(c * width, width)],
-            load_sem.at[3 + c * n_dp + d],
+            load_sem.at[2 + c * n_dp + d],
         )
         for c in range(n_col)
         for d in range(n_dp)
     ]
     for tile in tiles:
         tile.start()
+    greet(pairs, plane)
+    loads = [
+        pltpu.make_async_copy(mix, h, load_sem.at[0]),
+        pltpu.make_async_copy(branch, total, load_sem.at[1]),
+    ]
+    for load in loads:
+        load.start()
+    exchange = to_work(plane, back_home, upstream, plane_sems, 0)
+    exchange.start()
     order = [arrival(place, pairs, step) for step in range(pairs)]
 
     def load_gy(step):
@@ -1015,7 +1280,7 @@
         for at_end, rightward in ((place == 0, True), (place == last, False)):
             @pl.when(at_end & (dest != place))
             def _():
-                for cut in range(CUTS):
+                for cut in range(SUM_CUTS):
                     span = pl.ds(cut * height, height)
                     part[dest * 2 + side, span] = here(dest, span).astype(LOW)
                     line(dest, cut, rightward).start()
@@ -1042,21 +1307,30 @@
             send_first(step - 1)
     send_first(pairs - 1)
 
-    def pass_on(dest, rightward):
+    def pass_on(dest, cut, rightward):
         arrived = from_left if rightward else from_right
-        for cut in range(CUTS):
-            span = pl.ds(cut * height, height)
-            line(dest, cut, rightward).wait_recv()
-            part[dest * 2 + side, span] = (here(dest, span) + arrived[dest, span].astype(FULL)).astype(LOW)
-            line(dest, cut, rightward).start()
-
-    for reach in range(2, pairs):
-        rightward, leftward = (place > 0) & (place < reach), (place < last) & (place > last - reach)
-        pl.when(rightward & (place < pairs // 2))(functools.partial(pass_on, reach, True))
-        pl.when(leftward)(functools.partial(pass_on, last - reach, False))
-        pl.when(rightward & (place >= pairs // 2))(functools.partial(pass_on, reach, True))
-
-    for cut in range(CUTS):
+        span = pl.ds(cut * height, height)
+        line(dest, cut, rightward).wait_recv()
+        part[dest * 2 + side, span] = (here(dest, span) + arrived[dest, span].astype(FULL)).astype(LOW)
+        line(dest, cut, rightward).start()
+
+    for inner in range(1, pairs // 2):
+        order_here = [(reach, cut, 0, True, reach) for reach in range(inner + 1, pairs) for cut in range(SUM_CUTS)]
+        order_here += [
+            (last - dest, cut + last - 2 * inner, 1, False, dest) for dest in range(inner) for cut in range(SUM_CUTS)
+        ]
+        for reach, at, late, near, dest in sorted(order_here):
+            cut = at - (last - 2 * inner) * late
+
+            @pl.when(place == inner)
+            def _():
+                pass_on(dest, cut, near)
+
+            @pl.when(place == last - inner)
+            def _():
+                pass_on(last - dest, cut, not near)
+
+    for cut in range(SUM_CUTS):
         span = pl.ds(cut * height, height)
         total[span] = here(place, span)
 
@@ -1070,11 +1344,12 @@
             line(place, cut, False).wait_recv()
             total[span] += from_right[place, span].astype(FULL)
 
-    loads[2].wait()
+    exchange.arrive()
     grad = norm_backward(total[...], h[...])
     gh_out[...] = grad.astype(LOW)
     gy_out[...] = (upstream[...] + branch_weight(hyper) * grad).astype(LOW)
 
+    exchange.leave()
     gather.leave()
     for step in range(pairs):
         save_x(step).wait()
@@ -1083,7 +1358,7 @@
             save.wait()
     for dest in range(pairs):
         to_twin(dest).wait_send()
-        for cut in range(CUTS):
+        for cut in range(SUM_CUTS):
             @pl.when(place < dest)
             def _():
                 line(dest, cut, True).wait_send()
@@ -1093,11 +1368,10 @@
                 line(dest, cut, False).wait_send()
 
 
-def feed_forward(pairs, hyper, mix, branch, back, w_in, w_out, gy_rows, collective):
+def feed_forward(plane, pairs, hyper, mix, branch, back_home, w_in, w_out, gy_rows, collective):
     rows, width = mix.shape
     units = w_in.shape[1]
     half = units // 2
-    n_col, n_dp = w_out.shape[:2]
     low = jax.ShapeDtypeStruct((rows, width), LOW)
 
     def by_pair(last_width):
@@ -1106,7 +1380,7 @@
     blocks = pltpu.VMEM((pairs, rows, width), LOW)
     full = pltpu.VMEM((rows, width), FULL)
     outs = call_remote(
-        functools.partial(ffn_kernel, pairs),
+        functools.partial(ffn_kernel, plane, pairs),
         collective,
         in_specs=[SMEM, ANY, ANY, ANY, VMEM, ANY, ANY],
         out_specs=[ANY, ANY, ANY, ANY, VMEM, VMEM, VMEM],
@@ -1133,7 +1407,7 @@
             blocks,
             full,
             full,
-            DMA((3 + n_col * n_dp,)),
+            DMA((2 + plane[0] * plane[1],)),
             DMA((2,)),
             DMA((2,)),
             DMA((2,)),
@@ -1142,34 +1416,98 @@
             DMA((pairs,)),
             DMA((pairs,)),
         ]
-        + [DMA((pairs, CUTS))] * 4
+        + [DMA((pairs, SUM_CUTS))] * 4
+        + exchange_sems(plane, 1)
         + gather_sems(pairs, CUTS),
-    )(hyper, mix, branch, back, w_in, w_out, gy_rows.reshape(pairs, 2 * rows, width))
+    )(hyper, mix, branch, back_home, w_in, w_out, gy_rows.reshape(pairs, 2 * rows, width))
     tokens = 2 * pairs * rows
     return [value.reshape(tokens, -1) for value in outs[:4]] + list(outs[5:])
 
 
-def leave_kernel(plane, pairs, count, part, h, y_att, y_ffn, gh_ffn, *rest):
-    grads, rest = rest[:count], rest[count:]
-    homes, sums, rest = rest[:4], rest[4 : 4 + count], rest[4 + count :]
-    (total, last), plane_sems, scratch, rest = rest[:2], rest[2:5], rest[5:18], rest[18:]
-    scatter = Scatter(pairs, CUTS, part, scratch[:6], scratch[6:])
-    planes = plane_sums(grads, sums, rest)
+def leave_kernel(
+    plane, pairs, in_kernel, gy_in, x_in, heads_in, log_in, q, k, v, cosine, sine, start, w_in, w_out, h,
+    y_att, y_ffn, gh_ffn, *rest,
+):
+    if in_kernel:
+        ffn_grad, rest = rest[0], rest[1:]
+    homes, rest = rest[:4], rest[4:]
+    if in_kernel:
+        sums, rest = rest[:6], rest[6:]
+    (grad_in, grad_out, rows_in, units, back, k_sum, v_sum, part, total, last, load_sem), rest = (
+        rest[:11],
+        rest[11:],
+    )
+    plane_sems, scratch, rest = rest[:3], rest[3:13], rest[13:]
+    scatter = Scatter(pairs, SUM_CUTS, part, scratch[:3], scratch[3:])
+    load_gy = pltpu.make_async_copy(gy_in, rows_in, load_sem.at[0])
+    load_x = pltpu.make_async_copy(x_in, rows_in, load_sem.at[1])
+    load_gy.start()
+    planes = []
+    if in_kernel:
+        own_ffn, rest = rest[0], rest[1:]
+        for index, block_of in enumerate(
+            (
+                by_owner(ffn_grad, sums[0].shape[1]),
+                by_tiles(grad_out, *sums[2].shape[1:]),
+                by_rows(grad_in, sums[4].shape[1]),
+            )
+        ):
+            one = rest[8 * index : 8 * index + 8]
+            planes.append(
+                PlaneScatter(
+                    block_of,
+                    sums[2 * index],
+                    sums[2 * index + 1],
+                    (one[0], None if index else own_ffn, one[1], one[2]),
+                    one[3:],
+                )
+            )
     greet(pairs, plane)
-    scatter.start()
-    for one in planes:
-        one.start()
     ways = [
         to_home(plane, work, home, plane_sems, index)
         for index, (work, home) in enumerate(zip((y_att, y_ffn, gh_ffn, last), homes))
     ]
+    for one in planes[:1]:
+        one.start()
     for way in ways[:3]:
         way.start()
-    for step in range(pairs - 1):
-        for cut in range(CUTS):
-            scatter.step(step, cut)
-        if 0 < step <= len(planes):
-            planes[step - 1].forward()
+    load_gy.wait()
+    back[...] = dot_last(rows_in[...], w_out[...]).astype(LOW)
+    width = q.shape[1]
+    for head in range(width // HEAD):
+        attend_head_back(
+            head, back, q, k, v, log_in, cosine, sine, start, units, k_sum, v_sum
+        )
+    rows = total.shape[0]
+    for owner in range(2 * pairs):
+        part[owner] = dot_last(units[pl.ds(owner * rows, rows)], w_in[...]).astype(LOW)
+    scatter.start()
+    scatter.begin()
+    grad_out[...] = dot_first(heads_in[...], rows_in[...]).astype(LOW)
+    load_x.start()
+    for one in planes[1:2]:
+        one.start()
+    load_x.wait()
+    quarter = D // SUM_CUTS
+    polls = list(range(scatter.polls()))
+    for cut in range(SUM_CUTS):
+        for index in polls[:2]:
+            scatter.poll(index)
+        polls = polls[2:]
+
+        @pl.loop(0, quarter // UNIT)
+        def _(index):
+            at = pl.multiple_of(cut * quarter + index * UNIT, UNIT)
+            grad_in[pl.ds(at, UNIT)] = dot_first(rows_in[:, pl.ds(at, UNIT)], units[...]).astype(LOW)
+
+    for one in planes[2:]:
+        one.start()
+    for one in planes[:1]:
+        one.forward()
+    for index in polls:
+        scatter.poll(index)
+    for one in planes[1:]:
+        one.forward()
     scatter.finish(total)
     last[...] = norm_backward(total[...], h[...]).astype(last.dtype)
     ways[3].start()
@@ -1180,23 +1518,57 @@
         way.leave()
 
 
-def leave(plane, pairs, partial, h, works, grads, collective):
+def leave(
+    plane, pairs, ffn_grad, gy, x, heads, log_totals, q, k, v, tables, w_in, w_out, h, works, collective
+):
+    in_kernel = len(ffn_grad) > 0
     rows, width = h.shape
     n_dp, n_col = plane
+    tokens, local = q.shape
     home = jax.ShapeDtypeStruct((n_dp, n_col, rows // n_dp, width // n_col), works[0].dtype)
-    owned = [owned_shape(grad) for grad in grads]
+    grads = [(width, 3 * local), (local, width)]
+    extra, planes = [], []
+    if in_kernel:
+        owned = [(1,) + ffn_grad[0].shape[2:], (1, local // 2, width // 2), (3, width // 4, local)]
+        planes.append(pltpu.VMEM((2, 2, owned[0][1] // 2, owned[0][2]), LOW))
+        for shape in owned:
+            extra += [shape, (2, 8, shape[0] * shape[2])]
+            half = (shape[1] // 2, shape[0] * shape[2])
+            planes += [
+                pltpu.VMEM((2, 2) + half, LOW),
+                pltpu.VMEM((2,) + half, LOW),
+                pltpu.VMEM((2,) + half, LOW),
+                DMA((2, 2)),
+                DMA((2, 2)),
+                DMA((2, 2)),
+                DMA((2,)),
+                DMA((2,)),
+            ]
+    grad_refs = [pltpu.VMEM(shape, LOW) for shape in grads]
+    grad_outs = [] if in_kernel else [jax.ShapeDtypeStruct(shape, LOW) for shape in grads]
     outs = call_remote(
-        functools.partial(leave_kernel, plane, pairs, len(grads)),
+        functools.partial(leave_kernel, plane, pairs, in_kernel),
         collective,
-        in_specs=[ANY, VMEM, ANY, ANY, ANY] + [ANY] * len(grads),
-        out_specs=[ANY] * 4 + [VMEM] * len(grads),
-        out_shape=[home] * 4 + [jax.ShapeDtypeStruct(shape, FULL) for shape in owned],
-        scratch_shapes=[pltpu.VMEM((rows, width), FULL), pltpu.VMEM((rows, width), works[0].dtype)]
+        in_specs=[ANY, ANY] + [VMEM] * 11 + [ANY] * (3 + len(ffn_grad)),
+        out_specs=[ANY] * 4 + [VMEM] * (len(extra) + len(grad_outs)),
+        out_shape=[home] * 4 + [jax.ShapeDtypeStruct(shape, FULL) for shape in extra] + grad_outs,
+        scratch_shapes=(grad_refs if in_kernel else [])
+        + [
+            pltpu.VMEM(x.shape, LOW),
+            pltpu.VMEM((tokens, 3 * local), LOW),
+            pltpu.VMEM((tokens, local), LOW),
+            pltpu.VMEM((tokens, HEAD), FULL),
+            pltpu.VMEM((tokens, HEAD), FULL),
+            pltpu.VMEM((2 * pairs, rows, width), LOW),
+            pltpu.VMEM((rows, width), FULL),
+            pltpu.VMEM((rows, width), works[0].dtype),
+            DMA((2,)),
+        ]
         + exchange_sems(plane, 4)
-        + scatter_buffers(pairs, rows, width)
-        + scatter_sems(pairs, CUTS)
-        + sum([plane_scratch(*shape) for shape in owned], []),
-    )(partial.reshape(2 * pairs, rows, width), h, *works, *grads)
+        + scatter_buffers(pairs, rows, width, False)
+        + scatter_sems(pairs, SUM_CUTS)
+        + planes,
+    )(gy, x, heads, log_totals, q, k, v, *tables, w_in, w_out, h, *works, *ffn_grad)
     return outs[:4], outs[4:]
 
 
@@ -1339,12 +1711,9 @@
     group_tokens = segments.shape[2]
     slot = rows // n_dp
     travel = LOW if slot % 16 == 0 else FULL
-    attention_in_low = gather_blocks(side_by_side(attention_in).astype(LOW))
-    attention_out_low = whole_out(attention_out.astype(LOW), n_dp, n_col)
-    feedforward_in_low = gather_blocks(side_by_side(feedforward_in).astype(LOW))
-    feedforward_out_low = gather_blocks(feedforward_out.astype(LOW)).reshape(
-        n_col, n_dp, *feedforward_out.shape
-    )
+    in_kernel = plane == (2, 2)
+    attention_low = [side_by_side(attention_in).astype(LOW), attention_out.astype(LOW)]
+    feedforward_low = [side_by_side(feedforward_in).astype(LOW), feedforward_out.astype(LOW)]
 
     group = destination // group_tokens
     sent = (
@@ -1360,71 +1729,100 @@
     segment = lax.dynamic_index_in_dim(segments[:, 0], lax.axis_index("col"), 0, keepdims=False)
     cosine, sine, start = rotary_tables(segment)
 
-    rows_att, hidden_att, mix_work, back_work, gy_work = enter(
-        plane, pairs, h_home, mix_home, back_home, gy_home, 1
-    )
-    qkv = jnp.dot(rows_att, attention_in_low, preferred_element_type=FULL)
-    heads_low, log_totals, query_low, key_low, value_low = attend_forward(qkv, cosine, sine, start)
-    partial_att = jnp.dot(heads_low, attention_out_low, preferred_element_type=FULL).astype(LOW)
-    grad_rows_ffn, branch_low, branch_att, _ = duplex(
-        pairs, plane, partial_att, gy_work.astype(LOW), [], 2
-    )
+    feedforward_out_low = gather_blocks(feedforward_low[1]).reshape(n_col, n_dp, *feedforward_out.shape)
+    early = attention_low if in_kernel else []
+    rows_att, hidden_att, gy_work, wholes = enter(plane, pairs, h_home, gy_home, early, 1)
+    if not in_kernel:
+        wholes = [gather_blocks(attention_low[0]), whole_out(attention_low[1], n_dp, n_col)]
+    attention_in_low, attention_out_low = wholes
+    (
+        grad_rows_ffn,
+        mix_work,
+        heads_low,
+        log_totals,
+        query_low,
+        key_low,
+        value_low,
+        branch_low,
+        branch_att,
+    ), wholes = attend(
+        plane,
+        pairs,
+        rows_att,
+        attention_in_low,
+        attention_out_low,
+        cosine,
+        sine,
+        start,
+        gy_work.astype(LOW),
+        mix_home,
+        feedforward_low[:1] if in_kernel else [],
+        2,
+    )
+    feedforward_in_low = wholes[0] if in_kernel else gather_blocks(feedforward_low[0])
     rows_ffn, hidden_low, grad_units, partial_ffn, grad_hidden_ffn, grad_branch = feed_forward(
+        plane,
         pairs,
         hyper,
         mix_work,
         branch_att,
-        back_work,
+        back_home,
         feedforward_in_low,
         feedforward_out_low,
         grad_rows_ffn,
         3,
     )
-    in_kernel = plane == (2, 2)
-    grads_ffn = [
-        jnp.einsum("td,tu->du", rows_ffn, grad_units, preferred_element_type=FULL).astype(LOW),
-        jnp.einsum("tu,td->ud", hidden_low, grad_rows_ffn, preferred_element_type=FULL).astype(LOW),
-    ]
-    grad_rows_att, branch_ffn, _, sums_ffn = duplex(
-        pairs, plane, partial_ffn, grad_branch, grads_ffn if in_kernel else [], 5
-    )
-
-    grad_heads = jnp.einsum(
-        "td,ud->tu", grad_rows_att, attention_out_low, preferred_element_type=FULL
-    ).astype(LOW)
-    grad_units_att = jnp.concatenate(
-        attend_backward(grad_heads, query_low, key_low, value_low, log_totals, cosine, sine, start),
-        axis=1,
-    )
-    grads_att = [
-        jnp.einsum("td,tu->du", rows_att, grad_units_att, preferred_element_type=FULL).astype(LOW),
-        jnp.einsum("tu,td->ud", heads_low, grad_rows_att, preferred_element_type=FULL).astype(LOW),
-    ]
-    partial_grad = jnp.einsum(
-        "tu,du->td", grad_units_att, attention_in_low, preferred_element_type=FULL
-    ).astype(LOW)
+    if in_kernel:
+        grad_rows_att, branch_ffn, grad_out, sum_in, square = back_gather(
+            pairs, plane, grad_branch, partial_ffn, rows_ffn, grad_units, hidden_low, grad_rows_ffn, 5
+        )
+        ffn_grad, squares = [grad_out], [square]
+    else:
+        grad_rows_att = row_gather(pairs, grad_branch, 5)
+        branch_ffn = lax.psum_scatter(partial_ffn, "row", scatter_dimension=0, tiled=True)
+        sums_ffn = [
+            apart(
+                scatter_blocks(
+                    jnp.einsum("td,tu->du", rows_ffn, grad_units, preferred_element_type=FULL).astype(LOW)
+                ),
+                2,
+            ),
+            own_out(
+                jnp.einsum("tu,td->ud", hidden_low, grad_rows_ffn, preferred_element_type=FULL), n_dp, n_col
+            ),
+        ]
+        ffn_grad, squares = [], [value * value for value in sums_ffn]
+
     homes, sums_att = leave(
         plane,
         pairs,
-        partial_grad,
+        ffn_grad,
+        grad_rows_att,
+        rows_att,
+        heads_low,
+        log_totals,
+        query_low,
+        key_low,
+        value_low,
+        (cosine, sine, start),
+        attention_in_low,
+        attention_out_low,
         hidden_att,
         [value.astype(travel) for value in (branch_low, branch_ffn, grad_hidden_ffn)],
-        grads_att if in_kernel else [],
         6,
     )
-    if not in_kernel:
-        sums_ffn, sums_att = (
-            [scatter_blocks(grads[0]), own_out(grads[1], n_dp, n_col)] for grads in (grads_ffn, grads_att)
-        )
-    shard_feedforward_in, shard_feedforward_out = apart(sums_ffn[0], 2), sums_ffn[1]
-    shard_attention_in, shard_attention_out = apart(sums_att[0], 3), sums_att[1]
+    if in_kernel:
+        squares += sums_att[1::2]
+        shard_feedforward_out, shard_attention_out, shard_attention_in = sums_att[::2]
+        shard_feedforward_out, shard_attention_out = shard_feedforward_out[0], shard_attention_out[0]
+        shard_feedforward_in = sum_in
+    else:
+        shard_attention_in = apart(scatter_blocks(sums_att[0]), 3)
+        shard_attention_out = own_out(sums_att[1], n_dp, n_col)
+        squares += [value * value for value in (shard_attention_in, shard_attention_out)]
+        shard_feedforward_in, shard_feedforward_out = sums_ffn
+    square = sum(jnp.sum(value) for value in squares)
     streams_out, stream_grad, dots = finish(hyper, streams, cotangent, sent, homes)
-    square = (
-        jnp.sum(shard_attention_in * shard_attention_in)
-        + jnp.sum(shard_feedforward_in * shard_feedforward_in)
-        + jnp.sum(shard_attention_out * shard_attention_out)
-        + jnp.sum(shard_feedforward_out * shard_feedforward_out)
-    )
     dots = jnp.concatenate([jnp.sum(gram, axis=(1, 2)), jnp.sum(dots, axis=(1, 2)), square[None]])
     totals = sum_everywhere(plane, jnp.pad(dots, (0, 128 - dots.shape[0])).reshape(1, 128), 7)[0]
     a0, m0, c0 = hyper_weights[0, :, 0], hyper_weights[0, :, 1:5], hyper_weights[0, :, 5]

time: 752 us -> 652 us (0.87)
  matrix products: 62 us -> 0 us
  waiting for transfers between devices: 16.5 us -> 0.04 us
  Pallas kernels: 577 us -> 564 us
    dot_general x8 -> x0, matrix products: 62 us -> none  [the longest x1 15.9 us: body(): jnp.einsum('td,tu->du', rows_ffn, grad_units, preferred_element_type=FULL)]
    all_gather x4 -> x1, waiting for transfers between devices: 16.5 us -> 0.02 us  [gather_blocks(): return lax.all_gather(weight_low, ('col', 'dp'), axis=0, tiled=True)]
    pallas_call x1, Pallas kernels: 19.3 us -> 9.77 us  [sum_everywhere(): call_remote(functools.partial(total_kernel, plane, count), collective, in...]
    pallas_call x7 -> x5, Pallas kernels: 532 us -> 528 us  [the longest x1 126 us: feed_forward(): call_remote(functools.partial(ffn_kernel, plane, pairs), collective, in_s...]
  transfers between devices with their start and end apart: 4 -> 1, of which waited for: 1 -> 0; matrix products, arithmetic and copies ran while one was open for 4% -> 3% of each run, Pallas kernels for 28% -> 33%
where the time goes in v4:
time: 652 us; the launch traced here: 645 us
  Pallas kernels  564 us (87%)
  other arithmetic  43.9 us (7%)
  between operations  20.4 us (3%)
  local copies, waits for them, and re-layouts  16.2 us (2%)
    pallas_call x1, Pallas kernels, feed_forward(): call_remote(functools.partial(ffn_kernel, plane, pairs), collective, in_s...  126 us
    pallas_call x1, Pallas kernels, leave(): call_remote(functools.partial(leave_kernel, plane, pairs, in_kernel), col...  114 us
    pallas_call x1, Pallas kernels, attend(): call_remote(functools.partial(attend_kernel, plane, pairs, len(weights)),...  110 us
    pallas_call x1, Pallas kernels, enter(): call_remote(functools.partial(enter_kernel, plane, pairs, len(weights)),...  91.4 us
    pallas_call x1, Pallas kernels, back_gather(): call_remote(functools.partial(back_kernel, pairs, plane), collective, in_...  86.3 us
    sub x5, other arithmetic, adam_update(): weight - learning_rate * (new_one / fix_one / (jnp.sqrt(new_two / fix_two...  18.9 us
    pallas_call x1, Pallas kernels, finish(): pl.pallas_call(finish_kernel, grid=(micro, width // wide), in_specs=[SMEM...  13.6 us
  transfers between devices with their start and end apart: 1, of which 0 were waited for; matrix products, arithmetic and copies ran while one was open for 3% of the time, Pallas kernels for 33%

profile of v4, /device:TPU:0, one launch (start us, length us, event | category | flops | bytes accessed | tf_op | source)
XLA Modules:
  0.0 644.9 jit_solution(6979126842467156817)
XLA Ops:
  7.3 2.8 convert_element_type.27
  14.5 3.8 convert.20
  20.2 13.0 %shard_map.371 = (f32[2,2,96,1024]{3,2,1,0:T(8,128)}, f32[2,2,96,1024]{3,2,1,0:T(8,128)}, f32[2,2,96,1024]{3,2,1,0:T(8,128)}, bf16[2,2,96,1024]{3,2,1,0:T(8,128)(2,1)}, f32[16,8,256]{2,1,0:T(8,128)}) custom-call(f32[48]{0:T(128)} %reshape.162.hyper, f32[2,4,192,1024]{3,2,1,0:T(8,128)} %streams.3, f32[2,4,192,1024]{3,2,1,0:T(8,128)} %cotangent.3, ...), custom_call_target="tpu_custom_call" | custom-call | tf_op jit(solution)/shard_map/pallas_call | solution.py:140
  35.2 91.4 %shard_map.372 = (bf16[8,192,2048]{2,1,0:T(8,128)(2,1)}, f32[192,2048]{1,0:T(8,128)}, bf16[192,2048]{1,0:T(8,128)(2,1)}, bf16[2048,768]{1,0:T(8,128)(2,1)}, bf16[256,2048]{1,0:T(8,128)(2,1)}) custom-call(f32[2,2,96,1024]{3,2,1,0:T(8,128)} %get-tuple-element.67.h_home, bf16[2,2,96,1024]{3,2,1,0:T(8,128)(2,1)} %get-tuple-element.68.gy_home, ...), custom_call_target="tpu_custom_call" | custom-call | tf_op jit(solution)/shard_map/pallas_call | solution.py:895
  126.7 1.7 slice_bitcast_fusion.1
  128.4 1.5 pad_maximum_fusion.rest_0_
  129.9 2.8 fusion.4
  132.7 1.6 pad_maximum_fusion.2
  134.4 110.2 %shard_map.373 = (bf16[8,192,2048]{2,1,0:T(8,128)(2,1)}, f32[192,2048]{1,0:T(8,128)}, bf16[1536,256]{1,0:T(8,128)(2,1)}, f32[1536,2]{1,0:T(8,128)}, bf16[1536,25...) custom-call(bf16[1536,2048]{1,0:T(8,128)(2,1)} %bitcast.67, ...), custom_call_target="tpu_custom_call" | custom-call | tf_op jit(solution)/shard_map/pallas_call | solution.py:981
  244.8 125.8 %shard_map.374 = (bf16[8,192,2048]{2,1,0:T(8,128)(2,1)}, bf16[4,384,1024]{2,1,0:T(8,128)(2,1)}, bf16[4,384,2048]{2,1,0:T(8,128)(2,1)}, bf16[4,384,2048]{2,1,0:T(...) custom-call(f32[48]{0:T(128)} %reshape.162.hyper, ...), custom_call_target="tpu_custom_call" | custom-call | tf_op jit(solution)/shard_map/pallas_call | solution.py:1382
  370.6 86.3 %shard_map.375 = (bf16[8,192,2048]{2,1,0:T(8,128)(2,1)}, bf16[192,2048]{1,0:T(8,128)(2,1)}, bf16[2,2,512,1024]{3,2,1,0:T(8,128)(2,1)}, f32[2,512,1024]{2,1,0:T(8,128)}, f32[2,8,2048]{2,1,0:T(8,128)}) custom-call(bf16[192,2048]{1,0:T(8,128)(2,1)} %get-tuple-element.79.gathered, bf16[8,192,2048]{2,1,0:T(8,128)(2,1)} %bitcast.72, bf16[1536,2048]{1,0:T(8,128)(2,1)} %bitcast.70, ...), custom_call_target="tpu_custom_call" | custom-call | tf_op jit(solution)/shard_map/pallas_call | solution.py:1098
  456.9 114.2 %shard_map.376 = (bf16[2,2,96,1024]{3,2,1,0:T(8,128)(2,1)}, bf16[2,2,96,1024]{3,2,1,0:T(8,128)(2,1)}, bf16[2,2,96,1024]{3,2,1,0:T(8,128)(2,1)}, bf16[2,2,96,1024...) custom-call(bf16[1536,2048]{1,0:T(8,128)(2,1)} %bitcast.73, ...), custom_call_target="tpu_custom_call" | custom-call | tf_op jit(solution)/shard_map/pallas_call | solution.py:1549
  571.1 1.5 reduce_sum.119
  573.2 1.5 reduce_sum.120
  574.6 1.4 reduce_sum.121
  576.0 13.6 %shard_map.377 = (f32[2,4,192,1024]{3,2,1,0:T(8,128)}, f32[2,4,192,1024]{3,2,1,0:T(8,128)}, f32[17,8,256]{2,1,0:T(8,128)}) custom-call(f32[48]{0:T(128)} %reshape.162.hyper, f32[2,4,192,1024]{3,2,1,0:T(8,128)} %streams.3, f32[2,4,192,1024]{3,2,1,0:T(8,128)} %cotangent.3, s32[2,192,1]{2,1,0:T(8,128)} %copy.63.sent, ...), custom_call_target="tpu_custom_call" | custom-call | tf_op jit(solution)/shard_map/pallas_call | solution.py:194
  593.9 9.8 %shard_map.378 = f32[1,128]{1,0:T(1,128)} custom-call(f32[1,128]{1,0:T(1,128)} %fusion.8.own), custom_call_target="tpu_custom_call" | custom-call | tf_op jit(solution)/shard_map/pallas_call | solution.py:1624
  605.3 1.3 fusion.14
  610.3 7.8 %multiply_subtract_fusion.1 = (f32[512,1024]{1,0:T(8,128)}, f32[512,1024]{1,0:T(8,128)}, f32[512,1024]{1,0:T(8,128)}) fusion(f32[512,1024]{1,0:T(8,128)} %param.27, f32[]{:T(128)} %bitcast.37, f32[]{:T(128)} %bitcast.36, f32[]{:T(128)S(6)} %div.75, f32[512,1024]{1,0:T(8,128)} %param.35, f32[512,1024]{1,0:T(8,128)} %param.31, ...), kind=kLoop, calls=%fused_computation.9 | loop fusion | flops 8388608 | bytes 14680076 | tf_op jit(solution)/shard_map/sub | solution.py:1680
  618.1 1.4 multiply_subtract_fusion.3
  621.4 6.0 multiply_subtract_fusion
  627.4 3.0 multiply_subtract_fusion.2
  632.3 2.1 copy.78
  635.4 1.3 copy.80
  (87 shorter events, 18.5 us)
Async XLA Ops:
  7.2 5.0 copy-start
  7.2 3.0 copy-start.20
  7.2 3.6 copy-start.17
  7.2 4.2 copy-start.5
  7.2 237.6 %all-gather.2.cloned.1.call-start = ((), (), s32[]{:S(2)}) async-start(), calls=%async_computation | async-start | bytes 5242880 | tf_op jit(solution)/shard_map/all_gather | solution.py:1646
  10.1 1.3 copy-start.10
  456.9 115.6 %copy-start.18 = (f32[2,8,2048]{2,1,0:T(8,128)S(1)}, f32[2,8,2048]{2,1,0:T(8,128)}, u32[]{:S(2)}) copy-start(f32[2,8,2048]{2,1,0:T(8,128)} %get-tuple-element.103) | copy-start | bytes 393220
  576.0 42.0 %copy-start.11 = (f32[128,1024]{1,0:T(8,128)S(1)}, f32[128,1024]{1,0:T(8,128)}, u32[]{:S(2)}) copy-start(f32[128,1024]{1,0:T(8,128)} %param.26) | copy-start | bytes 1572868
  604.4 13.7 %copy-start.12 = (f32[1,128,1024]{2,1,0:T(8,128)S(1)}, f32[1,128,1024]{2,1,0:T(8,128)}, u32[]{:S(2)}) copy-start(f32[1,128,1024]{2,1,0:T(8,128)} %get-tuple-element.109) | copy-start | bytes 1572868
  604.4 13.7 %copy-start.15 = (f32[128,1024]{1,0:T(8,128)S(1)}, f32[128,1024]{1,0:T(8,128)}, u32[]{:S(2)}) copy-start(f32[128,1024]{1,0:T(8,128)} %param.34) | copy-start | bytes 1572868
  604.4 13.7 %copy-start.16 = (f32[128,1024]{1,0:T(8,128)S(1)}, f32[128,1024]{1,0:T(8,128)}, u32[]{:S(2)}) copy-start(f32[128,1024]{1,0:T(8,128)} %param.30) | copy-start | bytes 1572868
  608.9 21.6 %copy-start.19 = (f32[2,4,6]{2,1,0:T(4,128)}, f32[2,4,6]{2,1,0:T(4,128)S(1)}, u32[]{:S(2)}) copy-start(f32[2,4,6]{2,1,0:T(4,128)S(1)} %get-tuple-element.186) | copy-start | bytes 580
  610.2 9.3 %copy-start.2 = (f32[2,512,1024]{2,1,0:T(8,128)S(1)}, f32[2,512,1024]{2,1,0:T(8,128)}, u32[]{:S(2)}) copy-start(f32[2,512,1024]{2,1,0:T(8,128)} %param.25) | copy-start | bytes 12582916
  610.3 9.3 %copy-start.3 = (f32[2,512,1024]{2,1,0:T(8,128)S(1)}, f32[2,512,1024]{2,1,0:T(8,128)}, u32[]{:S(2)}) copy-start(f32[2,512,1024]{2,1,0:T(8,128)} %get-tuple-element.183) | copy-start | bytes 12582916
  610.3 9.9 %copy-start.8 = (f32[2,512,1024]{2,1,0:T(8,128)S(1)}, f32[2,512,1024]{2,1,0:T(8,128)}, u32[]{:S(2)}) copy-start(f32[2,512,1024]{2,1,0:T(8,128)} %param.33) | copy-start | bytes 12582916
  610.3 11.1 %copy-start.9 = (f32[2,512,1024]{2,1,0:T(8,128)S(1)}, f32[2,512,1024]{2,1,0:T(8,128)}, u32[]{:S(2)}) copy-start(f32[2,512,1024]{2,1,0:T(8,128)} %param.29) | copy-start | bytes 12582916
  621.3 6.0 copy-start.6
  621.3 6.0 copy-start.7
  621.4 6.1 copy-start.13
  621.4 6.1 copy-start.14
  627.4 3.1 copy-start.21
  627.4 3.1 copy-start.22
  632.3 3.1 copy-start.4
  634.4 2.3 copy-start.1
Sparse Core Ops, SparseCore 0:
  10.5 76.0 all-gather.1

commit v5 on v4

--- a/solution.py
+++ b/solution.py
@@ -30,20 +30,10 @@
 ROOM = 63 * 2**20
 
 
-def rotary_tables(segment):
-    length = segment.shape[0]
-    places = jnp.arange(length, dtype=jnp.int32)
+def rotary_parts(segment):
     starts = jnp.sum((segment[None, :] < segment[:, None]).astype(jnp.int32), axis=1)
-    offsets = (places - starts).astype(jnp.float32)
-    halves = jnp.arange(HEAD // 2, dtype=jnp.float32)
-    inverse = jnp.exp(halves * (-2.0 * math.log(10000.0) / HEAD))
-    angles = offsets[:, None] * inverse[None, :]
-    cosine, sine = jnp.cos(angles), jnp.sin(angles)
-    return (
-        jnp.concatenate([cosine, cosine], axis=1),
-        jnp.concatenate([-sine, sine], axis=1),
-        starts[:, None],
-    )
+    halves = jnp.tile(jnp.arange(HEAD // 2, dtype=jnp.float32), 2)
+    return starts[:, None], jnp.exp(halves * (-2.0 * math.log(10000.0) / HEAD))[None, :]
 
 
 def norm_forward(hidden):
@@ -97,11 +87,15 @@
 
 
 def place_rows(match, values_in):
+    match = match.astype(LOW)
     if values_in.dtype == LOW:
-        return jnp.dot(match.astype(LOW), values_in, preferred_element_type=FULL)
-    return jnp.dot(
-        match.astype(FULL), values_in, precision=lax.Precision.HIGHEST, preferred_element_type=FULL
-    )
+        return jnp.dot(match, values_in, preferred_element_type=FULL)
+    high = values_in.astype(LOW)
+    rest = values_in - high.astype(FULL)
+    middle = rest.astype(LOW)
+    last = (rest - middle.astype(FULL)).astype(LOW)
+    high, middle, last = (jnp.dot(match, piece, preferred_element_type=FULL) for piece in (high, middle, last))
+    return high + (middle + last)
 
 
 def prepare_kernel(hyper, streams, cotangent, sent, h_out, mix_out, back_out, gy_out, gram_out):
@@ -133,7 +127,7 @@
 
 def prepare(hyper, streams, cotangent, sent, n_dp, travel):
     micro, _, rows, width = streams.shape
-    slot, wide = rows // n_dp, 256
+    slot, wide = rows // n_dp, 512
     block = pl.BlockSpec((1, STREAMS, rows, wide), lambda m, f: (m, 0, 0, f))
     home = pl.BlockSpec((n_dp, 1, slot, wide), lambda m, f: (0, m, 0, f))
     shape = (n_dp, micro, slot, width)
@@ -187,7 +181,7 @@
 def finish(hyper, streams, cotangent, sent, homes):
     micro, _, rows, width = streams.shape
     n_dp, _, slot, _ = homes[0].shape
-    wide = 256
+    wide = 512
     block = pl.BlockSpec((1, STREAMS, rows, wide), lambda m, f: (m, 0, 0, f))
     home = pl.BlockSpec((n_dp, 1, slot, wide), lambda m, f: (0, m, 0, f))
     count = 4 * STREAMS + 1
@@ -569,17 +563,23 @@
             {"row": line_place()[0] - 2},
         )
 
-    def start(self):
+    def order(self):
         order = []
         for step in range(self.pairs):
             for dest in (self.pairs - 1 - step, step):
                 if dest not in order:
                     order.append(dest)
-        for dest in order:
-            for cut in range(self.cuts):
-                self.to_twin(dest, cut).start()
-                if self.own is not None:
-                    self.load(dest, cut).start()
+        return order
+
+    def offer(self, dest):
+        for cut in range(self.cuts):
+            self.to_twin(dest, cut).start()
+            if self.own is not None:
+                self.load(dest, cut).start()
+
+    def start(self):
+        for dest in self.order():
+            self.offer(dest)
 
     def here(self, dest, cut):
         return self.mine(dest, cut)[...].astype(FULL) + self.twin[dest, self.span(cut)].astype(FULL)
@@ -740,7 +740,10 @@
                 self.out[index, pl.ds(half * self.height, self.height)] = total[
                     :, index * width : (index + 1) * width
                 ]
-            self.square[half] = fold(total * total)
+            squares = fold(total * total)
+            self.square[half] = sum(
+                squares[:, at : at + 128] for at in range(0, squares.shape[1], 128)
+            )
         for half in range(2):
             for index in range(2):
                 self.move(half, index).wait_send()
@@ -781,9 +784,8 @@
         )
 
     def start(self):
-        for swap in range(2):
-            for half in range(2):
-                self.direct(half ^ swap, half).start()
+        for half in range(2):
+            self.direct(half, half).start()
         for half in range(2):
             self.stay(half).start()
 
@@ -791,6 +793,7 @@
         for half in range(2):
             self.direct(half, half).wait_recv()
             self.onward(half).start()
+            self.direct(1 - half, half).start()
 
     def finish(self):
         for half in range(2):
@@ -856,11 +859,13 @@
     ]
 
 
-def enter_kernel(plane, pairs, count, h_home, gy_home, *rest):
+def enter_kernel(plane, pairs, count, h_home, gy_home, start, inverse, w_in, *rest):
     weights, rest = rest[:count], rest[count:]
-    (rows_out, h, gy), rest = rest[:3], rest[3:]
+    (rows_out, h, gy, cosine, sine, w_low), rest = rest[:6], rest[6:]
     wholes, rest = rest[:count], rest[count:]
-    own, plane_sems, line_sems, rest = rest[0], rest[1:4], rest[4:10], rest[10:]
+    (own, w_full, load_sem), plane_sems, line_sems, rest = rest[:3], rest[3:6], rest[6:12], rest[12:]
+    load = pltpu.make_async_copy(w_in, w_full, load_sem)
+    load.start()
     gathers = plane_gathers(weights, wholes, rest)
     greet(pairs, plane)
     first = to_work(plane, h_home, h, plane_sems, 0)
@@ -872,8 +877,29 @@
     own[...] = norm_forward(h[...])[0].astype(LOW)
     gather = Gather(pairs, CUTS, own, rows_out, line_sems)
     gather.start()
+
+    def cast():
+        load.wait()
+        width = w_in.shape[2]
+        for index in range(w_in.shape[0]):
+            w_low[:, index * width : (index + 1) * width] = w_full[index].astype(LOW)
+
+    def angles():
+        places = lax.broadcasted_iota(jnp.int32, cosine.shape, 0)
+        return (places - start[...]).astype(FULL) * inverse[...]
+
+    def put_cosine():
+        cosine[...] = jnp.cos(angles())
+
+    def put_sine():
+        sign = 2 * (lax.broadcasted_iota(jnp.int32, sine.shape, 1) // (HEAD // 2)) - 1
+        sine[...] = jnp.sin(angles()) * sign.astype(FULL)
+
+    fillers = [cast, put_cosine, put_sine]
     for step in range(1, pairs):
         for cut in range(CUTS):
+            if fillers:
+                fillers.pop(0)()
             gather.step(step, cut)
         if step == 1:
             second.start()
@@ -888,27 +914,31 @@
     first.leave()
 
 
-def enter(plane, pairs, h_home, gy_home, weights, collective):
+def enter(plane, pairs, h_home, gy_home, start, inverse, w_in, weights, collective):
     n_dp, n_col, slot, width = h_home.shape
     rows = n_dp * slot
     work = jax.ShapeDtypeStruct((rows, n_col * width), FULL)
+    table = jax.ShapeDtypeStruct((start.shape[0], HEAD), FULL)
     outs = call_remote(
         functools.partial(enter_kernel, plane, pairs, len(weights)),
         collective,
-        in_specs=[ANY] * (2 + len(weights)),
-        out_specs=[ANY, VMEM, ANY] + [ANY] * len(weights),
+        in_specs=[ANY, ANY, VMEM, VMEM] + [ANY] * (1 + len(weights)),
+        out_specs=[ANY, VMEM, ANY, VMEM, VMEM, VMEM] + [ANY] * len(weights),
         out_shape=[
             jax.ShapeDtypeStruct((2 * pairs, rows, n_col * width), LOW),
             work,
             jax.ShapeDtypeStruct(work.shape, gy_home.dtype),
+            table,
+            table,
+            jax.ShapeDtypeStruct((w_in.shape[1], w_in.shape[0] * w_in.shape[2]), LOW),
         ]
         + whole_shapes(weights),
-        scratch_shapes=[pltpu.VMEM(work.shape, LOW)]
+        scratch_shapes=[pltpu.VMEM(work.shape, LOW), pltpu.VMEM(w_in.shape, FULL), DMA]
         + exchange_sems(plane, 2)
         + gather_sems(pairs, CUTS)
         + plane_gather_sems() * len(weights),
-    )(h_home, gy_home, *weights)
-    return outs[0].reshape(2 * pairs * rows, n_col * width), outs[1], outs[2], outs[3:]
+    )(h_home, gy_home, start, inverse, w_in, *weights)
+    return [outs[0].reshape(2 * pairs * rows, n_col * width)] + list(outs[1:6]), outs[6:]
 
 
 def attend_kernel(
@@ -929,7 +959,6 @@
     exchange = to_work(plane, mix_home, mix, plane_sems, 0)
     for one in gathers:
         one.start()
-    exchange.start()
     load.wait()
     width = q.shape[1]
     heads = width // HEAD
@@ -944,12 +973,16 @@
         if head == 0:
             for cut in range(CUTS):
                 gather.step(1, cut)
+    for one in gathers:
+        one.forward()
+    exchange.start()
     rows = total.shape[0]
-    for owner in range(2 * pairs):
-        part[owner] = jnp.dot(
-            heads_out[pl.ds(owner * rows, rows)], w_out[...], preferred_element_type=FULL
-        ).astype(LOW)
-    scatter.start()
+    for dest in scatter.order():
+        for owner in (2 * dest, 2 * dest + 1):
+            part[owner] = jnp.dot(
+                heads_out[pl.ds(owner * rows, rows)], w_out[...], preferred_element_type=FULL
+            ).astype(LOW)
+        scatter.offer(dest)
     scatter.begin()
     polls = list(range(scatter.polls()))
     for step in range(2, pairs):
@@ -958,9 +991,6 @@
             for index in polls[:2]:
                 scatter.poll(index)
             polls = polls[2:]
-        if step == 2:
-            for one in gathers:
-                one.forward()
     for index in polls:
         scatter.poll(index)
     scatter.finish(total)
@@ -1105,7 +1135,7 @@
             jax.ShapeDtypeStruct((rows, width), LOW),
             jax.ShapeDtypeStruct((2, 2, narrow // 2, width // 2), LOW),
             jax.ShapeDtypeStruct((2, height, wide // 2), FULL),
-            jax.ShapeDtypeStruct((2, 8, wide), FULL),
+            jax.ShapeDtypeStruct((2, 8, 128), FULL),
         ],
         scratch_shapes=[
             pltpu.VMEM((rows, width), FULL),
@@ -1247,10 +1277,17 @@
         @pl.loop(0, D // UNIT)
         def _(unit):
             at = pl.multiple_of(unit * UNIT, UNIT)
-            y_tile = jnp.dot(hid[slot], wd[:, pl.ds(at, UNIT)], preferred_element_type=FULL)
-            y[slot, :, pl.ds(at, UNIT)] = y_tile.astype(LOW)
             tile = dot_last(units[slot], w_in[pl.ds(at, UNIT)]).astype(LOW)
             part[pl.ds(order[step] * 2, 2), :, pl.ds(at, UNIT)] = tile.reshape(2, rows, UNIT)
+
+    def work_out(step):
+        slot = step % 2
+
+        @pl.loop(0, D // UNIT)
+        def _(unit):
+            at = pl.multiple_of(unit * UNIT, UNIT)
+            tile = jnp.dot(hid[slot], wd[:, pl.ds(at, UNIT)], preferred_element_type=FULL)
+            y[slot, :, pl.ds(at, UNIT)] = tile.astype(LOW)
 
     def to_twin(dest):
         return remote(
@@ -1301,11 +1338,13 @@
                 save.wait()
         work(step)
         to_twin(order[step]).start()
+        if step > 0:
+            send_first(step - 1)
+        if step == pairs - 1:
+            send_first(step)
+        work_out(step)
         for save in saves(step):
             save.start()
-        if step > 0:
-            send_first(step - 1)
-    send_first(pairs - 1)
 
     def pass_on(dest, cut, rightward):
         arrived = from_left if rightward else from_right
@@ -1479,9 +1518,10 @@
             head, back, q, k, v, log_in, cosine, sine, start, units, k_sum, v_sum
         )
     rows = total.shape[0]
-    for owner in range(2 * pairs):
-        part[owner] = dot_last(units[pl.ds(owner * rows, rows)], w_in[...]).astype(LOW)
-    scatter.start()
+    for dest in scatter.order():
+        for owner in (2 * dest, 2 * dest + 1):
+            part[owner] = dot_last(units[pl.ds(owner * rows, rows)], w_in[...]).astype(LOW)
+        scatter.offer(dest)
     scatter.begin()
     grad_out[...] = dot_first(heads_in[...], rows_in[...]).astype(LOW)
     load_x.start()
@@ -1532,7 +1572,7 @@
         owned = [(1,) + ffn_grad[0].shape[2:], (1, local // 2, width // 2), (3, width // 4, local)]
         planes.append(pltpu.VMEM((2, 2, owned[0][1] // 2, owned[0][2]), LOW))
         for shape in owned:
-            extra += [shape, (2, 8, shape[0] * shape[2])]
+            extra += [shape, (2, 8, 128)]
             half = (shape[1] // 2, shape[0] * shape[2])
             planes += [
                 pltpu.VMEM((2, 2) + half, LOW),
@@ -1713,7 +1753,7 @@
     travel = LOW if slot % 16 == 0 else FULL
     in_kernel = plane == (2, 2)
     attention_low = [side_by_side(attention_in).astype(LOW), attention_out.astype(LOW)]
-    feedforward_low = [side_by_side(feedforward_in).astype(LOW), feedforward_out.astype(LOW)]
+    feedforward_out_own = feedforward_out.astype(LOW)
 
     group = destination // group_tokens
     sent = (
@@ -1727,11 +1767,13 @@
         hyper, streams, cotangent, sent, n_dp, travel
     )
     segment = lax.dynamic_index_in_dim(segments[:, 0], lax.axis_index("col"), 0, keepdims=False)
-    cosine, sine, start = rotary_tables(segment)
-
-    feedforward_out_low = gather_blocks(feedforward_low[1]).reshape(n_col, n_dp, *feedforward_out.shape)
+    start, inverse = rotary_parts(segment)
+
+    feedforward_out_low = gather_blocks(feedforward_out_own).reshape(n_col, n_dp, *feedforward_out.shape)
     early = attention_low if in_kernel else []
-    rows_att, hidden_att, gy_work, wholes = enter(plane, pairs, h_home, gy_home, early, 1)
+    (rows_att, hidden_att, gy_work, cosine, sine, feedforward_in_own), wholes = enter(
+        plane, pairs, h_home, gy_home, start, inverse, feedforward_in, early, 1
+    )
     if not in_kernel:
         wholes = [gather_blocks(attention_low[0]), whole_out(attention_low[1], n_dp, n_col)]
     attention_in_low, attention_out_low = wholes
@@ -1756,10 +1798,10 @@
         start,
         gy_work.astype(LOW),
         mix_home,
-        feedforward_low[:1] if in_kernel else [],
+        [feedforward_in_own] if in_kernel else [],
         2,
     )
-    feedforward_in_low = wholes[0] if in_kernel else gather_blocks(feedforward_low[0])
+    feedforward_in_low = wholes[0] if in_kernel else gather_blocks(feedforward_in_own)
     rows_ffn, hidden_low, grad_units, partial_ffn, grad_hidden_ffn, grad_branch = feed_forward(
         plane,
         pairs,

time: 652 us -> 640 us (0.982)
  other arithmetic: 43.9 us -> 36.5 us
  transfers between devices with their start and end apart: 1 -> 1, of which waited for: 0 -> 0; matrix products, arithmetic and copies ran while one was open for 3% -> 1% of each run, Pallas kernels for 33% -> 34%
where the time goes in v5:
time: 640 us; the launch traced here: 631 us
  Pallas kernels  559 us (87%)
  other arithmetic  36.5 us (6%)
  between operations  20.4 us (3%)
  local copies, waits for them, and re-layouts  14.9 us (2%)
    pallas_call x1, Pallas kernels, feed_forward(): call_remote(functools.partial(ffn_kernel, plane, pairs), collective, in_s...  125 us
    pallas_call x1, Pallas kernels, leave(): call_remote(functools.partial(leave_kernel, plane, pairs, in_kernel), col...  114 us
    pallas_call x1, Pallas kernels, attend(): call_remote(functools.partial(attend_kernel, plane, pairs, len(weights)),...  109 us
    pallas_call x1, Pallas kernels, enter(): call_remote(functools.partial(enter_kernel, plane, pairs, len(weights)),...  91.8 us
    pallas_call x1, Pallas kernels, back_gather(): call_remote(functools.partial(back_kernel, pairs, plane), collective, in_...  86.2 us
    sub x5, other arithmetic, adam_update(): weight - learning_rate * (new_one / fix_one / (jnp.sqrt(new_two / fix_two...  21 us
  transfers between devices with their start and end apart: 1, of which 0 were waited for; matrix products, arithmetic and copies ran while one was open for 1% of the time, Pallas kernels for 34%

profile of v5, /device:TPU:0, one launch (start us, length us, event | category | flops | bytes accessed | tf_op | source)
XLA Modules:
  0.0 631.0 jit_solution(13211614493074705093)
XLA Ops:
  7.3 2.8 convert_element_type.18
  15.7 1.1 broadcast_in_dim.35.start
  17.0 10.8 %shard_map.371 = (f32[2,2,96,1024]{3,2,1,0:T(8,128)}, f32[2,2,96,1024]{3,2,1,0:T(8,128)}, f32[2,2,96,1024]{3,2,1,0:T(8,128)}, bf16[2,2,96,1024]{3,2,1,0:T(8,128)(2,1)}, f32[16,8,512]{2,1,0:T(8,128)}) custom-call(f32[48]{0:T(128)} %reshape.166.hyper, f32[2,4,192,1024]{3,2,1,0:T(8,128)} %streams.3, f32[2,4,192,1024]{3,2,1,0:T(8,128)} %cotangent.3, ...), custom_call_target="tpu_custom_call" | custom-call | tf_op jit(solution)/shard_map/pallas_call | solution.py:134
  27.8 1.2 reduce_sum.113
  30.0 91.8 %shard_map.372 = (bf16[8,192,2048]{2,1,0:T(8,128)(2,1)}, f32[192,2048]{1,0:T(8,128)}, bf16[192,2048]{1,0:T(8,128)(2,1)}, f32[1536,128]{1,0:T(8,128)}, f32[1536,1...) custom-call(f32[2,2,96,1024]{3,2,1,0:T(8,128)} %get-tuple-element.70.h_home, ...), custom_call_target="tpu_custom_call" | custom-call | tf_op jit(solution)/shard_map/pallas_call | solution.py:922
  121.8 109.2 %shard_map.373 = (bf16[8,192,2048]{2,1,0:T(8,128)(2,1)}, f32[192,2048]{1,0:T(8,128)}, bf16[1536,256]{1,0:T(8,128)(2,1)}, f32[1536,2]{1,0:T(8,128)}, bf16[1536,25...) custom-call(bf16[1536,2048]{1,0:T(8,128)(2,1)} %bitcast.63, ...), custom_call_target="tpu_custom_call" | custom-call | tf_op jit(solution)/shard_map/pallas_call | solution.py:1011
  231.2 124.8 %shard_map.374 = (bf16[8,192,2048]{2,1,0:T(8,128)(2,1)}, bf16[4,384,1024]{2,1,0:T(8,128)(2,1)}, bf16[4,384,2048]{2,1,0:T(8,128)(2,1)}, bf16[4,384,2048]{2,1,0:T(...) custom-call(f32[48]{0:T(128)} %reshape.166.hyper, ...), custom_call_target="tpu_custom_call" | custom-call | tf_op jit(solution)/shard_map/pallas_call | solution.py:1421
  356.0 86.2 %shard_map.375 = (bf16[8,192,2048]{2,1,0:T(8,128)(2,1)}, bf16[192,2048]{1,0:T(8,128)(2,1)}, bf16[2,2,512,1024]{3,2,1,0:T(8,128)(2,1)}, f32[2,512,1024]{2,1,0:T(8,128)}, f32[2,8,128]{2,1,0:T(8,128)}) custom-call(bf16[192,2048]{1,0:T(8,128)(2,1)} %get-tuple-element.85.gathered, bf16[8,192,2048]{2,1,0:T(8,128)(2,1)} %bitcast.68, bf16[1536,2048]{1,0:T(8,128)(2,1)} %bitcast.66, ...), custom_call_target="tpu_custom_call" | custom-call | tf_op jit(solution)/shard_map/pallas_call | solution.py:1128
  442.2 1.3 reduce_sum.115
  443.5 114.0 %shard_map.376 = (bf16[2,2,96,1024]{3,2,1,0:T(8,128)(2,1)}, bf16[2,2,96,1024]{3,2,1,0:T(8,128)(2,1)}, bf16[2,2,96,1024]{3,2,1,0:T(8,128)(2,1)}, bf16[2,2,96,1024...) custom-call(bf16[1536,2048]{1,0:T(8,128)(2,1)} %bitcast.69, ...), custom_call_target="tpu_custom_call" | custom-call | tf_op jit(solution)/shard_map/pallas_call | solution.py:1589
  557.5 1.3 reduce_sum.118
  558.8 1.3 reduce_sum.117
  560.1 1.3 reduce_sum.116
  561.4 12.5 %shard_map.377 = (f32[2,4,192,1024]{3,2,1,0:T(8,128)}, f32[2,4,192,1024]{3,2,1,0:T(8,128)}, f32[17,8,512]{2,1,0:T(8,128)}) custom-call(f32[48]{0:T(128)} %reshape.166.hyper, f32[2,4,192,1024]{3,2,1,0:T(8,128)} %streams.3, f32[2,4,192,1024]{3,2,1,0:T(8,128)} %cotangent.3, s32[2,192,1]{2,1,0:T(8,128)} %copy.65.sent, ...), custom_call_target="tpu_custom_call" | custom-call | tf_op jit(solution)/shard_map/pallas_call | solution.py:188
  573.9 1.2 reduce_sum.114
  578.3 9.8 %shard_map.378 = f32[1,128]{1,0:T(1,128)} custom-call(f32[1,128]{1,0:T(1,128)} %fusion.7.own), custom_call_target="tpu_custom_call" | custom-call | tf_op jit(solution)/shard_map/pallas_call | solution.py:1664
  588.9 1.3 fusion.13
  594.7 2.9 multiply_subtract_fusion.3
  597.7 5.1 multiply_subtract_fusion.2
  602.9 6.4 %multiply_subtract_fusion.1 = (f32[512,1024]{1,0:T(8,128)}, f32[512,1024]{1,0:T(8,128)}, f32[512,1024]{1,0:T(8,128)}) fusion(f32[512,1024]{1,0:T(8,128)S(1)} %copy-done.4, f32[]{:T(128)} %bitcast.35, f32[]{:T(128)} %bitcast.34, f32[]{:T(128)S(6)} %div.75, f32[512,1024]{1,0:T(8,128)S(1)} %copy-done.13, f32[512,1024]{1,0:T(8,128)} %param.31, ...), kind=kLoop, calls=%fused_computation.8 | loop fusion | flops 8388608 | bytes 14680076 | tf_op jit(solution)/shard_map/sub | solution.py:1720
  609.3 1.7 copy-done.9
  611.0 5.9 multiply_subtract_fusion
  618.7 2.0 copy.80
  621.5 1.3 copy.82
  (73 shorter events, 13.2 us)
Async XLA Ops:
  7.2 7.4 %copy-start = (s32[2,1,1536]{2,1,0:T(1,128)S(1)}, s32[2,1,1536]{2,1,0:T(1,128)}, u32[]{:S(2)}) copy-start(s32[2,1,1536]{2,1,0:T(1,128)} %param.23) | copy-start | bytes 36868
  7.2 3.7 copy-start.14
  7.2 4.9 copy-start.16
  7.2 6.6 %copy-start.11 = (f32[128,1024]{1,0:T(8,128)S(1)}, f32[128,1024]{1,0:T(8,128)}, u32[]{:S(2)}) copy-start(f32[128,1024]{1,0:T(8,128)} %param.26) | copy-start | bytes 1572868
  7.2 223.9 %all-gather.2.cloned.1.call-start = ((), (), s32[]{:S(2)}) async-start(), calls=%async_computation | async-start | bytes 5242880 | tf_op jit(solution)/shard_map/all_gather | solution.py:1686
  10.1 6.8 %copy-start.6 = (f32[3,512,256]{2,1,0:T(8,128)S(1)}, f32[3,512,256]{2,1,0:T(8,128)}, u32[]{:S(2)}) copy-start(f32[3,512,256]{2,1,0:T(8,128)} %param.24) | copy-start | bytes 4718596
  588.1 9.6 %copy-start.7 = (f32[3,512,256]{2,1,0:T(8,128)S(1)}, f32[3,512,256]{2,1,0:T(8,128)}, u32[]{:S(2)}) copy-start(f32[3,512,256]{2,1,0:T(8,128)} %param.24) | copy-start | bytes 4718596
  588.1 9.6 %copy-start.8 = (f32[3,512,256]{2,1,0:T(8,128)S(1)}, f32[3,512,256]{2,1,0:T(8,128)}, u32[]{:S(2)}) copy-start(f32[3,512,256]{2,1,0:T(8,128)} %get-tuple-element.183) | copy-start | bytes 4718596
  593.3 23.6 %copy-start.15 = (f32[2,4,6]{2,1,0:T(4,128)}, f32[2,4,6]{2,1,0:T(4,128)S(1)}, u32[]{:S(2)}) copy-start(f32[2,4,6]{2,1,0:T(4,128)S(1)} %get-tuple-element.187) | copy-start | bytes 580
  597.7 5.2 copy-start.4
  597.7 5.2 copy-start.5
  597.7 5.2 copy-start.13
  597.7 11.6 %copy-start.10 = (f32[2,512,1024]{2,1,0:T(8,128)S(1)}, f32[2,512,1024]{2,1,0:T(8,128)}, u32[]{:S(2)}) copy-start(f32[2,512,1024]{2,1,0:T(8,128)} %param.29) | copy-start | bytes 12582916
  602.9 6.4 %copy-start.2 = (f32[2,512,1024]{2,1,0:T(8,128)S(1)}, f32[2,512,1024]{2,1,0:T(8,128)}, u32[]{:S(2)}) copy-start(f32[2,512,1024]{2,1,0:T(8,128)} %w_in.1) | copy-start | bytes 12582916
  602.9 6.4 %copy-start.3 = (f32[2,512,1024]{2,1,0:T(8,128)S(1)}, f32[2,512,1024]{2,1,0:T(8,128)}, u32[]{:S(2)}) copy-start(f32[2,512,1024]{2,1,0:T(8,128)} %get-tuple-element.184) | copy-start | bytes 12582916
  602.9 8.1 %copy-start.9 = (f32[2,512,1024]{2,1,0:T(8,128)S(1)}, f32[2,512,1024]{2,1,0:T(8,128)}, u32[]{:S(2)}) copy-start(f32[2,512,1024]{2,1,0:T(8,128)} %param.33) | copy-start | bytes 12582916
  611.0 5.9 copy-start.17
  611.0 5.9 copy-start.18
  618.7 2.0 copy-start.12
  620.7 2.1 copy-start.1
Sparse Core Ops, SparseCore 0:
  10.5 76.0 all-gather.1

commit v6 on v5

--- a/solution.py
+++ b/solution.py
@@ -1226,7 +1226,6 @@
     for load in loads:
         load.start()
     exchange = to_work(plane, back_home, upstream, plane_sems, 0)
-    exchange.start()
     order = [arrival(place, pairs, step) for step in range(pairs)]
 
     def load_gy(step):
@@ -1337,6 +1336,8 @@
             for save in saves(step - 2):
                 save.wait()
         work(step)
+        if step == 1:
+            exchange.start()
         to_twin(order[step]).start()
         if step > 0:
             send_first(step - 1)
@@ -1612,7 +1613,9 @@
     return outs[:4], outs[4:]
 
 
-def total_kernel(plane, count, own, out, line, flat, line_send, line_recv, flat_send, flat_recv):
+def total_kernel(plane, count, groups, *refs):
+    parts, refs = refs[: len(groups)], refs[len(groups) :]
+    out, line, flat, line_send, line_recv, flat_send, flat_recv = refs
     n_dp, n_col = plane
     me = lax.axis_index("row")
     here = lax.axis_index("dp") * n_col + lax.axis_index("col")
@@ -1625,7 +1628,15 @@
             barrier, inc=1, device_id=peer(plane, offset), device_id_type=pl.DeviceIdType.MESH
         )
     pl.semaphore_wait(barrier, count - 1 + n_dp * n_col - 1)
-    line[me] = own[...]
+    lane = lax.broadcasted_iota(jnp.int32, out.shape, 1)
+    own = jnp.zeros(out.shape, FULL)
+    first = 0
+    for part, group in zip(parts, groups):
+        for index in range(part.shape[0]):
+            value = jnp.sum(jnp.sum(part[index], axis=0, keepdims=True), axis=1, keepdims=True)
+            own = own + jnp.where(lane == first + index * group, value, 0.0)
+        first = first + part.shape[0] * group
+    line[me] = own
     copies = [
         remote(line.at[me], line.at[me], line_send.at[step], line_recv.at[step], {"row": row})
         for step, row in enumerate(rows)
@@ -1658,13 +1669,14 @@
     out[...] = sums
 
 
-def sum_everywhere(plane, values_in, collective):
+def sum_everywhere(plane, parts, squares, collective):
     count = lax.axis_size("row")
-    shape = values_in.shape
+    shape = (1, 128)
+    groups = [1] * len(parts) + [0] * len(squares)
     return call_remote(
-        functools.partial(total_kernel, plane, count),
+        functools.partial(total_kernel, plane, count, groups),
         collective,
-        in_specs=[VMEM],
+        in_specs=[VMEM] * len(groups),
         out_specs=VMEM,
         out_shape=jax.ShapeDtypeStruct(shape, FULL),
         scratch_shapes=[
@@ -1675,7 +1687,7 @@
             DMA(plane),
             DMA(plane),
         ],
-    )(values_in)
+    )(*parts, *squares)
 
 
 def mat(left, right):
@@ -1863,10 +1875,11 @@
         shard_attention_out = own_out(sums_att[1], n_dp, n_col)
         squares += [value * value for value in (shard_attention_in, shard_attention_out)]
         shard_feedforward_in, shard_feedforward_out = sums_ffn
-    square = sum(jnp.sum(value) for value in squares)
+    if not in_kernel:
+        square = sum(jnp.sum(value) for value in squares)
+        squares = [jnp.zeros((1, 8, 128), FULL).at[0, 0, 0].set(square)]
     streams_out, stream_grad, dots = finish(hyper, streams, cotangent, sent, homes)
-    dots = jnp.concatenate([jnp.sum(gram, axis=(1, 2)), jnp.sum(dots, axis=(1, 2)), square[None]])
-    totals = sum_everywhere(plane, jnp.pad(dots, (0, 128 - dots.shape[0])).reshape(1, 128), 7)[0]
+    totals = sum_everywhere(plane, [gram, dots], squares, 7)[0]
     a0, m0, c0 = hyper_weights[0, :, 0], hyper_weights[0, :, 1:5], hyper_weights[0, :, 5]
     a1, m1, c1 = hyper_weights[1, :, 0], hyper_weights[1, :, 1:5], hyper_weights[1, :, 5]
     gram = totals[:16].reshape(STREAMS, STREAMS)

time: 640 us -> 627 us (0.980)
  other arithmetic: 36.5 us -> 26.3 us
    reduce_sum x6 -> x0, other arithmetic: 7.54 us -> none  [the longest x4 5.21 us: body(): square = sum((jnp.sum(value) for value in squares))]
where the time goes in v6:
time: 627 us; the launch traced here: 619 us
  Pallas kernels  560 us (89%)
  other arithmetic  26.3 us (4%)
  between operations  17.8 us (3%)
  local copies, waits for them, and re-layouts  15 us (2%)
    pallas_call x1, Pallas kernels, feed_forward(): call_remote(functools.partial(ffn_kernel, plane, pairs), collective, in_s...  124 us
    pallas_call x1, Pallas kernels, leave(): call_remote(functools.partial(leave_kernel, plane, pairs, in_kernel), col...  114 us
    pallas_call x1, Pallas kernels, attend(): call_remote(functools.partial(attend_kernel, plane, pairs, len(weights)),...  109 us
    pallas_call x1, Pallas kernels, enter(): call_remote(functools.partial(enter_kernel, plane, pairs, len(weights)),...  91.6 us
    pallas_call x1, Pallas kernels, back_gather(): call_remote(functools.partial(back_kernel, pairs, plane), collective, in_...  87.1 us
    sub x5, other arithmetic, adam_update(): weight - learning_rate * (new_one / fix_one / (jnp.sqrt(new_two / fix_two...  18.9 us
    pallas_call x1, Pallas kernels, finish(): pl.pallas_call(finish_kernel, grid=(micro, width // wide), in_specs=[SMEM...  12.6 us
  transfers between devices with their start and end apart: 1, of which 0 were waited for; matrix products, arithmetic and copies ran while one was open for 1% of the time, Pallas kernels for 34%

profile of v6, /device:TPU:0, one launch (start us, length us, event | category | flops | bytes accessed | tf_op | source)
XLA Modules:
  0.0 619.0 jit_solution(3370519109375536679)
XLA Ops:
  7.3 2.8 convert_element_type.16
  10.2 1.1 convert_reduce_fusion
  11.3 1.2 broadcast_in_dim.15.start
  15.1 0.8 copy.65.sent
  16.9 10.8 %shard_map.371 = (f32[2,2,96,1024]{3,2,1,0:T(8,128)}, f32[2,2,96,1024]{3,2,1,0:T(8,128)}, f32[2,2,96,1024]{3,2,1,0:T(8,128)}, bf16[2,2,96,1024]{3,2,1,0:T(8,128)(2,1)}, f32[16,8,512]{2,1,0:T(8,128)}) custom-call(f32[48]{0:T(128)} %reshape.163.hyper, f32[2,4,192,1024]{3,2,1,0:T(8,128)} %streams.3, f32[2,4,192,1024]{3,2,1,0:T(8,128)} %cotangent.3, ...), custom_call_target="tpu_custom_call" | custom-call | tf_op jit(solution)/shard_map/pallas_call | solution.py:134
  27.8 0.9 pad_maximum_fusion.rest_0_
  28.7 91.6 %shard_map.372 = (bf16[8,192,2048]{2,1,0:T(8,128)(2,1)}, f32[192,2048]{1,0:T(8,128)}, bf16[192,2048]{1,0:T(8,128)(2,1)}, f32[1536,128]{1,0:T(8,128)}, f32[1536,1...) custom-call(f32[2,2,96,1024]{3,2,1,0:T(8,128)} %get-tuple-element.70.h_home, ...), custom_call_target="tpu_custom_call" | custom-call | tf_op jit(solution)/shard_map/pallas_call | solution.py:922
  120.3 109.4 %shard_map.373 = (bf16[8,192,2048]{2,1,0:T(8,128)(2,1)}, f32[192,2048]{1,0:T(8,128)}, bf16[1536,256]{1,0:T(8,128)(2,1)}, f32[1536,2]{1,0:T(8,128)}, bf16[1536,25...) custom-call(bf16[1536,2048]{1,0:T(8,128)(2,1)} %bitcast.60, ...), custom_call_target="tpu_custom_call" | custom-call | tf_op jit(solution)/shard_map/pallas_call | solution.py:1011
  229.9 124.2 %shard_map.374 = (bf16[8,192,2048]{2,1,0:T(8,128)(2,1)}, bf16[4,384,1024]{2,1,0:T(8,128)(2,1)}, bf16[4,384,2048]{2,1,0:T(8,128)(2,1)}, bf16[4,384,2048]{2,1,0:T(...) custom-call(f32[48]{0:T(128)} %reshape.163.hyper, ...), custom_call_target="tpu_custom_call" | custom-call | tf_op jit(solution)/shard_map/pallas_call | solution.py:1422
  354.2 87.1 %shard_map.375 = (bf16[8,192,2048]{2,1,0:T(8,128)(2,1)}, bf16[192,2048]{1,0:T(8,128)(2,1)}, bf16[2,2,512,1024]{3,2,1,0:T(8,128)(2,1)}, f32[2,512,1024]{2,1,0:T(8,128)}, f32[2,8,128]{2,1,0:T(8,128)}) custom-call(bf16[192,2048]{1,0:T(8,128)(2,1)} %get-tuple-element.85.gathered, bf16[8,192,2048]{2,1,0:T(8,128)(2,1)} %bitcast.65, bf16[1536,2048]{1,0:T(8,128)(2,1)} %bitcast.63, ...), custom_call_target="tpu_custom_call" | custom-call | tf_op jit(solution)/shard_map/pallas_call | solution.py:1128
  441.3 114.0 %shard_map.376 = (bf16[2,2,96,1024]{3,2,1,0:T(8,128)(2,1)}, bf16[2,2,96,1024]{3,2,1,0:T(8,128)(2,1)}, bf16[2,2,96,1024]{3,2,1,0:T(8,128)(2,1)}, bf16[2,2,96,1024...) custom-call(bf16[1536,2048]{1,0:T(8,128)(2,1)} %bitcast.66, ...), custom_call_target="tpu_custom_call" | custom-call | tf_op jit(solution)/shard_map/pallas_call | solution.py:1590
  555.3 12.6 %shard_map.377 = (f32[2,4,192,1024]{3,2,1,0:T(8,128)}, f32[2,4,192,1024]{3,2,1,0:T(8,128)}, f32[17,8,512]{2,1,0:T(8,128)}) custom-call(f32[48]{0:T(128)} %reshape.163.hyper, f32[2,4,192,1024]{3,2,1,0:T(8,128)} %streams.3, f32[2,4,192,1024]{3,2,1,0:T(8,128)} %cotangent.3, s32[2,192,1]{2,1,0:T(8,128)} %copy.65.sent, ...), custom_call_target="tpu_custom_call" | custom-call | tf_op jit(solution)/shard_map/pallas_call | solution.py:188
  567.9 10.1 %shard_map.378 = f32[1,128]{1,0:T(1,128)} custom-call(f32[16,8,512]{2,1,0:T(8,128)} %get-tuple-element.107.refs_0_, f32[17,8,512]{2,1,0:T(8,128)} %get-tuple-element.108.refs_1_, f32[2,8,128]{2,1,0:T(8,128)} %get-tuple-element.109.refs_2_, f32[2,8,128]{2,1,0:T(8,128)} %get-tuple-element.110.refs_3_, f32[2,8,128]{2,1,0:T(8,128)} %get-tuple-element.111.refs_4_, ...), custom_call_target="tpu_custom_call" | custom-call | tf_op jit(solution)/shard_map/pallas_call | solution.py:1676
  578.7 0.8 slice_bitcast_fusion.8
  579.5 1.3 fusion.12
  584.4 7.8 %multiply_subtract_fusion.1 = (f32[512,1024]{1,0:T(8,128)}, f32[512,1024]{1,0:T(8,128)}, f32[512,1024]{1,0:T(8,128)}) fusion(f32[512,1024]{1,0:T(8,128)} %param.27, f32[]{:T(128)} %bitcast.33, f32[]{:T(128)} %bitcast.32, f32[]{:T(128)S(6)} %div.75, f32[512,1024]{1,0:T(8,128)} %param.35, f32[512,1024]{1,0:T(8,128)} %param.31, ...), kind=kLoop, calls=%fused_computation.8 | loop fusion | flops 8388608 | bytes 14680076 | tf_op jit(solution)/shard_map/sub | solution.py:1732
  592.2 1.4 multiply_subtract_fusion.3
  594.3 1.2 copy-done.9
  595.5 6.0 multiply_subtract_fusion
  601.6 3.0 multiply_subtract_fusion.2
  605.2 1.1 copy.79
  606.4 2.1 copy.80
  608.5 0.8 copy.81
  609.5 1.3 copy.82
  (72 shorter events, 7.5 us)
Async XLA Ops:
  7.2 3.0 copy-start
  7.2 5.2 copy-start.19
  7.2 5.8 copy-start.17
  7.2 6.4 %copy-start.5 = (f32[3,512,256]{2,1,0:T(8,128)S(1)}, f32[3,512,256]{2,1,0:T(8,128)}, u32[]{:S(2)}) copy-start(f32[3,512,256]{2,1,0:T(8,128)} %param.24) | copy-start | bytes 4718596
  7.2 222.7 %all-gather.2.cloned.1.call-start = ((), (), s32[]{:S(2)}) async-start(), calls=%async_computation | async-start | bytes 5242880 | tf_op jit(solution)/shard_map/all_gather | solution.py:1698
  10.1 3.6 copy-start.10
  555.3 36.9 %copy-start.11 = (f32[128,1024]{1,0:T(8,128)S(1)}, f32[128,1024]{1,0:T(8,128)}, u32[]{:S(2)}) copy-start(f32[128,1024]{1,0:T(8,128)} %param.26) | copy-start | bytes 1572868
  579.5 12.7 %copy-start.12 = (f32[1,128,1024]{2,1,0:T(8,128)S(1)}, f32[1,128,1024]{2,1,0:T(8,128)}, u32[]{:S(2)}) copy-start(f32[1,128,1024]{2,1,0:T(8,128)} %get-tuple-element.115) | copy-start | bytes 1572868
  579.5 12.7 %copy-start.15 = (f32[128,1024]{1,0:T(8,128)S(1)}, f32[128,1024]{1,0:T(8,128)}, u32[]{:S(2)}) copy-start(f32[128,1024]{1,0:T(8,128)} %param.34) | copy-start | bytes 1572868
  579.5 12.7 %copy-start.16 = (f32[128,1024]{1,0:T(8,128)S(1)}, f32[128,1024]{1,0:T(8,128)}, u32[]{:S(2)}) copy-start(f32[128,1024]{1,0:T(8,128)} %param.30) | copy-start | bytes 1572868
  583.0 21.6 %copy-start.18 = (f32[2,4,6]{2,1,0:T(4,128)}, f32[2,4,6]{2,1,0:T(4,128)S(1)}, u32[]{:S(2)}) copy-start(f32[2,4,6]{2,1,0:T(4,128)S(1)} %get-tuple-element.187) | copy-start | bytes 580
  584.4 9.3 %copy-start.2 = (f32[2,512,1024]{2,1,0:T(8,128)S(1)}, f32[2,512,1024]{2,1,0:T(8,128)}, u32[]{:S(2)}) copy-start(f32[2,512,1024]{2,1,0:T(8,128)} %w_in.1) | copy-start | bytes 12582916
  584.4 9.3 %copy-start.3 = (f32[2,512,1024]{2,1,0:T(8,128)S(1)}, f32[2,512,1024]{2,1,0:T(8,128)}, u32[]{:S(2)}) copy-start(f32[2,512,1024]{2,1,0:T(8,128)} %get-tuple-element.184) | copy-start | bytes 12582916
  584.4 9.9 %copy-start.8 = (f32[2,512,1024]{2,1,0:T(8,128)S(1)}, f32[2,512,1024]{2,1,0:T(8,128)}, u32[]{:S(2)}) copy-start(f32[2,512,1024]{2,1,0:T(8,128)} %param.33) | copy-start | bytes 12582916
  584.4 11.1 %copy-start.9 = (f32[2,512,1024]{2,1,0:T(8,128)S(1)}, f32[2,512,1024]{2,1,0:T(8,128)}, u32[]{:S(2)}) copy-start(f32[2,512,1024]{2,1,0:T(8,128)} %param.29) | copy-start | bytes 12582916
  595.5 6.0 copy-start.6
  595.5 6.0 copy-start.7
  595.5 6.1 copy-start.13
  595.5 6.1 copy-start.14
  601.5 3.1 copy-start.20
  601.5 3.1 copy-start.21
  606.4 3.1 copy-start.4
  608.5 2.3 copy-start.1
Sparse Core Ops, SparseCore 0:
  10.5 77.6 all-gather.1
